TPU v7x, 32 devices: a whole 2x2x4 slice. The times are simulated.
32 devices in a mesh: gx: 8 (over z, y), gy: 4 (over x, core).
Axes of the slice: x: 2, y: 2, z: 4, core: 2. Of those that a mesh axis runs over, the one named last changes fastest.
Arguments:
- water_content: float32 [16, 512, 2048], P(None, 'gx', 'gy'), may hold values from 0.15 to 0.35
- porosity: float32 [512, 2048], P('gx', 'gy'), may hold values from 0.4 to 0.5
- conduct: float32 [512, 2048], P('gx', 'gy'), may hold values from 0.05 to 0.5
- exponent: float32 [512, 2048], P('gx', 'gy'), may hold values from 3 to 6
- infiltration: float32 [512, 2048], P('gx', 'gy'), may hold values from 0.02 to 0.2
- column_target: int32 [512, 2048], P('gx', 'gy'), may hold values from 0 to 16383, as said below
- send_blocks: int32 [32, 32, 4], P(('gx', 'gy')), may hold values from -1 to 7, as said below
- prior_heads: float32 [256, 128], P(('gx', 'gy')), may hold values from -6 to 6
- block_pattern: int32 [256, 7], P(('gx', 'gy')), may hold values from -1 to 255, as said below
- aquifer_blocks: float32 [256, 7, 128, 128], P(('gx', 'gy')), as said below
Outputs:
- soil_water: float32 [16, 512, 2048], P(None, 'gx', 'gy')
- aquifer_heads: float32 [256, 128], P(('gx', 'gy'))
- column_heads: float32 [512, 2048], P('gx', 'gy')
Inputs may be any that keep to these rules, and one draw needn't show every extreme that they name: send_blocks[d, o, s] is a block number of owner o or -1; the blocks of one (d, o) are distinct and the -1 entries come last; entries other than -1 stand only where o is d or the device next to d along gx or along gy, without wrap; send_blocks[d, d] holds 4 blocks, every neighbour at least one, and in every draw some owner receives 4 blocks from each of its neighbours. `column_target`: every column of device d's tile names an owner o that is d or next to d along gx or gy, a slot s with send_blocks[d, o, s] >= 0, and a cell below 128. block_pattern[r, 0] = r; every other entry is -1 or a block on r's own device or on the device next to it along gx or along gy, without wrap; no row names a block twice, and block s appears in row r exactly when r appears in row s. `aquifer_blocks`: blocks where block_pattern is -1 are zero; the block that row r holds for s is the transpose of the one that row s holds for r, and the assembled matrix is symmetric and strictly diagonally dominant with a positive diagonal.
All inputs are finite; a program needn't handle non-finite values.
Results may differ from a plain program's by a relative error of at most 0.0003.
Values sent between devices are 32-bit elements; how exact they have to be, the bound alone decides.
No kernel may reach another device: no remote copies, remote signals or barrier semaphores. Data moves between devices by JAX's collectives and lax.ppermute only.
A program may use at most 64 MiB of HBM per device.

v0:
```python
import jax
import jax.numpy as jnp
from jax import lax
from jax.sharding import PartitionSpec as P

SWEEPS = 8
ITERS = 3


residual_content = 0.05


def padded(cells, sides, width):
    for axis, dim in sides:
        count = lax.axis_size(axis)
        ends = count - 1
        head = lax.slice_in_dim(cells, 0, width, axis=dim)
        tail = lax.slice_in_dim(cells, cells.shape[dim] - width, cells.shape[dim], axis=dim)
        cells = jnp.concatenate(
            [
                lax.ppermute(tail, axis, [(i, (i + 1) % count) for i in range(ends)]),
                cells,
                lax.ppermute(head, axis, [((i + 1) % count, i) for i in range(ends)]),
            ],
            axis=dim,
        )
    return cells


def soil_sweeps(water_content, porosity, conduct, exponent, infiltration):
    span = porosity - residual_content

    def layer(flux, content):
        saturation = (content - residual_content) / span
        conduct_now = conduct * jnp.exp(exponent * jnp.log(saturation))
        slope = exponent * conduct_now / (saturation * span)
        change = (flux - conduct_now) / (1.0 + slope)
        return (conduct_now + slope * change, content + change)

    recharge = jnp.zeros_like(infiltration)
    for sweep_index in range(SWEEPS):
        bottom, water_content = lax.scan(layer, infiltration, water_content)
        recharge = recharge + bottom
    return (water_content, recharge)


def deliver(got_ids, got_values, own_blocks):
    flat_ids = got_ids.reshape(1, -1)
    selector = (jnp.arange(own_blocks, dtype=jnp.int32)[:, None] == flat_ids).astype(jnp.float32)
    return jnp.dot(
        selector, got_values, precision=lax.Precision.HIGHEST, preferred_element_type=jnp.float32
    )


def paired(residual, image):
    return lax.psum((jnp.sum(residual * residual), jnp.sum(residual * image)), ("gx", "gy"))


def body(
    water_content,
    porosity,
    conduct,
    exponent,
    infiltration,
    column_target,
    send_blocks,
    prior_heads,
    block_pattern,
    aquifer_blocks,
):
    devices = send_blocks.shape[1]
    slot_count = send_blocks.shape[2]
    own_blocks = prior_heads.shape[0]
    width = prior_heads.shape[1]
    gy_count = lax.axis_size("gy")
    tile_x = lax.axis_index("gx")
    tile_y = lax.axis_index("gy")
    myself = tile_x * gy_count + tile_y
    my_ids = send_blocks[0]
    zero_row = jnp.zeros((1, width), jnp.float32)
    owner = block_pattern // own_blocks
    local = (
        (owner // gy_count - tile_x + 1) * 3 + (owner % gy_count - tile_y + 1)
    ) * own_blocks + block_pattern % own_blocks
    index = jnp.where(block_pattern < 0, 9 * own_blocks, local)

    def fetch(field):
        framed = padded(field.reshape(1, 1, own_blocks, width), (("gx", 0), ("gy", 1)), 1)
        return jnp.concatenate([framed.reshape(9 * own_blocks, width), zero_row], axis=0)[index]

    def apply_operator(field):
        return jnp.einsum(
            "rkij,rkj->ri", aquifer_blocks, fetch(field), precision=lax.Precision.HIGHEST
        )

    soil_water, recharge = soil_sweeps(water_content, porosity, conduct, exponent, infiltration)
    start_image = apply_operator(prior_heads)
    area = own_blocks * width / (recharge.shape[0] * recharge.shape[1])
    partial_value = jax.ops.segment_sum(
        recharge.reshape(-1), column_target.reshape(-1), num_segments=devices * slot_count * width
    )
    partial_value = partial_value.reshape(devices, slot_count, width)

    def placed(target_owner):
        safe = jnp.clip(target_owner, 0, devices - 1)
        return deliver(my_ids[safe], partial_value[safe], own_blocks)

    outgoing = jnp.stack(
        [
            jnp.stack([placed(myself - gy_count), placed(myself + 1)]),
            jnp.stack([placed(myself - 1), placed(myself + gy_count)]),
        ]
    )
    framed_sums = padded(outgoing, (("gx", 0), ("gy", 1)), 1)
    cells = deliver(my_ids[myself], partial_value[myself], own_blocks)
    cells = cells + framed_sums[0, 2] + framed_sums[3, 1] + framed_sums[1, 0] + framed_sums[2, 3]
    rhs = prior_heads + area * cells
    heads = prior_heads
    residual = rhs - start_image
    image = apply_operator(residual)
    norm_now, curvature = paired(residual, image)
    step_size = norm_now / curvature
    direction, along = (residual, image)
    for iteration in range(ITERS):
        heads = heads + step_size * direction
        residual = residual - step_size * along
        if iteration + 1 < ITERS:
            image = apply_operator(residual)
            norm_next, curvature = paired(residual, image)
            ratio = norm_next / norm_now
            step_size = norm_next / (curvature - ratio * norm_next / step_size)
            direction = residual + ratio * direction
            along = image + ratio * along
            norm_now = norm_next
    framed_back = padded(heads.reshape(1, 1, own_blocks, width), (("gx", 0), ("gy", 1)), 1)
    target_owner = column_target // (slot_count * width)
    block = my_ids.reshape(-1)[column_target // width]
    place = (
        (target_owner // gy_count - tile_x + 1) * 3 + (target_owner % gy_count - tile_y + 1)
    ) * own_blocks + block
    column_heads = framed_back.reshape(-1)[place * width + column_target % width]
    return (soil_water, heads, column_heads)


def solution(mesh):
    placed = (
        P(None, "gx", "gy"),
        P("gx", "gy"),
        P("gx", "gy"),
        P("gx", "gy"),
        P("gx", "gy"),
        P("gx", "gy"),
        P(("gx", "gy"), None, None),
        P(("gx", "gy"), None),
        P(("gx", "gy"), None),
        P(("gx", "gy"), None, None, None),
    )
    return jax.shard_map(
        body,
        mesh=mesh,
        in_specs=placed,
        out_specs=(P(None, "gx", "gy"), P(("gx", "gy"), None), P("gx", "gy")),
        check_vma=False,
    )
```

profile of v0, /device:TPU:0, one launch (start us, length us, event | category | flops | bytes accessed | tf_op | source)
XLA Modules:
  0.0 1051.7 jit_solution(8544628376351971194)
XLA Ops:
  1.6 5.0 collective-permute-start.4
  6.6 1.3 collective-permute-start.5
  8.3 33.1 %while.112 = (s32[]{:T(128)}, f32[64,512]{1,0:T(8,128)S(1)}, f32[16,64,512]{2,1,0:T(8,128)S(1)}, f32[16,64,512]{2,1,0:T(8,128)}, f32[64,512]{1,0:T(8,128)S(1)}, ...) while((s32[]{:T(128)}, f32[64,512]{1,0:T(8,128)S(1)}, f32[16,64,512]{2,1,0:T(8,128)S(1)}, ...), condition=%wide.region_1.2_spmd, body=%wide.region_0.1_spmd.sunk | while | flops 753666 | bytes 1572957 | solution.py:42
  41.5 1.6 broadcast.174.clone.5
  43.1 14.5 %while.113 = (s32[]{:T(128)}, f32[64,512]{1,0:T(8,128)S(1)}, f32[16,64,512]{2,1,0:T(8,128)}, f32[16,64,512]{2,1,0:T(8,128)S(1)}, f32[64,512]{1,0:T(8,128)S(1)}, ...) while((s32[]{:T(128)}, f32[64,512]{1,0:T(8,128)S(1)}, f32[16,64,512]{2,1,0:T(8,128)}, ...), condition=%wide.region_3.4_spmd, body=%wide.region_2.3_spmd.sunk | while | flops 753666 | bytes 1573465 | solution.py:42
  57.9 33.1 %while.114 = (s32[]{:T(128)}, f32[64,512]{1,0:T(8,128)S(1)}, f32[16,64,512]{2,1,0:T(8,128)S(1)}, f32[16,64,512]{2,1,0:T(8,128)}, f32[64,512]{1,0:T(8,128)S(1)}, ...) while((s32[]{:T(128)}, f32[64,512]{1,0:T(8,128)S(1)}, f32[16,64,512]{2,1,0:T(8,128)S(1)}, ...), condition=%wide.region_5.6_spmd, body=%wide.region_4.5_spmd.sunk | while | flops 753666 | bytes 1572957 | solution.py:42
  91.0 1.6 broadcast.174.clone.3
  92.6 14.5 %while.115 = (s32[]{:T(128)}, f32[64,512]{1,0:T(8,128)S(1)}, f32[16,64,512]{2,1,0:T(8,128)}, f32[16,64,512]{2,1,0:T(8,128)S(1)}, f32[64,512]{1,0:T(8,128)S(1)}, ...) while((s32[]{:T(128)}, f32[64,512]{1,0:T(8,128)S(1)}, f32[16,64,512]{2,1,0:T(8,128)}, ...), condition=%wide.region_7.8_spmd, body=%wide.region_6.7_spmd.sunk | while | flops 753666 | bytes 1573465 | solution.py:42
  107.4 33.1 %while.116 = (s32[]{:T(128)}, f32[64,512]{1,0:T(8,128)S(1)}, f32[16,64,512]{2,1,0:T(8,128)S(1)}, f32[16,64,512]{2,1,0:T(8,128)}, f32[64,512]{1,0:T(8,128)S(1)}, ...) while((s32[]{:T(128)}, f32[64,512]{1,0:T(8,128)S(1)}, f32[16,64,512]{2,1,0:T(8,128)S(1)}, ...), condition=%wide.region_9.10_spmd, body=%wide.region_8.9_spmd.sunk | while | flops 753666 | bytes 1572957 | solution.py:42
  140.5 1.6 broadcast.174.clone.1
  142.1 14.5 %while.117 = (s32[]{:T(128)}, f32[64,512]{1,0:T(8,128)S(1)}, f32[16,64,512]{2,1,0:T(8,128)}, f32[16,64,512]{2,1,0:T(8,128)S(1)}, f32[64,512]{1,0:T(8,128)S(1)}, ...) while((s32[]{:T(128)}, f32[64,512]{1,0:T(8,128)S(1)}, f32[16,64,512]{2,1,0:T(8,128)}, ...), condition=%wide.region_11.12_spmd, body=%wide.region_10.11_spmd.sunk | while | flops 753666 | bytes 1573465 | solution.py:42
  156.9 33.1 %while.118 = (s32[]{:T(128)}, f32[64,512]{1,0:T(8,128)S(1)}, f32[16,64,512]{2,1,0:T(8,128)S(1)}, f32[16,64,512]{2,1,0:T(8,128)}, f32[64,512]{1,0:T(8,128)S(1)}, ...) while((s32[]{:T(128)}, f32[64,512]{1,0:T(8,128)S(1)}, f32[16,64,512]{2,1,0:T(8,128)S(1)}, ...), condition=%wide.region_13.14_spmd, body=%wide.region_12.13_spmd.sunk | while | flops 753666 | bytes 1572957 | solution.py:42
  190.0 1.6 broadcast.174
  191.6 14.5 %while.119 = (s32[]{:T(128)}, f32[64,512]{1,0:T(8,128)S(1)}, f32[16,64,512]{2,1,0:T(8,128)}, f32[16,64,512]{2,1,0:T(8,128)S(1)}, f32[64,512]{1,0:T(8,128)S(1)}, ...) while((s32[]{:T(128)}, f32[64,512]{1,0:T(8,128)S(1)}, f32[16,64,512]{2,1,0:T(8,128)}, ...), condition=%wide.region_15.16_spmd, body=%wide.region_14.15_spmd.sunk | while | flops 753666 | bytes 1573465 | solution.py:42
  207.3 226.4 %scatter_custom_fusion = f32[16384]{0:T(1024)S(1)} fusion(s32[32768]{0:T(1024)S(1)} %bitcast.338, f32[32768]{0:T(1024)S(1)} %bitcast.337, f32[]{:T(128)} %constant.333.clone.1), kind=kCustom, calls=%fused_computation.121 | custom fusion | flops 32768 | bytes 65540 | tf_op jit(solution)/shard_map/scatter-add | solution.py:99
  434.2 4.6 collective-permute-start
  439.0 1.3 collective-permute-start.1
  442.4 1.3 collective-permute-start.7
  445.0 3.4 collective-permute-start.2
  448.3 1.3 collective-permute-start.3
  450.3 5.5 fusion.73
  455.9 5.0 collective-permute-start.8
  460.8 1.3 collective-permute-start.9
  462.2 5.1 collective-permute-done.9
  467.3 3.1 collective-permute-start.10
  470.4 1.3 collective-permute-start.11
  471.7 4.2 collective-permute-done.11
  476.4 5.5 fusion.74
  482.5 43.2 %all-reduce.6 = (f32[]{:T(128)}, f32[]{:T(128)}) all-reduce(f32[]{:T(128)} %get-tuple-element.744, f32[]{:T(128)} %get-tuple-element.743), channel_id=1, replica_groups=mesh['gx'=8,'gy'=4] {'gx','gy'}, use_global_device_ids=true, to_apply=%region_18.19 | all-reduce | flops 2 | bytes 16 | tf_op jit(solution)/shard_map/psum | solution.py:56
  527.1 4.4 collective-permute-start.12
  531.5 1.3 collective-permute-start.13
  532.8 4.2 collective-permute-done.13
  537.0 1.4 collective-permute-start.14
  539.7 2.0 collective-permute-done.15
  542.4 5.5 fusion.75
  548.5 42.5 %all-reduce.5 = (f32[]{:T(128)}, f32[]{:T(128)}) all-reduce(f32[]{:T(128)} %get-tuple-element.742, f32[]{:T(128)} %get-tuple-element.741), channel_id=1, replica_groups=mesh['gx'=8,'gy'=4] {'gx','gy'}, use_global_device_ids=true, to_apply=%region_22.23 | all-reduce | flops 2 | bytes 16 | tf_op jit(solution)/shard_map/psum | solution.py:56
  595.5 4.4 collective-permute-start.16
  599.9 1.3 collective-permute-start.17
  601.4 4.0 collective-permute-done.17
  606.7 1.3 collective-permute-start.19
  608.2 193.9 %gather_fusion.4 = s32[32768]{0:T(1024)S(1)} fusion(s32[128]{0:T(128)S(1)} %reshape_squeeze.3, s32[32768]{0:T(1024)S(1)} %broadcast_clamp_fusion.1), kind=kCustom, calls=%fused_computation.4 | custom fusion | bytes 393216 | tf_op jit(solution)/shard_map/gather | solution.py:137
  802.8 5.5 fusion.76
  808.9 43.1 %all-reduce.4 = (f32[]{:T(128)}, f32[]{:T(128)}) all-reduce(f32[]{:T(128)} %get-tuple-element.740, f32[]{:T(128)} %get-tuple-element.739), channel_id=1, replica_groups=mesh['gx'=8,'gy'=4] {'gx','gy'}, use_global_device_ids=true, to_apply=%region_26.27 | all-reduce | flops 2 | bytes 16 | tf_op jit(solution)/shard_map/psum | solution.py:56
  855.9 4.4 collective-permute-start.20
  861.9 3.9 collective-permute-done.21
  867.1 1.3 collective-permute-start.23
  868.4 2.0 collective-permute-done.23
  870.4 180.5 %gather_fusion.5 = f32[32768]{0:T(1024)S(1)} fusion(f32[9216]{0:T(1024)S(1)} %bitcast.317, s32[32768]{0:T(1024)S(1)} %broadcast_clamp_fusion), kind=kCustom, calls=%fused_computation.5 | custom fusion | bytes 393216 | tf_op jit(solution)/shard_map/gather | solution.py:141
  (355 shorter events, 207.0 us)
Async XLA Ops:
  0.6 7.4 copy-start.3
  1.6 6.7 copy-start
  1.6 6.7 copy-start.1
  1.6 439.5 %collective-permute-start.4 = (f32[1,1,8,128]{3,2,1,0:T(8,128)}, f32[1,1,8,128]{3,2,1,0:T(8,128)S(1)}, u32[]{:S(2)}, u32[]{:S(2)}) collective-permute-start(f32[1,1,8,128]{3,2,1,0:T(8,128)} %bitcast.351), channel_id=1, source_target_pairs={{0,4},{4,8},{8,12},{12,16},{16,20},{20,24},{24,28},{1,5},{5,9},{9,... | collective-permute-start | bytes 12296 | tf_op jit(solution)/shard_map/ppermute | solution.py:21
  6.6 434.5 %collective-permute-start.5 = (f32[1,1,8,128]{3,2,1,0:T(8,128)}, f32[1,1,8,128]{3,2,1,0:T(8,128)S(1)}, u32[]{:S(2)}, u32[]{:S(2)}) collective-permute-start(f32[1,1,8,128]{3,2,1,0:T(8,128)} %bitcast.352), channel_id=1, source_target_pairs={{4,0},{8,4},{12,8},{16,12},{20,16},{24,20},{28,24},{5,1},{9,5},{13... | collective-permute-start | bytes 12296 | tf_op jit(solution)/shard_map/ppermute | solution.py:23
  191.6 242.0 %copy-start.4 = (s32[1,32,4]{1,2,0:T(4,128)S(1)}, s32[1,32,4]{1,2,0:T(4,128)}, u32[]{:S(2)}) copy-start(s32[1,32,4]{1,2,0:T(4,128)} %param.32) | copy-start | bytes 1540
  191.6 249.5 %copy-start.5 = (f32[8,128]{1,0:T(8,128)S(1)}, f32[8,128]{1,0:T(8,128)}, u32[]{:S(2)}) copy-start(f32[8,128]{1,0:T(8,128)} %param.33) | copy-start | bytes 12292
  434.2 9.6 collective-permute-start
  439.0 6.0 collective-permute-start.1
  441.1 8.5 collective-permute-start.6
  442.4 7.2 collective-permute-start.7
  445.0 10.8 %collective-permute-start.2 = (f32[4,1,8,128]{3,2,1,0:T(8,128)S(1)}, f32[4,1,8,128]{3,2,1,0:T(8,128)S(1)}, u32[]{:S(2)}, u32[]{:S(2)}) collective-permute-start(f32[4,1,8,128]{3,2,1,0:T(8,128)S(1)} %get-tuple-element.868), channel_id=1, source_target_pairs={{0,1},{1,2},{2,3},{4,5},{5,6},{6,7},{8,9},{9,10},{10,11},{12,13},{... | collective-permute-start | bytes 49160 | tf_op jit(solution)/shard_map/ppermute | solution.py:21
  448.3 7.4 collective-permute-start.3
  455.9 6.3 collective-permute-start.8
  460.8 6.4 collective-permute-start.9
  467.3 4.4 collective-permute-start.10
  470.4 5.5 collective-permute-start.11
  527.1 5.7 collective-permute-start.12
  531.5 5.5 collective-permute-start.13
  537.0 64.2 %copy-start.2 = (s32[64,512]{1,0:T(8,128)S(1)}, s32[64,512]{1,0:T(8,128)}, u32[]{:S(2)}) copy-start(s32[64,512]{1,0:T(8,128)} %param.31) | copy-start | bytes 393220
  537.0 2.7 collective-permute-start.14
  538.4 3.3 collective-permute-start.15
  595.5 5.8 collective-permute-start.16
  599.9 5.5 collective-permute-start.17
  605.4 196.7 %collective-permute-start.18 = (f32[3,1,8,128]{3,2,1,0:T(8,128)S(1)}, f32[3,1,8,128]{3,2,1,0:T(8,128)S(1)}, u32[]{:S(2)}, u32[]{:S(2)}) collective-permute-start(f32[3,1,8,128]{3,2,1,0:T(8,128)S(1)} %pad_maximum_fusion.9), channel_id=1, source_target_pairs={{0,1},{1,2},{2,3},{4,5},{5,6},{6,7},{8,9},{9,10},{10,11},{12,13},{... | collective-permute-start | bytes 36872 | tf_op jit(solution)/shard_map/ppermute | solution.py:21
  606.7 195.5 %collective-permute-start.19 = (f32[3,1,8,128]{3,2,1,0:T(8,128)S(1)}, f32[3,1,8,128]{3,2,1,0:T(8,128)S(1)}, u32[]{:S(2)}, u32[]{:S(2)}) collective-permute-start(f32[3,1,8,128]{3,2,1,0:T(8,128)S(1)} %pad_maximum_fusion.9), channel_id=1, source_target_pairs={{1,0},{2,1},{3,2},{5,4},{6,5},{7,6},{9,8},{10,9},{11,10},{13,12},{... | collective-permute-start | bytes 36872 | tf_op jit(solution)/shard_map/ppermute | solution.py:23
  855.9 195.1 %copy-start.6 = (f32[8,128]{1,0:T(8,128)}, f32[8,128]{1,0:T(8,128)S(1)}, u32[]{:S(2)}) copy-start(f32[8,128]{1,0:T(8,128)S(1)} %multiply_add_fusion.8) | copy-start | bytes 12292
  855.9 6.0 collective-permute-start.20
  860.3 5.5 collective-permute-start.21
  865.8 2.6 collective-permute-start.22
  867.1 3.4 collective-permute-start.23
where the time goes:
time: 1060 us; the launch traced here: 1050 us
  other arithmetic  418 us (39%)
  local copies, waits for them, and re-layouts  387 us (37%)
  blocking collectives  129 us (12%)
  starting transfers between devices  54.8 us (5%)
  waiting for transfers between devices  26.7 us (3%)
  matrix products  22.5 us (2%)
  between operations  11.1 us (1%)
    scatter-add x1, other arithmetic, body(): jax.ops.segment_sum(recharge.reshape(-1), column_target.reshape(-1), num_...  226 us
    gather x2, local copies, waits for them, and re-layouts, body(): block = my_ids.reshape(-1)[column_target // width]  194 us
    gather x2, local copies, waits for them, and re-layouts, body(): framed_back.reshape(-1)[place * width + column_target % width]  181 us
    psum x3, blocking collectives, paired(): lax.psum((jnp.sum(residual * residual), jnp.sum(residual * image)), ('gx'...  129 us
    dynamic_update_slice x128, other arithmetic, soil_sweeps(): bottom, water_content = lax.scan(layer, infiltration, water_content)  115 us
    add x128, other arithmetic, layer(): return (conduct_now + slope * change, content + change)  73.8 us
    ppermute x12, starting transfers between devices, padded(): lax.ppermute(tail, axis, [(i, (i + 1) % count) for i in range(ends)])  39.3 us
    ppermute x12, waiting for transfers between devices, padded(): lax.ppermute(head, axis, [((i + 1) % count, i) for i in range(ends)])  26.6 us
  transfers between devices with their start and end apart: 24, of which 8 were waited for; matrix products, arithmetic and copies ran while one was open for 60% of the time, Pallas kernels for 0%

commit v1 on v0

v1 whole, which is shorter than its diff:
```python
import functools

import jax
import jax.numpy as jnp
from jax import lax
from jax.experimental import pallas as pl
from jax.experimental.pallas import tpu as pltpu
from jax.sharding import PartitionSpec as P

SWEEPS = 8
RESIDUAL = 0.05
SIDES = 4
BOTH = ("gx", "gy")
F32 = jnp.float32


def partner_of(index, count, odd):
    other = ((index - odd) ^ 1) + odd
    return other, 0 <= index - odd and 0 <= other < count


def swaps(gx_count, gy_count):
    perms = []
    for axis, odd in ((1, 0), (1, 1), (0, 0), (0, 1)):
        perm = []
        for x in range(gx_count):
            for y in range(gy_count):
                if axis == 1:
                    other, fits = partner_of(y, gy_count, odd)
                    across = gy_count - 1 - y if gy_count % 2 == 0 else y
                    target = (x, other if fits else across)
                else:
                    other, fits = partner_of(x, gx_count, odd)
                    beside = y ^ 1 if gy_count % 2 == 0 and gx_count % 2 == 0 else y
                    target = (other, y) if fits else (x, beside)
                perm.append((x * gy_count + y, target[0] * gy_count + target[1]))
        perms.append(perm)
    return perms


def owners_here(gx_count, gy_count):
    x = lax.axis_index("gx")
    y = lax.axis_index("gy")

    def neighbour(index, count, odd, make):
        other = ((index - odd) ^ 1) + odd
        fits = (index >= odd) & (other < count)
        return jnp.where(fits, make(other), -1)

    along = lambda other: x * gy_count + other
    across = lambda other: other * gy_count + y
    return [
        x * gy_count + y,
        neighbour(y, gy_count, 0, along),
        neighbour(y, gy_count, 1, along),
        neighbour(x, gx_count, 0, across),
        neighbour(x, gx_count, 1, across),
    ]


def slot_keys(owner_ref, slots, rows):
    row = lax.broadcasted_iota(jnp.int32, (rows, 128), 0)
    keys = jnp.full((rows, 128), -1, jnp.int32)
    for k in range(SIDES + 1):
        owner = owner_ref[0, k]
        inside = (row >= k * slots) & (row < (k + 1) * slots) & (owner >= 0)
        keys = jnp.where(inside, owner * slots + row - k * slots, keys)
    return keys


def soil_kernel(
    own_blocks, slots, width,
    owner_ref, send_ref, pattern_ref,
    water_ref, porosity_ref, conduct_ref, exponent_ref, inflow_ref, target_ref, heads_ref,
    soil_ref, index_ref, own_ref, *rest,
):
    side_refs = rest[:SIDES]
    offset_ref, recharge_ref, totals_ref = rest[SIDES:]
    step = pl.program_id(0)
    steps = pl.num_programs(0)
    layers, rows, columns = water_ref.shape
    hi_rows = -(-(SIDES + 1) * slots // 8) * 8

    @pl.when(step == 0)
    def _():
        totals_ref[...] = jnp.zeros_like(totals_ref)

    exponent = exponent_ref[...]
    offset_ref[...] = jnp.log2(conduct_ref[...]) - exponent * jnp.log2(porosity_ref[...] - RESIDUAL)
    recharge_ref[...] = jnp.zeros_like(recharge_ref)
    soil_ref[...] = water_ref[...] - RESIDUAL

    def layer(flux, content):
        power = exponent_ref[...]
        conduct_now = jnp.exp2(power * jnp.log2(content) + offset_ref[...])
        steep = power * conduct_now
        share = (flux - conduct_now) * pl.reciprocal(content + steep)
        return conduct_now + steep * share, content + content * share

    pair = 2

    @pl.loop(0, SWEEPS // pair)
    def _(_):
        fluxes = [inflow_ref[...] for _ in range(pair)]
        for diagonal in range(layers + pair - 1):
            for sweep in range(pair):
                at = diagonal - sweep
                if 0 <= at < layers:
                    flux, content = layer(fluxes[sweep], soil_ref[at])
                    fluxes[sweep] = flux
                    soil_ref[at] = content
        recharge_ref[...] += fluxes[0] + fluxes[1]

    soil_ref[...] = soil_ref[...] + RESIDUAL

    keys = slot_keys(owner_ref, slots, hi_rows)
    keys = jnp.concatenate([keys] * (columns // 128), axis=1)
    cell = lax.broadcasted_iota(jnp.int32, (width, columns), 0)

    @pl.loop(0, rows)
    def _(row):
        target = target_ref[pl.ds(row, 1), :]
        value = recharge_ref[pl.ds(row, 1), :]
        cells = jnp.broadcast_to(target & (width - 1), (width, columns))
        one_hot = jnp.where(cells == cell, 1.0, 0.0).astype(jnp.bfloat16)
        high = value.astype(jnp.bfloat16).astype(F32)
        low = value - high
        hit = jnp.broadcast_to(target // width, (hi_rows, columns)) == keys
        spread = jnp.concatenate(
            [
                jnp.where(hit, jnp.broadcast_to(high, (hi_rows, columns)), 0.0),
                jnp.where(hit, jnp.broadcast_to(low, (hi_rows, columns)), 0.0),
            ],
            axis=0,
        ).astype(jnp.bfloat16)
        totals_ref[...] += lax.dot_general(
            one_hot, spread, (((1,), (1,)), ((), ())), preferred_element_type=F32
        )

    @pl.when(step == steps - 1)
    def _():
        totals = totals_ref[...]
        padded = jnp.concatenate([totals, jnp.zeros((width, 128 - totals.shape[1]), F32)], axis=1)
        turned = padded.T
        sums = turned[:hi_rows] + turned[hi_rows : 2 * hi_rows]
        block = lax.broadcasted_iota(jnp.int32, (own_blocks, width), 0)
        for k in range(SIDES + 1):
            owner = owner_ref[0, k]
            placed = jnp.zeros((own_blocks, width), F32)
            for slot in range(slots):
                ident = send_ref[0, jnp.maximum(owner, 0), slot]
                at = k * slots + slot
                placed = placed + jnp.where(block == ident, sums[at : at + 1], 0.0)
            if k == 0:
                own_ref[...] = placed
            else:
                side_refs[k - 1][0:own_blocks, :] = placed
                side_refs[k - 1][own_blocks : 2 * own_blocks, :] = heads_ref[...]
        for r in range(own_blocks):
            for k in range(pattern_ref.shape[1]):
                ident = pattern_ref[r, k]
                owner = ident // own_blocks
                place = (SIDES + 1) * own_blocks
                for side in range(SIDES + 1):
                    fits = (owner == owner_ref[0, side]) & (ident >= 0)
                    place = jnp.where(fits, side * own_blocks + ident % own_blocks, place)
                index_ref[r, k] = place


def operate(index_ref, blocks_ref, table_ref):
    own_blocks, most, width = blocks_ref.shape[:3]
    image = jnp.zeros((own_blocks, width), F32)
    row = lax.broadcasted_iota(jnp.int32, (own_blocks, 3 * width), 0)
    for r in range(own_blocks):
        total = jnp.zeros((width, width), F32)
        for k in range(most):
            total = total + blocks_ref[r, k] * table_ref[pl.ds(index_ref[r, k], 1), :]
        first = total.astype(jnp.bfloat16)
        rest = total - first.astype(F32)
        second = rest.astype(jnp.bfloat16)
        third = (rest - second.astype(F32)).astype(jnp.bfloat16)
        parts = jnp.concatenate([first, second, third], axis=1)
        ones = jnp.where(row == r, 1.0, 0.0).astype(jnp.bfloat16)
        image = image + lax.dot_general(
            ones, parts, (((1,), (1,)), ((), ())), preferred_element_type=F32
        )
    return image


def fill_table(table_ref, own, sides, own_blocks):
    table_ref[0:own_blocks, :] = own
    for k, side in enumerate(sides):
        table_ref[(k + 1) * own_blocks : (k + 2) * own_blocks, :] = side
    table_ref[(SIDES + 1) * own_blocks :, :] = jnp.zeros((own_blocks, own.shape[1]), F32)


def start_kernel(area, index_ref, blocks_ref, own_ref, heads_ref, *rest):
    side_refs, (residual_ref, table_ref) = rest[:SIDES], rest[SIDES:]
    own_blocks = heads_ref.shape[0]
    fill_table(table_ref, heads_ref[...], [s[own_blocks:, :] for s in side_refs], own_blocks)
    cells = own_ref[...]
    for side in side_refs:
        cells = cells + side[:own_blocks, :]
    residual_ref[...] = heads_ref[...] + area * cells - operate(index_ref, blocks_ref, table_ref)


def apply_kernel(index_ref, blocks_ref, field_ref, *rest):
    side_refs, (image_ref, table_ref) = rest[:SIDES], rest[SIDES:]
    fill_table(table_ref, field_ref[...], [s[...] for s in side_refs], field_ref.shape[0])
    image_ref[...] = operate(index_ref, blocks_ref, table_ref)


def whole_sum(values):
    return jnp.sum(jnp.sum(values, axis=0, keepdims=True), axis=1, keepdims=True)


def last_kernel(index_ref, blocks_ref, r_ref, w_ref, field_ref, *rest):
    side_refs, (sums_ref, table_ref) = rest[:SIDES], rest[SIDES:]
    fill_table(table_ref, field_ref[...], [s[...] for s in side_refs], field_ref.shape[0])
    z = operate(index_ref, blocks_ref, table_ref)
    r, w, v = r_ref[...], w_ref[...], field_ref[...]
    rr = whole_sum(r * r)
    ratio = whole_sum(w * w) / rr
    shift = jnp.where((ratio > 0.0) & (ratio < 1e30), jnp.sqrt(ratio), 1.0)
    inverse = 1.0 / shift
    w1 = w * inverse - r
    v1 = (v * inverse - w) * inverse
    z1 = ((z * inverse - v) * inverse) * inverse
    v2 = v1 - w1
    z2 = z1 - v1
    z3 = z2 - v2
    sums = [
        rr, shift,
        whole_sum(r * w1), whole_sum(w1 * w1), whole_sum(r * v2), whole_sum(w1 * v2), whole_sum(v2 * v2),
        whole_sum(r * z3), whole_sum(w1 * z3), whole_sum(v2 * z3),
    ]
    lane = lax.broadcasted_iota(jnp.int32, (1, 128), 1)
    packed = jnp.zeros((1, 128), F32)
    for position, value in enumerate(sums):
        packed = jnp.where(lane == position, value, packed)
    sums_ref[...] = jnp.broadcast_to(packed[None], sums_ref.shape)


def solve_step(all_sums):
    lane = lax.broadcasted_iota(jnp.int32, all_sums.shape, 1)

    def take(position):
        return jnp.sum(jnp.where(lane == position, all_sums, 0.0), axis=1, keepdims=True)

    rr, shift, rw, ww, rv, wv, vv, rz, wz, vz = [take(p) for p in range(10)]

    def over(values):
        return jnp.sum(values, axis=0, keepdims=True)

    m0 = over(rr)
    theta = over(shift * (rw + rr)) / m0
    ratio = shift / theta
    e = ratio - 1.0
    p2 = ratio * ratio
    p3 = p2 * ratio
    p4 = p2 * p2
    rw, ww, rv = rw * ratio, ww * p2, rv * p2
    wv, rz = wv * p3, rz * p3
    vv, wz = vv * p4, wz * p4
    vz = vz * (p4 * ratio)
    e2 = e * e
    twice = 2.0 * e
    new_w_r = rw + e * rr
    new_w_w = ww + e * rw
    new_v_r = rv + twice * rw + e2 * rr
    new_v_w = wv + twice * ww + e2 * rw
    new_v_v = vv + twice * wv + e2 * rv
    m1 = over(new_w_r)
    m2 = over(new_w_w + e * new_w_r)
    m3 = over(wv + e * rv + twice * new_w_w + e2 * new_w_r)
    m4 = over(new_v_v + twice * new_v_w + e2 * new_v_r)
    m5 = over(vz + twice * wz + e2 * rz + 3.0 * e * new_v_v + 3.0 * e2 * new_v_w + e * e2 * new_v_r)
    a00, a01, a02 = m0 + m1, m1 + m2, m2 + m3
    a11, a12, a22 = m2 + m3, m3 + m4, m4 + m5
    f1 = a01 / a00
    f2 = a02 / a00
    b11 = a11 - f1 * a01
    b12 = a12 - f1 * a02
    b22 = a22 - f2 * a02
    g1 = m1 - f1 * m0
    g2 = m2 - f2 * m0
    f3 = b12 / b11
    y2 = (g2 - f3 * g1) / (b22 - f3 * b12)
    y1 = (g1 - b12 * y2) / b11
    y0 = (m0 - a01 * y1 - a02 * y2) / a00
    inverse = 1.0 / theta
    y2 = y2 * inverse
    return (y0 - y1) * inverse + y2, (y1 * inverse - 2.0 * y2) * inverse, y2 * inverse * inverse


def heads_kernel(slots, owner_ref, send_ref, all_ref, target_ref, heads_ref, r_ref, w_ref, v_ref, *rest):
    sides = rest[: 4 * SIDES]
    heads_out, columns_out, table_ref, slot_ref, keys_ref = rest[4 * SIDES :]
    own_blocks, width = heads_ref.shape
    hi_rows = keys_ref.shape[0]
    weight_r, weight_w, weight_v = solve_step(all_ref[:, 0, :])

    def new_heads(heads, r, w, v):
        return heads + weight_r * r + weight_w * w + weight_v * v

    mine = new_heads(heads_ref[...], r_ref[...], w_ref[...], v_ref[...])
    heads_out[...] = mine
    table_ref[0:own_blocks, :] = mine
    for k in range(SIDES):
        old, r, w, v = sides[4 * k : 4 * k + 4]
        table_ref[(k + 1) * own_blocks : (k + 2) * own_blocks, :] = new_heads(
            old[own_blocks:, :], r[...], w[...], v[...]
        )
    for k in range(SIDES + 1):
        owner = jnp.maximum(owner_ref[0, k], 0)
        for slot in range(slots):
            ident = jnp.maximum(send_ref[0, owner, slot], 0)
            slot_ref[k * slots + slot : k * slots + slot + 1, :] = table_ref[
                pl.ds(k * own_blocks + ident, 1), :
            ]
    keys_ref[...] = slot_keys(owner_ref, slots, hi_rows)
    rows, columns = target_ref.shape
    entries = (SIDES + 1) * slots

    @pl.loop(0, rows // 8)
    def _(step):
        at = pl.multiple_of(step * 8, 8)
        for part in range(columns // 128):
            target = target_ref[pl.ds(at, 8), part * 128 : (part + 1) * 128]
            lanes = target & (width - 1)
            key = target // width
            found = jnp.zeros((8, 128), F32)
            for entry in range(entries):
                table = jnp.broadcast_to(slot_ref[entry : entry + 1, :], (8, 128))
                values = jnp.take_along_axis(table, lanes, axis=1, mode="promise_in_bounds")
                wanted = jnp.broadcast_to(keys_ref[entry : entry + 1, :], (8, 128))
                found = jnp.where(key == wanted, values, found)
            columns_out[pl.ds(at, 8), part * 128 : (part + 1) * 128] = found


VMEM = pl.BlockSpec(memory_space=pltpu.VMEM)
SMEM = pl.BlockSpec(memory_space=pltpu.SMEM)


def body(
    water_content,
    porosity,
    conduct,
    exponent,
    infiltration,
    column_target,
    send_blocks,
    prior_heads,
    block_pattern,
    aquifer_blocks,
    gx_count,
    gy_count,
):
    devices, slots = send_blocks.shape[1:]
    own_blocks, width = prior_heads.shape
    layers, rows, columns = water_content.shape
    most = block_pattern.shape[1]
    hi_rows = -(-(SIDES + 1) * slots // 8) * 8
    area = own_blocks * width / (rows * columns)
    perms = swaps(gx_count, gy_count)
    owners = jnp.stack(owners_here(gx_count, gy_count)).astype(jnp.int32).reshape(1, SIDES + 1)
    blocks = pltpu.with_memory_space_constraint(aquifer_blocks, pltpu.VMEM)
    in_hbm = lambda array: pltpu.with_memory_space_constraint(array, pltpu.HBM)
    field = jax.ShapeDtypeStruct((own_blocks, width), F32)
    two = jax.ShapeDtypeStruct((2 * own_blocks, width), F32)
    table = pltpu.VMEM(((SIDES + 2) * own_blocks, width), F32)

    def trade(array):
        return [lax.ppermute(array, BOTH, perm) for perm in perms]

    chunk = 16
    flat = pl.BlockSpec((chunk, columns), lambda i: (i, 0))
    deep = pl.BlockSpec((layers, chunk, columns), lambda i: (0, i, 0))
    whole = lambda shape: pl.BlockSpec(shape, lambda i: (0,) * len(shape))
    outs = pl.pallas_call(
        functools.partial(soil_kernel, own_blocks, slots, width),
        grid=(rows // chunk,),
        in_specs=[SMEM, SMEM, SMEM, deep, flat, flat, flat, flat, flat, whole((own_blocks, width))],
        out_specs=[deep, SMEM, whole((own_blocks, width))] + [whole((2 * own_blocks, width))] * SIDES,
        out_shape=[
            jax.ShapeDtypeStruct(water_content.shape, F32),
            jax.ShapeDtypeStruct((own_blocks, most), jnp.int32),
            field,
        ]
        + [two] * SIDES,
        scratch_shapes=[
            pltpu.VMEM((chunk, columns), F32),
            pltpu.VMEM((chunk, columns), F32),
            pltpu.VMEM((width, 2 * hi_rows), F32),
        ],
        compiler_params=pltpu.CompilerParams(vmem_limit_bytes=24 * 2**20),
        name="soil",
    )(
        owners, send_blocks, block_pattern,
        *map(in_hbm, (water_content, porosity, conduct, exponent, infiltration, column_target)),
        prior_heads,
    )
    soil_water, index, own = outs[:3]
    got = [lax.ppermute(out, BOTH, perm) for out, perm in zip(outs[3:], perms)]

    def small(kernel, args, shape, name):
        return pl.pallas_call(
            kernel,
            in_specs=[SMEM] + [VMEM] * (len(args) - 1),
            out_specs=VMEM,
            out_shape=shape,
            scratch_shapes=[table],
            compiler_params=pltpu.CompilerParams(vmem_limit_bytes=16 * 2**20),
            name=name,
        )(*args)

    r = small(functools.partial(start_kernel, area), (index, blocks, own, prior_heads, *got), field, "start")
    r_sides = trade(r)
    w = small(apply_kernel, (index, blocks, r, *r_sides), field, "once")
    w_sides = trade(w)
    v = small(apply_kernel, (index, blocks, w, *w_sides), field, "twice")
    v_sides = trade(v)
    sums = small(
        last_kernel, (index, blocks, r, w, v, *v_sides), jax.ShapeDtypeStruct((devices, 1, 128), F32), "sums"
    )
    all_sums = lax.all_to_all(sums, BOTH, 0, 0)
    sides = []
    for k in range(SIDES):
        sides += [got[k], r_sides[k], w_sides[k], v_sides[k]]
    heads, column_heads = pl.pallas_call(
        functools.partial(heads_kernel, slots),
        in_specs=[SMEM, SMEM] + [VMEM] * (6 + 4 * SIDES),
        out_specs=[VMEM, VMEM],
        out_shape=[field, jax.ShapeDtypeStruct((rows, columns), F32)],
        scratch_shapes=[
            pltpu.VMEM(((SIDES + 1) * own_blocks, width), F32),
            pltpu.VMEM((hi_rows, width), F32),
            pltpu.VMEM((hi_rows, width), jnp.int32),
        ],
        compiler_params=pltpu.CompilerParams(vmem_limit_bytes=16 * 2**20),
        name="heads",
    )(owners, send_blocks, all_sums, column_target, prior_heads, r, w, v, *sides)
    return soil_water, heads, column_heads


def solution(mesh):
    placed = (
        P(None, "gx", "gy"),
        P("gx", "gy"),
        P("gx", "gy"),
        P("gx", "gy"),
        P("gx", "gy"),
        P("gx", "gy"),
        P(("gx", "gy"), None, None),
        P(("gx", "gy"), None),
        P(("gx", "gy"), None),
        P(("gx", "gy"), None, None, None),
    )
    return jax.shard_map(
        functools.partial(body, gx_count=mesh.shape["gx"], gy_count=mesh.shape["gy"]),
        mesh=mesh,
        in_specs=placed,
        out_specs=(P(None, "gx", "gy"), P(("gx", "gy"), None), P("gx", "gy")),
        check_vma=False,
    )
```

time: 1060 us -> 72.5 us (0.07)
  other arithmetic: 418 us -> 0 us
  local copies, waits for them, and re-layouts: 387 us -> 4.27 us
  blocking collectives: 129 us -> 8.84 us
  starting transfers between devices: 54.8 us -> 18.2 us
  Pallas kernels: 0 us -> 31 us
  matrix products: 22.5 us -> 0 us
  waiting for transfers between devices: 26.7 us -> 9.27 us
    gather x8 -> x0, local copies, waits for them, and re-layouts: 377 us -> none  [the longest x2 194 us: body(): block = my_ids.reshape(-1)[column_target // width]]
    scatter-add x1 -> x0, other arithmetic: 226 us -> none  [body(): jax.ops.segment_sum(recharge.reshape(-1), column_target.reshape(-1), num_...]
    psum x3 -> x0, blocking collectives: 129 us -> none  [paired(): lax.psum((jnp.sum(residual * residual), jnp.sum(residual * image)), ('gx'...]
    dynamic_update_slice x128 -> x0, other arithmetic: 115 us -> none  [soil_sweeps(): bottom, water_content = lax.scan(layer, infiltration, water_content)]
    add x129 -> x0, other arithmetic: 73.8 us -> none  [the longest x128 73.8 us: layer(): return (conduct_now + slope * change, content + change)]
    ppermute x24 -> x16, starting transfers between devices: 54.8 us -> 18.2 us  [the longest x12 13.6 us: trade(): return [lax.ppermute(array, BOTH, perm) for perm in perms]]
    pallas_call x0 -> x6, Pallas kernels: none -> 31 us  [the longest x1 23.5 us: body(): pl.pallas_call(functools.partial(soil_kernel, own_blocks, slots, width),...]
    dot_general x9 -> x0, matrix products: 22.5 us -> none  [the longest x4 21.9 us: apply_operator(): jnp.einsum('rkij,rkj->ri', aquifer_blocks, fetch(field), precision=lax.Pr...]
  transfers between devices with their start and end apart: 24 -> 16, of which waited for: 8 -> 7; matrix products, arithmetic and copies ran while one was open for 60% -> 0% of each run, Pallas kernels for 0% -> 0%
where the time goes in v1:
time: 72.5 us; the launch traced here: 72.2 us
  Pallas kernels  31 us (43%)
  starting transfers between devices  18.2 us (25%)
  waiting for transfers between devices  9.27 us (13%)
  blocking collectives  8.84 us (12%)
  local copies, waits for them, and re-layouts  4.27 us (6%)
    pallas_call x1, Pallas kernels, body(): pl.pallas_call(functools.partial(soil_kernel, own_blocks, slots, width),...  23.5 us
    ppermute x12, starting transfers between devices, trade(): return [lax.ppermute(array, BOTH, perm) for perm in perms]  13.6 us
    all_to_all x1, blocking collectives, body(): all_sums = lax.all_to_all(sums, BOTH, 0, 0)  8.84 us
    ppermute x12, waiting for transfers between devices, trade(): return [lax.ppermute(array, BOTH, perm) for perm in perms]  7.15 us
    ppermute x4, starting transfers between devices, body(): got = [lax.ppermute(out, BOTH, perm) for out, perm in zip(outs[3:], perms)]  4.59 us
    pallas_call x4, Pallas kernels, small(): pl.pallas_call(kernel, in_specs=[SMEM] + [VMEM] * (len(args) - 1), out_sp...  4.43 us
    unnamed x11, local copies, waits for them, and re-layouts  4.18 us
    pallas_call x1, Pallas kernels, body(): pl.pallas_call(functools.partial(heads_kernel, slots), in_specs=[SMEM, SM...  3.03 us
  transfers between devices with their start and end apart: 16, of which 7 were waited for; matrix products, arithmetic and copies ran while one was open for 0% of the time, Pallas kernels for 0%

profile of v1, /device:TPU:0, one launch (start us, length us, event | category | flops | bytes accessed | tf_op | source)
XLA Modules:
  0.0 72.2 jit_solution(1034205199593097107)
XLA Ops:
  0.7 0.8 %copy.13.send_ref = s32[1,32,4]{2,1,0:T(8,128)S(1)} copy(s32[1,32,4]{1,2,0:T(4,128)} %param.16) | data formatting | bytes 1024 | tf_op args[6]
  1.4 0.1 stack.23
  1.5 0.0 copy-start.3
  1.5 0.7 copy-done.3
  2.2 0.0 copy-start.4
  2.2 0.7 copy-done.4
  2.9 23.5 %soil.1 = (f32[16,64,512]{2,1,0:T(8,128)}, s32[8,7]{1,0:T(8,128)S(1)}, f32[8,128]{1,0:T(8,128)S(1)}, f32[16,128]{1,0:T(8,128)S(1)}, f32[16,128]{1,0:T(8,128)S(1)...) custom-call(s32[1,5]{1,0:T(1,128)S(1)} %bitcast.6, s32[1,32,4]{2,1,0:T(8,128)S(1)} %copy.13.send_ref, ...), custom_call_target="tpu_custom_call" | custom-call | tf_op jit(solution)/shard_map/soil/pallas_call | solution.py:380
  26.4 0.5 collective-permute-start
  26.9 2.6 %collective-permute-start.1 = (f32[16,128]{1,0:T(8,128)S(1)}, f32[16,128]{1,0:T(8,128)S(1)}, u32[]{:S(2)}, u32[]{:S(2)}) collective-permute-start(f32[16,128]{1,0:T(8,128)S(1)} %get-tuple-element.16), channel_id=1, source_target_pairs={{0,3},{1,2},{2,1},{3,0},{4,7},{5,6},{6,5},{7,4},{8,11},{9,10},{10,... | collective-permute-start | bytes 24584 | tf_op jit(solution)/shard_map/ppermute | solution.py:404
  29.5 1.5 %collective-permute-start.2 = (f32[16,128]{1,0:T(8,128)S(1)}, f32[16,128]{1,0:T(8,128)S(1)}, u32[]{:S(2)}, u32[]{:S(2)}) collective-permute-start(f32[16,128]{1,0:T(8,128)S(1)} %get-tuple-element.17), channel_id=1, source_target_pairs={{0,4},{1,5},{2,6},{3,7},{4,0},{5,1},{6,2},{7,3},{8,12},{9,13},{10,... | collective-permute-start | bytes 24584 | tf_op jit(solution)/shard_map/ppermute | solution.py:404
  31.0 0.0 collective-permute-start.3
  31.0 0.0 collective-permute-done.rest_0_
  31.0 0.0 collective-permute-done.1.rest_1_.rest_4_
  31.0 2.1 %collective-permute-done.2.rest_2_.rest_8_ = f32[16,128]{1,0:T(8,128)S(1)} collective-permute-done((f32[16,128]{1,0:T(8,128)S(1)}, f32[16,128]{1,0:T(8,128)S(1)}, u32[]{:S(2)}, u32[]{:S(2)}) %collective-permute-start.2) | collective-permute-done | bytes 8224 | tf_op jit(solution)/shard_map/ppermute | solution.py:404
  33.1 0.0 collective-permute-done.3.rest_3_.rest_12_
  33.1 2.0 %copy-done = f32[8,7,128,128]{3,2,1,0:T(8,128)S(1)} copy-done((f32[8,7,128,128]{3,2,1,0:T(8,128)S(1)}, f32[8,7,128,128]{3,2,1,0:T(8,128)}, u32[]{:S(2)}) %copy-start) | copy-done | bytes 3670040
  35.2 1.1 %start.1.field_ref.r_ref = f32[8,128]{1,0:T(8,128)S(1)} custom-call(s32[8,7]{1,0:T(8,128)S(1)} %get-tuple-element.13.index_ref, f32[8,7,128,128]{3,2,1,0:T(8,128)S(1)} %copy-done, f32[8,128]{1,0:T(8,128)S(1)} %get-tuple-element.14.own_ref, f32[8,128]{1,0:T(8,128)S(1)} %copy-done.3, f32[16,128]{1,0:T(8,128)S(1)} %collective-permute-done.rest_0_, ...), custom_call_target="tpu_custom_call" | custom-call | tf_op jit(solution)/shard_map/start/pallas_call | solution.py:407
  36.3 0.0 collective-permute-start.7
  36.3 5.5 %collective-permute-start.6 = (f32[8,128]{1,0:T(8,128)S(1)}, f32[8,128]{1,0:T(8,128)S(1)}, u32[]{:S(2)}, u32[]{:S(2)}) collective-permute-start(f32[8,128]{1,0:T(8,128)S(1)} %start.1.field_ref.r_ref), channel_id=1, source_target_pairs={{0,4},{1,5},{2,6},{3,7},{4,0},{5,1},{6,2},{7,3},{8,12},{9,13},{10,... | collective-permute-start | bytes 12296 | tf_op jit(solution)/shard_map/ppermute | solution.py:374
  41.7 0.0 collective-permute-start.5
  41.7 0.6 collective-permute-start.4
  42.4 0.0 collective-permute-done.7.rest_3_.rest_13_
  42.4 0.9 %collective-permute-done.6.rest_2_.rest_9_ = f32[8,128]{1,0:T(8,128)S(1)} collective-permute-done((f32[8,128]{1,0:T(8,128)S(1)}, f32[8,128]{1,0:T(8,128)S(1)}, u32[]{:S(2)}, u32[]{:S(2)}) %collective-permute-start.6) | collective-permute-done | bytes 4128 | tf_op jit(solution)/shard_map/ppermute | solution.py:374
  43.3 1.4 %collective-permute-done.5.rest_1_.rest_5_ = f32[8,128]{1,0:T(8,128)S(1)} collective-permute-done((f32[8,128]{1,0:T(8,128)S(1)}, f32[8,128]{1,0:T(8,128)S(1)}, u32[]{:S(2)}, u32[]{:S(2)}) %collective-permute-start.5) | collective-permute-done | bytes 4128 | tf_op jit(solution)/shard_map/ppermute | solution.py:374
  44.8 0.0 collective-permute-done.4.rest_0_.rest_1_
  44.8 0.0 copy-done.1
  44.8 1.1 %once.1.field_ref.w_ref = f32[8,128]{1,0:T(8,128)S(1)} custom-call(s32[8,7]{1,0:T(8,128)S(1)} %get-tuple-element.13.index_ref, f32[8,7,128,128]{3,2,1,0:T(8,128)S(1)} %copy-done.1, f32[8,128]{1,0:T(8,128)S(1)} %start.1.field_ref.r_ref, f32[8,128]{1,0:T(8,128)S(1)} %collective-permute-done.4.rest_0_.rest_1_, ...), custom_call_target="tpu_custom_call" | custom-call | tf_op jit(solution)/shard_map/once/pallas_call | solution.py:407
  45.8 0.0 collective-permute-start.11
  45.9 3.1 %collective-permute-start.10 = (f32[8,128]{1,0:T(8,128)S(1)}, f32[8,128]{1,0:T(8,128)S(1)}, u32[]{:S(2)}, u32[]{:S(2)}) collective-permute-start(f32[8,128]{1,0:T(8,128)S(1)} %once.1.field_ref.w_ref), channel_id=1, source_target_pairs={{0,4},{1,5},{2,6},{3,7},{4,0},{5,1},{6,2},{7,3},{8,12},{9,13},{10,... | collective-permute-start | bytes 12296 | tf_op jit(solution)/shard_map/ppermute | solution.py:374
  48.9 0.0 collective-permute-start.9
  48.9 0.6 collective-permute-start.8
  49.6 0.0 collective-permute-done.11.rest_3_.rest_14_
  49.6 0.9 %collective-permute-done.10.rest_2_.rest_10_ = f32[8,128]{1,0:T(8,128)S(1)} collective-permute-done((f32[8,128]{1,0:T(8,128)S(1)}, f32[8,128]{1,0:T(8,128)S(1)}, u32[]{:S(2)}, u32[]{:S(2)}) %collective-permute-start.10) | collective-permute-done | bytes 4128 | tf_op jit(solution)/shard_map/ppermute | solution.py:374
  50.5 1.4 %collective-permute-done.9.rest_1_.rest_6_ = f32[8,128]{1,0:T(8,128)S(1)} collective-permute-done((f32[8,128]{1,0:T(8,128)S(1)}, f32[8,128]{1,0:T(8,128)S(1)}, u32[]{:S(2)}, u32[]{:S(2)}) %collective-permute-start.9) | collective-permute-done | bytes 4128 | tf_op jit(solution)/shard_map/ppermute | solution.py:374
  52.0 0.0 collective-permute-done.8.rest_0_.rest_2_
  52.0 1.1 %twice.1.field_ref.v_ref = f32[8,128]{1,0:T(8,128)S(1)} custom-call(s32[8,7]{1,0:T(8,128)S(1)} %get-tuple-element.13.index_ref, f32[8,7,128,128]{3,2,1,0:T(8,128)S(1)} %copy-done.1, f32[8,128]{1,0:T(8,128)S(1)} %once.1.field_ref.w_ref, f32[8,128]{1,0:T(8,128)S(1)} %collective-permute-done.8.rest_0_.rest_2_, ...), custom_call_target="tpu_custom_call" | custom-call | tf_op jit(solution)/shard_map/twice/pallas_call | solution.py:407
  53.0 0.0 collective-permute-start.15
  53.1 3.0 %collective-permute-start.14 = (f32[8,128]{1,0:T(8,128)S(1)}, f32[8,128]{1,0:T(8,128)S(1)}, u32[]{:S(2)}, u32[]{:S(2)}) collective-permute-start(f32[8,128]{1,0:T(8,128)S(1)} %twice.1.field_ref.v_ref), channel_id=1, source_target_pairs={{0,4},{1,5},{2,6},{3,7},{4,0},{5,1},{6,2},{7,3},{8,12},{9,13},{10,... | collective-permute-start | bytes 12296 | tf_op jit(solution)/shard_map/ppermute | solution.py:374
  56.1 0.0 collective-permute-start.13
  56.1 0.6 collective-permute-start.12
  56.7 0.0 collective-permute-done.15.rest_3_.rest_15_
  56.8 0.9 %collective-permute-done.14.rest_2_.rest_11_ = f32[8,128]{1,0:T(8,128)S(1)} collective-permute-done((f32[8,128]{1,0:T(8,128)S(1)}, f32[8,128]{1,0:T(8,128)S(1)}, u32[]{:S(2)}, u32[]{:S(2)}) %collective-permute-start.14) | collective-permute-done | bytes 4128 | tf_op jit(solution)/shard_map/ppermute | solution.py:374
  57.7 1.4 %collective-permute-done.13.rest_1_.rest_7_ = f32[8,128]{1,0:T(8,128)S(1)} collective-permute-done((f32[8,128]{1,0:T(8,128)S(1)}, f32[8,128]{1,0:T(8,128)S(1)}, u32[]{:S(2)}, u32[]{:S(2)}) %collective-permute-start.13) | collective-permute-done | bytes 4128 | tf_op jit(solution)/shard_map/ppermute | solution.py:374
  59.1 0.0 collective-permute-done.12.rest_0_.rest_3_
  59.1 1.2 %sums.1 = f32[32,1,128]{2,1,0:T(1,128)S(1)} custom-call(s32[8,7]{1,0:T(8,128)S(1)} %get-tuple-element.13.index_ref, f32[8,7,128,128]{3,2,1,0:T(8,128)S(1)} %copy-done.1, f32[8,128]{1,0:T(8,128)S(1)} %start.1.field_ref.r_ref, f32[8,128]{1,0:T(8,128)S(1)} %once.1.field_ref.w_ref, f32[8,128]{1,0:T(8,128)S(1)} %twice.1.field_ref.v_ref, ...), custom_call_target="tpu_custom_call" | custom-call | tf_op jit(solution)/shard_map/sums/pallas_call | solution.py:407
  60.3 8.8 %all_to_all.5.all_ref = f32[32,1,128]{2,1,0:T(1,128)S(1)} all-to-all(f32[32,1,128]{2,1,0:T(1,128)S(1)} %sums.1), channel_id=1, replica_groups=mesh['gx'=8,'gy'=4] {'gx','gy'}, dimensions={0} | all-to-all | bytes 32768 | tf_op jit(solution)/shard_map/all_to_all | solution.py:426
  69.2 0.0 copy-done.2
  69.2 3.0 %heads.1 = (f32[8,128]{1,0:T(8,128)}, f32[64,512]{1,0:T(8,128)}) custom-call(s32[1,5]{1,0:T(1,128)S(1)} %bitcast.7, s32[1,32,4]{2,1,0:T(8,128)S(1)} %copy.13.send_ref, f32[32,1,128]{2,1,0:T(1,128)S(1)} %all_to_all.5.all_ref, s32[64,512]{1,0:T(8,128)S(1)} %copy-done.2, f32[8,128]{1,0:T(8,128)S(1)} %copy-done.3, f32[8,128]{1,0:T(8,128)S(1)} %start.1.field_ref.r_ref, ...), custom_call_target="tpu_custom_call" | custom-call | tf_op jit(solution)/shard_map/heads/pallas_call | solution.py:430
  (3 shorter events, 0.0 us)
Async XLA Ops:
  1.5 0.7 copy-start.3
  2.2 0.7 copy-start.4
  26.4 4.6 %collective-permute-start = (f32[16,128]{1,0:T(8,128)S(1)}, f32[16,128]{1,0:T(8,128)S(1)}, u32[]{:S(2)}, u32[]{:S(2)}) collective-permute-start(f32[16,128]{1,0:T(8,128)S(1)} %get-tuple-element.15), channel_id=1, source_target_pairs={{0,1},{1,0},{2,3},{3,2},{4,5},{5,4},{6,7},{7,6},{8,9},{9,8},{10,11... | collective-permute-start | bytes 24584 | tf_op jit(solution)/shard_map/ppermute | solution.py:404
  26.9 4.1 %collective-permute-start.1 = (f32[16,128]{1,0:T(8,128)S(1)}, f32[16,128]{1,0:T(8,128)S(1)}, u32[]{:S(2)}, u32[]{:S(2)}) collective-permute-start(f32[16,128]{1,0:T(8,128)S(1)} %get-tuple-element.16), channel_id=1, source_target_pairs={{0,3},{1,2},{2,1},{3,0},{4,7},{5,6},{6,5},{7,4},{8,11},{9,10},{10,... | collective-permute-start | bytes 24584 | tf_op jit(solution)/shard_map/ppermute | solution.py:404
  29.5 3.7 %collective-permute-start.2 = (f32[16,128]{1,0:T(8,128)S(1)}, f32[16,128]{1,0:T(8,128)S(1)}, u32[]{:S(2)}, u32[]{:S(2)}) collective-permute-start(f32[16,128]{1,0:T(8,128)S(1)} %get-tuple-element.17), channel_id=1, source_target_pairs={{0,4},{1,5},{2,6},{3,7},{4,0},{5,1},{6,2},{7,3},{8,12},{9,13},{10,... | collective-permute-start | bytes 24584 | tf_op jit(solution)/shard_map/ppermute | solution.py:404
  31.0 2.1 %collective-permute-start.3 = (f32[16,128]{1,0:T(8,128)S(1)}, f32[16,128]{1,0:T(8,128)S(1)}, u32[]{:S(2)}, u32[]{:S(2)}) collective-permute-start(f32[16,128]{1,0:T(8,128)S(1)} %get-tuple-element.18), channel_id=1, source_target_pairs={{0,1},{1,0},{2,3},{3,2},{4,8},{5,9},{6,10},{7,11},{8,4},{9,5},{10,... | collective-permute-start | bytes 24584 | tf_op jit(solution)/shard_map/ppermute | solution.py:404
  33.1 2.0 %copy-start = (f32[8,7,128,128]{3,2,1,0:T(8,128)S(1)}, f32[8,7,128,128]{3,2,1,0:T(8,128)}, u32[]{:S(2)}) copy-start(f32[8,7,128,128]{3,2,1,0:T(8,128)} %blocks_ref.7) | copy-start | bytes 11010052
  35.2 9.6 %copy-start.1 = (f32[8,7,128,128]{3,2,1,0:T(8,128)S(1)}, f32[8,7,128,128]{3,2,1,0:T(8,128)}, u32[]{:S(2)}) copy-start(f32[8,7,128,128]{3,2,1,0:T(8,128)} %blocks_ref.7) | copy-start | bytes 11010052
  36.3 6.1 %collective-permute-start.7 = (f32[8,128]{1,0:T(8,128)S(1)}, f32[8,128]{1,0:T(8,128)S(1)}, u32[]{:S(2)}, u32[]{:S(2)}) collective-permute-start(f32[8,128]{1,0:T(8,128)S(1)} %start.1.field_ref.r_ref), channel_id=1, source_target_pairs={{0,1},{1,0},{2,3},{3,2},{4,8},{5,9},{6,10},{7,11},{8,4},{9,5},{10,... | collective-permute-start | bytes 12296 | tf_op jit(solution)/shard_map/ppermute | solution.py:374
  36.3 7.1 %collective-permute-start.6 = (f32[8,128]{1,0:T(8,128)S(1)}, f32[8,128]{1,0:T(8,128)S(1)}, u32[]{:S(2)}, u32[]{:S(2)}) collective-permute-start(f32[8,128]{1,0:T(8,128)S(1)} %start.1.field_ref.r_ref), channel_id=1, source_target_pairs={{0,4},{1,5},{2,6},{3,7},{4,0},{5,1},{6,2},{7,3},{8,12},{9,13},{10,... | collective-permute-start | bytes 12296 | tf_op jit(solution)/shard_map/ppermute | solution.py:374
  41.7 3.0 %collective-permute-start.5 = (f32[8,128]{1,0:T(8,128)S(1)}, f32[8,128]{1,0:T(8,128)S(1)}, u32[]{:S(2)}, u32[]{:S(2)}) collective-permute-start(f32[8,128]{1,0:T(8,128)S(1)} %start.1.field_ref.r_ref), channel_id=1, source_target_pairs={{0,3},{1,2},{2,1},{3,0},{4,7},{5,6},{6,5},{7,4},{8,11},{9,10},{10,... | collective-permute-start | bytes 12296 | tf_op jit(solution)/shard_map/ppermute | solution.py:374
  41.7 3.0 %collective-permute-start.4 = (f32[8,128]{1,0:T(8,128)S(1)}, f32[8,128]{1,0:T(8,128)S(1)}, u32[]{:S(2)}, u32[]{:S(2)}) collective-permute-start(f32[8,128]{1,0:T(8,128)S(1)} %start.1.field_ref.r_ref), channel_id=1, source_target_pairs={{0,1},{1,0},{2,3},{3,2},{4,5},{5,4},{6,7},{7,6},{8,9},{9,8},{10,11... | collective-permute-start | bytes 12296 | tf_op jit(solution)/shard_map/ppermute | solution.py:374
  45.8 3.7 %collective-permute-start.11 = (f32[8,128]{1,0:T(8,128)S(1)}, f32[8,128]{1,0:T(8,128)S(1)}, u32[]{:S(2)}, u32[]{:S(2)}) collective-permute-start(f32[8,128]{1,0:T(8,128)S(1)} %once.1.field_ref.w_ref), channel_id=1, source_target_pairs={{0,1},{1,0},{2,3},{3,2},{4,8},{5,9},{6,10},{7,11},{8,4},{9,5},{10,... | collective-permute-start | bytes 12296 | tf_op jit(solution)/shard_map/ppermute | solution.py:374
  45.9 4.7 %collective-permute-start.10 = (f32[8,128]{1,0:T(8,128)S(1)}, f32[8,128]{1,0:T(8,128)S(1)}, u32[]{:S(2)}, u32[]{:S(2)}) collective-permute-start(f32[8,128]{1,0:T(8,128)S(1)} %once.1.field_ref.w_ref), channel_id=1, source_target_pairs={{0,4},{1,5},{2,6},{3,7},{4,0},{5,1},{6,2},{7,3},{8,12},{9,13},{10,... | collective-permute-start | bytes 12296 | tf_op jit(solution)/shard_map/ppermute | solution.py:374
  48.9 3.0 %collective-permute-start.9 = (f32[8,128]{1,0:T(8,128)S(1)}, f32[8,128]{1,0:T(8,128)S(1)}, u32[]{:S(2)}, u32[]{:S(2)}) collective-permute-start(f32[8,128]{1,0:T(8,128)S(1)} %once.1.field_ref.w_ref), channel_id=1, source_target_pairs={{0,3},{1,2},{2,1},{3,0},{4,7},{5,6},{6,5},{7,4},{8,11},{9,10},{10,... | collective-permute-start | bytes 12296 | tf_op jit(solution)/shard_map/ppermute | solution.py:374
  48.9 3.0 %collective-permute-start.8 = (f32[8,128]{1,0:T(8,128)S(1)}, f32[8,128]{1,0:T(8,128)S(1)}, u32[]{:S(2)}, u32[]{:S(2)}) collective-permute-start(f32[8,128]{1,0:T(8,128)S(1)} %once.1.field_ref.w_ref), channel_id=1, source_target_pairs={{0,1},{1,0},{2,3},{3,2},{4,5},{5,4},{6,7},{7,6},{8,9},{9,8},{10,11... | collective-permute-start | bytes 12296 | tf_op jit(solution)/shard_map/ppermute | solution.py:374
  53.0 16.2 %copy-start.2 = (s32[64,512]{1,0:T(8,128)S(1)}, s32[64,512]{1,0:T(8,128)}, u32[]{:S(2)}) copy-start(s32[64,512]{1,0:T(8,128)} %target_ref.3) | copy-start | bytes 393220
  53.0 3.7 %collective-permute-start.15 = (f32[8,128]{1,0:T(8,128)S(1)}, f32[8,128]{1,0:T(8,128)S(1)}, u32[]{:S(2)}, u32[]{:S(2)}) collective-permute-start(f32[8,128]{1,0:T(8,128)S(1)} %twice.1.field_ref.v_ref), channel_id=1, source_target_pairs={{0,1},{1,0},{2,3},{3,2},{4,8},{5,9},{6,10},{7,11},{8,4},{9,5},{10,... | collective-permute-start | bytes 12296 | tf_op jit(solution)/shard_map/ppermute | solution.py:374
  53.1 4.6 %collective-permute-start.14 = (f32[8,128]{1,0:T(8,128)S(1)}, f32[8,128]{1,0:T(8,128)S(1)}, u32[]{:S(2)}, u32[]{:S(2)}) collective-permute-start(f32[8,128]{1,0:T(8,128)S(1)} %twice.1.field_ref.v_ref), channel_id=1, source_target_pairs={{0,4},{1,5},{2,6},{3,7},{4,0},{5,1},{6,2},{7,3},{8,12},{9,13},{10,... | collective-permute-start | bytes 12296 | tf_op jit(solution)/shard_map/ppermute | solution.py:374
  56.1 3.0 %collective-permute-start.13 = (f32[8,128]{1,0:T(8,128)S(1)}, f32[8,128]{1,0:T(8,128)S(1)}, u32[]{:S(2)}, u32[]{:S(2)}) collective-permute-start(f32[8,128]{1,0:T(8,128)S(1)} %twice.1.field_ref.v_ref), channel_id=1, source_target_pairs={{0,3},{1,2},{2,1},{3,0},{4,7},{5,6},{6,5},{7,4},{8,11},{9,10},{10,... | collective-permute-start | bytes 12296 | tf_op jit(solution)/shard_map/ppermute | solution.py:374
  56.1 3.0 %collective-permute-start.12 = (f32[8,128]{1,0:T(8,128)S(1)}, f32[8,128]{1,0:T(8,128)S(1)}, u32[]{:S(2)}, u32[]{:S(2)}) collective-permute-start(f32[8,128]{1,0:T(8,128)S(1)} %twice.1.field_ref.v_ref), channel_id=1, source_target_pairs={{0,1},{1,0},{2,3},{3,2},{4,5},{5,4},{6,7},{7,6},{8,9},{9,8},{10,11... | collective-permute-start | bytes 12296 | tf_op jit(solution)/shard_map/ppermute | solution.py:374

commit v2 on v1

--- a/solution.py
+++ b/solution.py
@@ -1,4 +1,5 @@
 import functools
+import math
 
 import jax
 import jax.numpy as jnp
@@ -12,6 +13,7 @@
 SIDES = 4
 BOTH = ("gx", "gy")
 F32 = jnp.float32
+BF16 = jnp.bfloat16
 
 
 def partner_of(index, count, odd):
@@ -58,111 +60,148 @@
     ]
 
 
-def slot_keys(owner_ref, slots, rows):
-    row = lax.broadcasted_iota(jnp.int32, (rows, 128), 0)
-    keys = jnp.full((rows, 128), -1, jnp.int32)
-    for k in range(SIDES + 1):
-        owner = owner_ref[0, k]
+def soil_tile(place, water_ref, porosity_ref, conduct_ref, exponent_ref, inflow_ref, soil_ref, recharge_ref):
+    layers = water_ref.shape[0]
+    power = exponent_ref[place]
+    less = power - 1.0
+    inverse = 1.0 / power
+    kappa = jnp.exp2(
+        (jnp.log2(power * conduct_ref[place]) - power * jnp.log2(porosity_ref[place] - RESIDUAL)) / less
+    )
+    back = 1.0 / kappa
+    bend = less * (-0.5 * math.log(2.0))
+    inflow = inflow_ref[place] * (kappa * power)
+
+    def layer(flux, content):
+        turn = jnp.tanh(bend * jnp.log2(content))
+        whole = flux + content
+        kept = whole * (0.5 + 0.5 * turn)
+        return whole - kept, content + (kept - content) * inverse
+
+    pair = 2
+    total = None
+    for first in range(0, SWEEPS, pair):
+        fluxes = [inflow] * pair
+        contents = [None] * layers
+        for diagonal in range(layers + pair - 1):
+            for sweep in reversed(range(pair)):
+                at = diagonal - sweep
+                if not 0 <= at < layers:
+                    continue
+                here = (at,) + place
+                if sweep:
+                    content = contents[at]
+                elif first:
+                    content = soil_ref[here]
+                else:
+                    content = (water_ref[here] - RESIDUAL) * kappa
+                fluxes[sweep], content = layer(fluxes[sweep], content)
+                contents[at] = content
+                if sweep == pair - 1:
+                    last = first + pair == SWEEPS
+                    soil_ref[here] = content * back + RESIDUAL if last else content
+        for flux in fluxes:
+            total = flux if total is None else total + flux
+    recharge_ref[place] = total * (back * inverse)
+
+
+def bin_rows(target_ref, recharge_ref, keys, totals_ref, width):
+    rows, columns = target_ref.shape
+    slots_high = keys.shape[0]
+    shift = width.bit_length() - 1
+    keys = jnp.concatenate([keys] * (columns // 128), axis=1)
+    cell = lax.broadcasted_iota(jnp.int32, (width, columns), 0).astype(F32).astype(BF16)
+    target = target_ref[...]
+    value = recharge_ref[...]
+    cells = (target & (width - 1)).astype(F32)
+    slot = lax.shift_right_logical(target, shift)
+    high = value.astype(BF16).astype(F32)
+    low = value - high
+    one_hot = []
+    spread = []
+    for row in range(rows):
+        line = slice(row, row + 1)
+        wide = jnp.broadcast_to(cells[line], (16, columns)).astype(BF16)
+        wide = jnp.concatenate([wide] * (width // 16), axis=0)
+        one_hot.append(jnp.where(wide == cell, BF16(1), BF16(0)))
+        hit = jnp.broadcast_to(slot[line], (slots_high, columns)) == keys
+        parts = [
+            jnp.where(hit, jnp.broadcast_to(part[line], (slots_high, columns)), 0.0) for part in (high, low)
+        ]
+        spread.append(jnp.concatenate(parts, axis=0).astype(BF16))
+    totals_ref[...] += lax.dot_general(
+        jnp.concatenate(spread, axis=1),
+        jnp.concatenate(one_hot, axis=1),
+        (((1,), (1,)), ((), ())),
+        preferred_element_type=F32,
+    )
+
+
+def soil_kernel(
+    gx_count, gy_count,
+    water_ref, porosity_ref, conduct_ref, exponent_ref, inflow_ref, target_ref, heads_ref,
+    send_hbm, pattern_hbm, blocks_hbm,
+    soil_ref, index_ref, entry_ref, own_ref, *rest,
+):
+    side_refs = rest[:SIDES]
+    blocks_out, recharge_ref, totals_ref, send_ref, pattern_ref, sems = rest[SIDES:]
+    step = pl.program_id(0)
+    steps = pl.num_programs(0)
+    rows, columns = recharge_ref.shape
+    own_blocks, width = heads_ref.shape
+    slots = send_ref.shape[0]
+    hi_rows = entry_ref.shape[1]
+    owners = owners_here(gx_count, gy_count)
+    copies = [
+        pltpu.make_async_copy(send_hbm, send_ref, sems.at[0]),
+        pltpu.make_async_copy(pattern_hbm, pattern_ref, sems.at[1]),
+        pltpu.make_async_copy(blocks_hbm, blocks_out, sems.at[2]),
+    ]
+
+    @pl.when(step == 0)
+    def _():
+        for copy in copies:
+            copy.start()
+        totals_ref[...] = jnp.zeros_like(totals_ref)
+
+    @pl.loop(0, rows // 8)
+    def _(tile):
+        place = (pl.ds(pl.multiple_of(tile * 8, 8), 8), slice(None))
+        soil_tile(
+            place, water_ref, porosity_ref, conduct_ref, exponent_ref, inflow_ref, soil_ref, recharge_ref
+        )
+
+    row = lax.broadcasted_iota(jnp.int32, (hi_rows, 128), 0)
+    keys = jnp.full((hi_rows, 128), -1, jnp.int32)
+    for k, owner in enumerate(owners):
         inside = (row >= k * slots) & (row < (k + 1) * slots) & (owner >= 0)
         keys = jnp.where(inside, owner * slots + row - k * slots, keys)
-    return keys
-
-
-def soil_kernel(
-    own_blocks, slots, width,
-    owner_ref, send_ref, pattern_ref,
-    water_ref, porosity_ref, conduct_ref, exponent_ref, inflow_ref, target_ref, heads_ref,
-    soil_ref, index_ref, own_ref, *rest,
-):
-    side_refs = rest[:SIDES]
-    offset_ref, recharge_ref, totals_ref = rest[SIDES:]
-    step = pl.program_id(0)
-    steps = pl.num_programs(0)
-    layers, rows, columns = water_ref.shape
-    hi_rows = -(-(SIDES + 1) * slots // 8) * 8
-
-    @pl.when(step == 0)
-    def _():
-        totals_ref[...] = jnp.zeros_like(totals_ref)
-
-    exponent = exponent_ref[...]
-    offset_ref[...] = jnp.log2(conduct_ref[...]) - exponent * jnp.log2(porosity_ref[...] - RESIDUAL)
-    recharge_ref[...] = jnp.zeros_like(recharge_ref)
-    soil_ref[...] = water_ref[...] - RESIDUAL
-
-    def layer(flux, content):
-        power = exponent_ref[...]
-        conduct_now = jnp.exp2(power * jnp.log2(content) + offset_ref[...])
-        steep = power * conduct_now
-        share = (flux - conduct_now) * pl.reciprocal(content + steep)
-        return conduct_now + steep * share, content + content * share
-
-    pair = 2
-
-    @pl.loop(0, SWEEPS // pair)
-    def _(_):
-        fluxes = [inflow_ref[...] for _ in range(pair)]
-        for diagonal in range(layers + pair - 1):
-            for sweep in range(pair):
-                at = diagonal - sweep
-                if 0 <= at < layers:
-                    flux, content = layer(fluxes[sweep], soil_ref[at])
-                    fluxes[sweep] = flux
-                    soil_ref[at] = content
-        recharge_ref[...] += fluxes[0] + fluxes[1]
-
-    soil_ref[...] = soil_ref[...] + RESIDUAL
-
-    keys = slot_keys(owner_ref, slots, hi_rows)
-    keys = jnp.concatenate([keys] * (columns // 128), axis=1)
-    cell = lax.broadcasted_iota(jnp.int32, (width, columns), 0)
-
-    @pl.loop(0, rows)
-    def _(row):
-        target = target_ref[pl.ds(row, 1), :]
-        value = recharge_ref[pl.ds(row, 1), :]
-        cells = jnp.broadcast_to(target & (width - 1), (width, columns))
-        one_hot = jnp.where(cells == cell, 1.0, 0.0).astype(jnp.bfloat16)
-        high = value.astype(jnp.bfloat16).astype(F32)
-        low = value - high
-        hit = jnp.broadcast_to(target // width, (hi_rows, columns)) == keys
-        spread = jnp.concatenate(
-            [
-                jnp.where(hit, jnp.broadcast_to(high, (hi_rows, columns)), 0.0),
-                jnp.where(hit, jnp.broadcast_to(low, (hi_rows, columns)), 0.0),
-            ],
-            axis=0,
-        ).astype(jnp.bfloat16)
-        totals_ref[...] += lax.dot_general(
-            one_hot, spread, (((1,), (1,)), ((), ())), preferred_element_type=F32
-        )
+    bin_rows(target_ref, recharge_ref, keys, totals_ref, width)
 
     @pl.when(step == steps - 1)
     def _():
-        totals = totals_ref[...]
-        padded = jnp.concatenate([totals, jnp.zeros((width, 128 - totals.shape[1]), F32)], axis=1)
-        turned = padded.T
-        sums = turned[:hi_rows] + turned[hi_rows : 2 * hi_rows]
+        for copy in copies:
+            copy.wait()
+        sums = totals_ref[0:hi_rows, :] + totals_ref[hi_rows : 2 * hi_rows, :]
         block = lax.broadcasted_iota(jnp.int32, (own_blocks, width), 0)
-        for k in range(SIDES + 1):
-            owner = owner_ref[0, k]
+        for k, owner in enumerate(owners):
+            out_ref = side_refs[k - 1] if k else own_ref
             placed = jnp.zeros((own_blocks, width), F32)
             for slot in range(slots):
-                ident = send_ref[0, jnp.maximum(owner, 0), slot]
+                ident = send_ref[slot, jnp.maximum(owner, 0)]
                 at = k * slots + slot
                 placed = placed + jnp.where(block == ident, sums[at : at + 1], 0.0)
-            if k == 0:
-                own_ref[...] = placed
-            else:
-                side_refs[k - 1][0:own_blocks, :] = placed
-                side_refs[k - 1][own_blocks : 2 * own_blocks, :] = heads_ref[...]
+                entry_ref[0, at] = k * own_blocks + jnp.maximum(ident, 0)
+                entry_ref[1, at] = jnp.where(owner >= 0, owner * slots + slot, -1)
+            out_ref[0:own_blocks, :] = placed
+            out_ref[own_blocks : 2 * own_blocks, :] = heads_ref[...]
         for r in range(own_blocks):
             for k in range(pattern_ref.shape[1]):
                 ident = pattern_ref[r, k]
                 owner = ident // own_blocks
                 place = (SIDES + 1) * own_blocks
                 for side in range(SIDES + 1):
-                    fits = (owner == owner_ref[0, side]) & (ident >= 0)
+                    fits = (owner == owners[side]) & (ident >= 0)
                     place = jnp.where(fits, side * own_blocks + ident % own_blocks, place)
                 index_ref[r, k] = place
 
@@ -194,14 +233,15 @@
     table_ref[(SIDES + 1) * own_blocks :, :] = jnp.zeros((own_blocks, own.shape[1]), F32)
 
 
-def start_kernel(area, index_ref, blocks_ref, own_ref, heads_ref, *rest):
+def start_kernel(area, index_ref, blocks_ref, own_ref, *rest):
     side_refs, (residual_ref, table_ref) = rest[:SIDES], rest[SIDES:]
-    own_blocks = heads_ref.shape[0]
-    fill_table(table_ref, heads_ref[...], [s[own_blocks:, :] for s in side_refs], own_blocks)
-    cells = own_ref[...]
+    own_blocks = residual_ref.shape[0]
+    heads = own_ref[own_blocks:, :]
+    fill_table(table_ref, heads, [s[own_blocks:, :] for s in side_refs], own_blocks)
+    cells = own_ref[:own_blocks, :]
     for side in side_refs:
         cells = cells + side[:own_blocks, :]
-    residual_ref[...] = heads_ref[...] + area * cells - operate(index_ref, blocks_ref, table_ref)
+    residual_ref[...] = heads + area * cells - operate(index_ref, blocks_ref, table_ref)
 
 
 def apply_kernel(index_ref, blocks_ref, field_ref, *rest):
@@ -293,53 +333,44 @@
     return (y0 - y1) * inverse + y2, (y1 * inverse - 2.0 * y2) * inverse, y2 * inverse * inverse
 
 
-def heads_kernel(slots, owner_ref, send_ref, all_ref, target_ref, heads_ref, r_ref, w_ref, v_ref, *rest):
+def heads_kernel(slots, entry_ref, all_ref, target_ref, own_ref, r_ref, w_ref, v_ref, *rest):
     sides = rest[: 4 * SIDES]
-    heads_out, columns_out, table_ref, slot_ref, keys_ref = rest[4 * SIDES :]
-    own_blocks, width = heads_ref.shape
-    hi_rows = keys_ref.shape[0]
+    heads_out, columns_out, table_ref, slot_ref = rest[4 * SIDES :]
+    own_blocks, width = r_ref.shape
+    shift = width.bit_length() - 1
     weight_r, weight_w, weight_v = solve_step(all_ref[:, 0, :])
 
-    def new_heads(heads, r, w, v):
-        return heads + weight_r * r + weight_w * w + weight_v * v
-
-    mine = new_heads(heads_ref[...], r_ref[...], w_ref[...], v_ref[...])
+    def new_heads(old, r, w, v):
+        return old[own_blocks:, :] + weight_r * r[...] + weight_w * w[...] + weight_v * v[...]
+
+    mine = new_heads(own_ref, r_ref, w_ref, v_ref)
     heads_out[...] = mine
     table_ref[0:own_blocks, :] = mine
     for k in range(SIDES):
-        old, r, w, v = sides[4 * k : 4 * k + 4]
-        table_ref[(k + 1) * own_blocks : (k + 2) * own_blocks, :] = new_heads(
-            old[own_blocks:, :], r[...], w[...], v[...]
-        )
-    for k in range(SIDES + 1):
-        owner = jnp.maximum(owner_ref[0, k], 0)
-        for slot in range(slots):
-            ident = jnp.maximum(send_ref[0, owner, slot], 0)
-            slot_ref[k * slots + slot : k * slots + slot + 1, :] = table_ref[
-                pl.ds(k * own_blocks + ident, 1), :
-            ]
-    keys_ref[...] = slot_keys(owner_ref, slots, hi_rows)
+        table_ref[(k + 1) * own_blocks : (k + 2) * own_blocks, :] = new_heads(*sides[4 * k : 4 * k + 4])
+    entries = (SIDES + 1) * slots
+    for entry in range(entries):
+        slot_ref[entry] = jnp.broadcast_to(table_ref[pl.ds(entry_ref[0, entry], 1), :], (8, width))
     rows, columns = target_ref.shape
-    entries = (SIDES + 1) * slots
 
     @pl.loop(0, rows // 8)
     def _(step):
         at = pl.multiple_of(step * 8, 8)
         for part in range(columns // 128):
-            target = target_ref[pl.ds(at, 8), part * 128 : (part + 1) * 128]
+            here = (pl.ds(at, 8), slice(part * 128, (part + 1) * 128))
+            target = target_ref[here]
             lanes = target & (width - 1)
-            key = target // width
+            key = lax.shift_right_logical(target, shift)
             found = jnp.zeros((8, 128), F32)
             for entry in range(entries):
-                table = jnp.broadcast_to(slot_ref[entry : entry + 1, :], (8, 128))
-                values = jnp.take_along_axis(table, lanes, axis=1, mode="promise_in_bounds")
-                wanted = jnp.broadcast_to(keys_ref[entry : entry + 1, :], (8, 128))
-                found = jnp.where(key == wanted, values, found)
-            columns_out[pl.ds(at, 8), part * 128 : (part + 1) * 128] = found
+                values = jnp.take_along_axis(slot_ref[entry], lanes, axis=1, mode="promise_in_bounds")
+                found = jnp.where(key == entry_ref[1, entry], values, found)
+            columns_out[here] = found
 
 
 VMEM = pl.BlockSpec(memory_space=pltpu.VMEM)
 SMEM = pl.BlockSpec(memory_space=pltpu.SMEM)
+ANY = pl.BlockSpec(memory_space=pl.ANY)
 
 
 def body(
@@ -363,8 +394,6 @@
     hi_rows = -(-(SIDES + 1) * slots // 8) * 8
     area = own_blocks * width / (rows * columns)
     perms = swaps(gx_count, gy_count)
-    owners = jnp.stack(owners_here(gx_count, gy_count)).astype(jnp.int32).reshape(1, SIDES + 1)
-    blocks = pltpu.with_memory_space_constraint(aquifer_blocks, pltpu.VMEM)
     in_hbm = lambda array: pltpu.with_memory_space_constraint(array, pltpu.HBM)
     field = jax.ShapeDtypeStruct((own_blocks, width), F32)
     two = jax.ShapeDtypeStruct((2 * own_blocks, width), F32)
@@ -378,30 +407,38 @@
     deep = pl.BlockSpec((layers, chunk, columns), lambda i: (0, i, 0))
     whole = lambda shape: pl.BlockSpec(shape, lambda i: (0,) * len(shape))
     outs = pl.pallas_call(
-        functools.partial(soil_kernel, own_blocks, slots, width),
+        functools.partial(soil_kernel, gx_count, gy_count),
         grid=(rows // chunk,),
-        in_specs=[SMEM, SMEM, SMEM, deep, flat, flat, flat, flat, flat, whole((own_blocks, width))],
-        out_specs=[deep, SMEM, whole((own_blocks, width))] + [whole((2 * own_blocks, width))] * SIDES,
+        in_specs=[deep, flat, flat, flat, flat, flat, whole((own_blocks, width)), ANY, ANY, ANY],
+        out_specs=[deep, SMEM, SMEM] + [whole((2 * own_blocks, width))] * (SIDES + 1) + [ANY],
         out_shape=[
             jax.ShapeDtypeStruct(water_content.shape, F32),
             jax.ShapeDtypeStruct((own_blocks, most), jnp.int32),
-            field,
+            jax.ShapeDtypeStruct((2, hi_rows), jnp.int32),
         ]
-        + [two] * SIDES,
+        + [two] * (SIDES + 1)
+        + [pltpu.VMEM(aquifer_blocks.shape, F32)],
         scratch_shapes=[
             pltpu.VMEM((chunk, columns), F32),
-            pltpu.VMEM((chunk, columns), F32),
-            pltpu.VMEM((width, 2 * hi_rows), F32),
+            pltpu.VMEM((2 * hi_rows, width), F32),
+            pltpu.SMEM((slots, devices), jnp.int32),
+            pltpu.SMEM(block_pattern.shape, jnp.int32),
+            pltpu.SemaphoreType.DMA((3,)),
         ],
         compiler_params=pltpu.CompilerParams(vmem_limit_bytes=24 * 2**20),
         name="soil",
     )(
-        owners, send_blocks, block_pattern,
-        *map(in_hbm, (water_content, porosity, conduct, exponent, infiltration, column_target)),
-        prior_heads,
+        *map(
+            in_hbm,
+            (
+                water_content, porosity, conduct, exponent, infiltration, column_target, prior_heads,
+                send_blocks[0].T, block_pattern, aquifer_blocks,
+            ),
+        )
     )
-    soil_water, index, own = outs[:3]
-    got = [lax.ppermute(out, BOTH, perm) for out, perm in zip(outs[3:], perms)]
+    soil_water, index, entries, own = outs[:4]
+    blocks = pltpu.with_memory_space_constraint(outs[-1], pltpu.VMEM)
+    got = [lax.ppermute(out, BOTH, perm) for out, perm in zip(outs[4:], perms)]
 
     def small(kernel, args, shape, name):
         return pl.pallas_call(
@@ -414,7 +451,7 @@
             name=name,
         )(*args)
 
-    r = small(functools.partial(start_kernel, area), (index, blocks, own, prior_heads, *got), field, "start")
+    r = small(functools.partial(start_kernel, area), (index, blocks, own, *got), field, "start")
     r_sides = trade(r)
     w = small(apply_kernel, (index, blocks, r, *r_sides), field, "once")
     w_sides = trade(w)
@@ -429,17 +466,16 @@
         sides += [got[k], r_sides[k], w_sides[k], v_sides[k]]
     heads, column_heads = pl.pallas_call(
         functools.partial(heads_kernel, slots),
-        in_specs=[SMEM, SMEM] + [VMEM] * (6 + 4 * SIDES),
+        in_specs=[SMEM] + [VMEM] * (6 + 4 * SIDES),
         out_specs=[VMEM, VMEM],
         out_shape=[field, jax.ShapeDtypeStruct((rows, columns), F32)],
         scratch_shapes=[
             pltpu.VMEM(((SIDES + 1) * own_blocks, width), F32),
-            pltpu.VMEM((hi_rows, width), F32),
-            pltpu.VMEM((hi_rows, width), jnp.int32),
+            pltpu.VMEM((hi_rows, 8, width), F32),
         ],
         compiler_params=pltpu.CompilerParams(vmem_limit_bytes=16 * 2**20),
         name="heads",
-    )(owners, send_blocks, all_sums, column_target, prior_heads, r, w, v, *sides)
+    )(entries, all_sums, column_target, own, r, w, v, *sides)
     return soil_water, heads, column_heads
 
 

time: 72.5 us -> 57.5 us (0.79)
  Pallas kernels: 31 us -> 20.3 us
  local copies, waits for them, and re-layouts: 4.27 us -> 0.01 us
    pallas_call x2, Pallas kernels: 26.5 us -> 15.9 us  [the longest x1 13.1 us: body(): pl.pallas_call(functools.partial(soil_kernel, gx_count, gy_count), grid=(...]
    unnamed x11 -> x2, local copies, waits for them, and re-layouts: 4.18 us -> 0.01 us
where the time goes in v2:
time: 57.5 us; the launch traced here: 57.3 us
  Pallas kernels  20.3 us (35%)
  starting transfers between devices  18.2 us (32%)
  waiting for transfers between devices  9.27 us (16%)
  blocking collectives  8.84 us (15%)
  between operations  0.68 us (1%)
    ppermute x12, starting transfers between devices, trade(): return [lax.ppermute(array, BOTH, perm) for perm in perms]  13.6 us
    pallas_call x1, Pallas kernels, body(): pl.pallas_call(functools.partial(soil_kernel, gx_count, gy_count), grid=(...  13.1 us
    all_to_all x1, blocking collectives, body(): all_sums = lax.all_to_all(sums, BOTH, 0, 0)  8.84 us
    ppermute x12, waiting for transfers between devices, trade(): return [lax.ppermute(array, BOTH, perm) for perm in perms]  7.15 us
    ppermute x4, starting transfers between devices, body(): got = [lax.ppermute(out, BOTH, perm) for out, perm in zip(outs[4:], perms)]  4.66 us
    pallas_call x4, Pallas kernels, small(): pl.pallas_call(kernel, in_specs=[SMEM] + [VMEM] * (len(args) - 1), out_sp...  4.41 us
    pallas_call x1, Pallas kernels, body(): pl.pallas_call(functools.partial(heads_kernel, slots), in_specs=[SMEM] +...  2.77 us
    ppermute x4, waiting for transfers between devices, body(): got = [lax.ppermute(out, BOTH, perm) for out, perm in zip(outs[4:], perms)]  2.12 us
  transfers between devices with their start and end apart: 16, of which 7 were waited for; matrix products, arithmetic and copies ran while one was open for 0% of the time, Pallas kernels for 0%

profile of v2, /device:TPU:0, one launch (start us, length us, event | category | flops | bytes accessed | tf_op | source)
XLA Modules:
  0.0 57.3 jit_solution(9708589810685215699)
XLA Ops:
  0.6 13.1 %soil.1 = (f32[16,64,512]{2,1,0:T(8,128)}, s32[8,7]{1,0:T(8,128)S(1)}, s32[2,24]{1,0:T(2,128)S(1)}, f32[16,128]{1,0:T(8,128)S(1)}, f32[16,128]{1,0:T(8,128)S(1)}...) custom-call(f32[16,64,512]{2,1,0:T(8,128)} %water_ref.1, ...), custom_call_target="tpu_custom_call" | custom-call | tf_op jit(solution)/shard_map/soil/pallas_call | solution.py:409
  13.8 0.5 collective-permute-start
  14.3 2.6 %collective-permute-start.1 = (f32[16,128]{1,0:T(8,128)S(1)}, f32[16,128]{1,0:T(8,128)S(1)}, u32[]{:S(2)}, u32[]{:S(2)}) collective-permute-start(f32[16,128]{1,0:T(8,128)S(1)} %get-tuple-element.20), channel_id=1, source_target_pairs={{0,3},{1,2},{2,1},{3,0},{4,7},{5,6},{6,5},{7,4},{8,11},{9,10},{10,... | collective-permute-start | bytes 24584 | tf_op jit(solution)/shard_map/ppermute | solution.py:441
  16.9 1.5 %collective-permute-start.2 = (f32[16,128]{1,0:T(8,128)S(1)}, f32[16,128]{1,0:T(8,128)S(1)}, u32[]{:S(2)}, u32[]{:S(2)}) collective-permute-start(f32[16,128]{1,0:T(8,128)S(1)} %get-tuple-element.21), channel_id=1, source_target_pairs={{0,4},{1,5},{2,6},{3,7},{4,0},{5,1},{6,2},{7,3},{8,12},{9,13},{10,... | collective-permute-start | bytes 24584 | tf_op jit(solution)/shard_map/ppermute | solution.py:441
  18.4 0.0 collective-permute-start.3
  18.4 0.0 collective-permute-done.rest_0_
  18.4 0.0 collective-permute-done.1.rest_1_.rest_4_
  18.4 2.1 %collective-permute-done.2.rest_2_.rest_8_ = f32[16,128]{1,0:T(8,128)S(1)} collective-permute-done((f32[16,128]{1,0:T(8,128)S(1)}, f32[16,128]{1,0:T(8,128)S(1)}, u32[]{:S(2)}, u32[]{:S(2)}) %collective-permute-start.2) | collective-permute-done | bytes 8224 | tf_op jit(solution)/shard_map/ppermute | solution.py:441
  20.6 0.0 collective-permute-done.3.rest_3_.rest_12_
  20.6 1.1 %start.1.field_ref.r_ref = f32[8,128]{1,0:T(8,128)S(1)} custom-call(s32[8,7]{1,0:T(8,128)S(1)} %get-tuple-element.16.index_ref, f32[8,7,128,128]{3,2,1,0:T(8,128)S(1)} %get-tuple-element.17.blocks_ref, f32[16,128]{1,0:T(8,128)S(1)} %get-tuple-element.18.own_ref, f32[16,128]{1,0:T(8,128)S(1)} %collective-permute-done.rest_0_, ...), custom_call_target="tpu_custom_call" | custom-call | tf_op jit(solution)/shard_map/start/pallas_call | solution.py:444
  21.6 0.0 collective-permute-start.7
  21.6 5.5 %collective-permute-start.6 = (f32[8,128]{1,0:T(8,128)S(1)}, f32[8,128]{1,0:T(8,128)S(1)}, u32[]{:S(2)}, u32[]{:S(2)}) collective-permute-start(f32[8,128]{1,0:T(8,128)S(1)} %start.1.field_ref.r_ref), channel_id=1, source_target_pairs={{0,4},{1,5},{2,6},{3,7},{4,0},{5,1},{6,2},{7,3},{8,12},{9,13},{10,... | collective-permute-start | bytes 12296 | tf_op jit(solution)/shard_map/ppermute | solution.py:403
  27.1 0.0 collective-permute-start.5
  27.1 0.6 %collective-permute-start.4 = (f32[8,128]{1,0:T(8,128)S(1)}, f32[8,128]{1,0:T(8,128)S(1)}, u32[]{:S(2)}, u32[]{:S(2)}) collective-permute-start(f32[8,128]{1,0:T(8,128)S(1)} %start.1.field_ref.r_ref), channel_id=1, source_target_pairs={{0,1},{1,0},{2,3},{3,2},{4,5},{5,4},{6,7},{7,6},{8,9},{9,8},{10,11... | collective-permute-start | bytes 12296 | tf_op jit(solution)/shard_map/ppermute | solution.py:403
  27.8 0.0 collective-permute-done.7.rest_3_.rest_13_
  27.8 0.9 %collective-permute-done.6.rest_2_.rest_9_ = f32[8,128]{1,0:T(8,128)S(1)} collective-permute-done((f32[8,128]{1,0:T(8,128)S(1)}, f32[8,128]{1,0:T(8,128)S(1)}, u32[]{:S(2)}, u32[]{:S(2)}) %collective-permute-start.6) | collective-permute-done | bytes 4128 | tf_op jit(solution)/shard_map/ppermute | solution.py:403
  28.7 1.4 %collective-permute-done.5.rest_1_.rest_5_ = f32[8,128]{1,0:T(8,128)S(1)} collective-permute-done((f32[8,128]{1,0:T(8,128)S(1)}, f32[8,128]{1,0:T(8,128)S(1)}, u32[]{:S(2)}, u32[]{:S(2)}) %collective-permute-start.5) | collective-permute-done | bytes 4128 | tf_op jit(solution)/shard_map/ppermute | solution.py:403
  30.2 0.0 collective-permute-done.4.rest_0_.rest_1_
  30.2 1.1 %once.1.field_ref.w_ref = f32[8,128]{1,0:T(8,128)S(1)} custom-call(s32[8,7]{1,0:T(8,128)S(1)} %get-tuple-element.16.index_ref, f32[8,7,128,128]{3,2,1,0:T(8,128)S(1)} %get-tuple-element.17.blocks_ref, f32[8,128]{1,0:T(8,128)S(1)} %start.1.field_ref.r_ref, f32[8,128]{1,0:T(8,128)S(1)} %collective-permute-done.4.rest_0_.rest_1_, ...), custom_call_target="tpu_custom_call" | custom-call | tf_op jit(solution)/shard_map/once/pallas_call | solution.py:444
  31.2 0.0 copy-start
  31.2 0.0 collective-permute-start.11
  31.3 3.0 %collective-permute-start.10 = (f32[8,128]{1,0:T(8,128)S(1)}, f32[8,128]{1,0:T(8,128)S(1)}, u32[]{:S(2)}, u32[]{:S(2)}) collective-permute-start(f32[8,128]{1,0:T(8,128)S(1)} %once.1.field_ref.w_ref), channel_id=1, source_target_pairs={{0,4},{1,5},{2,6},{3,7},{4,0},{5,1},{6,2},{7,3},{8,12},{9,13},{10,... | collective-permute-start | bytes 12296 | tf_op jit(solution)/shard_map/ppermute | solution.py:403
  34.3 0.0 collective-permute-start.9
  34.3 0.6 %collective-permute-start.8 = (f32[8,128]{1,0:T(8,128)S(1)}, f32[8,128]{1,0:T(8,128)S(1)}, u32[]{:S(2)}, u32[]{:S(2)}) collective-permute-start(f32[8,128]{1,0:T(8,128)S(1)} %once.1.field_ref.w_ref), channel_id=1, source_target_pairs={{0,1},{1,0},{2,3},{3,2},{4,5},{5,4},{6,7},{7,6},{8,9},{9,8},{10,11... | collective-permute-start | bytes 12296 | tf_op jit(solution)/shard_map/ppermute | solution.py:403
  35.0 0.0 collective-permute-done.11.rest_3_.rest_14_
  35.0 0.9 %collective-permute-done.10.rest_2_.rest_10_ = f32[8,128]{1,0:T(8,128)S(1)} collective-permute-done((f32[8,128]{1,0:T(8,128)S(1)}, f32[8,128]{1,0:T(8,128)S(1)}, u32[]{:S(2)}, u32[]{:S(2)}) %collective-permute-start.10) | collective-permute-done | bytes 4128 | tf_op jit(solution)/shard_map/ppermute | solution.py:403
  35.9 1.4 %collective-permute-done.9.rest_1_.rest_6_ = f32[8,128]{1,0:T(8,128)S(1)} collective-permute-done((f32[8,128]{1,0:T(8,128)S(1)}, f32[8,128]{1,0:T(8,128)S(1)}, u32[]{:S(2)}, u32[]{:S(2)}) %collective-permute-start.9) | collective-permute-done | bytes 4128 | tf_op jit(solution)/shard_map/ppermute | solution.py:403
  37.3 0.0 collective-permute-done.8.rest_0_.rest_2_
  37.3 1.1 %twice.1.field_ref.v_ref = f32[8,128]{1,0:T(8,128)S(1)} custom-call(s32[8,7]{1,0:T(8,128)S(1)} %get-tuple-element.16.index_ref, f32[8,7,128,128]{3,2,1,0:T(8,128)S(1)} %get-tuple-element.17.blocks_ref, f32[8,128]{1,0:T(8,128)S(1)} %once.1.field_ref.w_ref, f32[8,128]{1,0:T(8,128)S(1)} %collective-permute-done.8.rest_0_.rest_2_, ...), custom_call_target="tpu_custom_call" | custom-call | tf_op jit(solution)/shard_map/twice/pallas_call | solution.py:444
  38.4 0.0 collective-permute-start.15
  38.4 3.1 %collective-permute-start.14 = (f32[8,128]{1,0:T(8,128)S(1)}, f32[8,128]{1,0:T(8,128)S(1)}, u32[]{:S(2)}, u32[]{:S(2)}) collective-permute-start(f32[8,128]{1,0:T(8,128)S(1)} %twice.1.field_ref.v_ref), channel_id=1, source_target_pairs={{0,4},{1,5},{2,6},{3,7},{4,0},{5,1},{6,2},{7,3},{8,12},{9,13},{10,... | collective-permute-start | bytes 12296 | tf_op jit(solution)/shard_map/ppermute | solution.py:403
  41.5 0.0 collective-permute-start.13
  41.5 0.6 %collective-permute-start.12 = (f32[8,128]{1,0:T(8,128)S(1)}, f32[8,128]{1,0:T(8,128)S(1)}, u32[]{:S(2)}, u32[]{:S(2)}) collective-permute-start(f32[8,128]{1,0:T(8,128)S(1)} %twice.1.field_ref.v_ref), channel_id=1, source_target_pairs={{0,1},{1,0},{2,3},{3,2},{4,5},{5,4},{6,7},{7,6},{8,9},{9,8},{10,11... | collective-permute-start | bytes 12296 | tf_op jit(solution)/shard_map/ppermute | solution.py:403
  42.1 0.0 collective-permute-done.15.rest_3_.rest_15_
  42.1 0.9 %collective-permute-done.14.rest_2_.rest_11_ = f32[8,128]{1,0:T(8,128)S(1)} collective-permute-done((f32[8,128]{1,0:T(8,128)S(1)}, f32[8,128]{1,0:T(8,128)S(1)}, u32[]{:S(2)}, u32[]{:S(2)}) %collective-permute-start.14) | collective-permute-done | bytes 4128 | tf_op jit(solution)/shard_map/ppermute | solution.py:403
  43.1 1.4 %collective-permute-done.13.rest_1_.rest_7_ = f32[8,128]{1,0:T(8,128)S(1)} collective-permute-done((f32[8,128]{1,0:T(8,128)S(1)}, f32[8,128]{1,0:T(8,128)S(1)}, u32[]{:S(2)}, u32[]{:S(2)}) %collective-permute-start.13) | collective-permute-done | bytes 4128 | tf_op jit(solution)/shard_map/ppermute | solution.py:403
  44.5 0.0 collective-permute-done.12.rest_0_.rest_3_
  44.5 1.2 %sums.1 = f32[32,1,128]{2,1,0:T(1,128)S(1)} custom-call(s32[8,7]{1,0:T(8,128)S(1)} %get-tuple-element.16.index_ref, f32[8,7,128,128]{3,2,1,0:T(8,128)S(1)} %get-tuple-element.17.blocks_ref, f32[8,128]{1,0:T(8,128)S(1)} %start.1.field_ref.r_ref, f32[8,128]{1,0:T(8,128)S(1)} %once.1.field_ref.w_ref, f32[8,128]{1,0:T(8,128)S(1)} %twice.1.field_ref.v_ref, ...), custom_call_target="tpu_custom_call" | custom-call | tf_op jit(solution)/shard_map/sums/pallas_call | solution.py:444
  45.7 8.8 %all_to_all.5.all_ref = f32[32,1,128]{2,1,0:T(1,128)S(1)} all-to-all(f32[32,1,128]{2,1,0:T(1,128)S(1)} %sums.1), channel_id=1, replica_groups=mesh['gx'=8,'gy'=4] {'gx','gy'}, dimensions={0} | all-to-all | bytes 32768 | tf_op jit(solution)/shard_map/all_to_all | solution.py:463
  54.6 0.0 copy-done
  54.6 2.8 %heads.1 = (f32[8,128]{1,0:T(8,128)}, f32[64,512]{1,0:T(8,128)}) custom-call(s32[2,24]{1,0:T(2,128)S(1)} %get-tuple-element.15.entry_ref, f32[32,1,128]{2,1,0:T(1,128)S(1)} %all_to_all.5.all_ref, s32[64,512]{1,0:T(8,128)S(1)} %copy-done, f32[16,128]{1,0:T(8,128)S(1)} %get-tuple-element.18.own_ref, f32[8,128]{1,0:T(8,128)S(1)} %start.1.field_ref.r_ref, ...), custom_call_target="tpu_custom_call" | custom-call | tf_op jit(solution)/shard_map/heads/pallas_call | solution.py:467
Async XLA Ops:
  13.8 4.7 %collective-permute-start = (f32[16,128]{1,0:T(8,128)S(1)}, f32[16,128]{1,0:T(8,128)S(1)}, u32[]{:S(2)}, u32[]{:S(2)}) collective-permute-start(f32[16,128]{1,0:T(8,128)S(1)} %get-tuple-element.19), channel_id=1, source_target_pairs={{0,1},{1,0},{2,3},{3,2},{4,5},{5,4},{6,7},{7,6},{8,9},{9,8},{10,11... | collective-permute-start | bytes 24584 | tf_op jit(solution)/shard_map/ppermute | solution.py:441
  14.3 4.1 %collective-permute-start.1 = (f32[16,128]{1,0:T(8,128)S(1)}, f32[16,128]{1,0:T(8,128)S(1)}, u32[]{:S(2)}, u32[]{:S(2)}) collective-permute-start(f32[16,128]{1,0:T(8,128)S(1)} %get-tuple-element.20), channel_id=1, source_target_pairs={{0,3},{1,2},{2,1},{3,0},{4,7},{5,6},{6,5},{7,4},{8,11},{9,10},{10,... | collective-permute-start | bytes 24584 | tf_op jit(solution)/shard_map/ppermute | solution.py:441
  16.9 3.7 %collective-permute-start.2 = (f32[16,128]{1,0:T(8,128)S(1)}, f32[16,128]{1,0:T(8,128)S(1)}, u32[]{:S(2)}, u32[]{:S(2)}) collective-permute-start(f32[16,128]{1,0:T(8,128)S(1)} %get-tuple-element.21), channel_id=1, source_target_pairs={{0,4},{1,5},{2,6},{3,7},{4,0},{5,1},{6,2},{7,3},{8,12},{9,13},{10,... | collective-permute-start | bytes 24584 | tf_op jit(solution)/shard_map/ppermute | solution.py:441
  18.4 2.1 %collective-permute-start.3 = (f32[16,128]{1,0:T(8,128)S(1)}, f32[16,128]{1,0:T(8,128)S(1)}, u32[]{:S(2)}, u32[]{:S(2)}) collective-permute-start(f32[16,128]{1,0:T(8,128)S(1)} %get-tuple-element.22), channel_id=1, source_target_pairs={{0,1},{1,0},{2,3},{3,2},{4,8},{5,9},{6,10},{7,11},{8,4},{9,5},{10,... | collective-permute-start | bytes 24584 | tf_op jit(solution)/shard_map/ppermute | solution.py:441
  21.6 6.1 %collective-permute-start.7 = (f32[8,128]{1,0:T(8,128)S(1)}, f32[8,128]{1,0:T(8,128)S(1)}, u32[]{:S(2)}, u32[]{:S(2)}) collective-permute-start(f32[8,128]{1,0:T(8,128)S(1)} %start.1.field_ref.r_ref), channel_id=1, source_target_pairs={{0,1},{1,0},{2,3},{3,2},{4,8},{5,9},{6,10},{7,11},{8,4},{9,5},{10,... | collective-permute-start | bytes 12296 | tf_op jit(solution)/shard_map/ppermute | solution.py:403
  21.6 7.1 %collective-permute-start.6 = (f32[8,128]{1,0:T(8,128)S(1)}, f32[8,128]{1,0:T(8,128)S(1)}, u32[]{:S(2)}, u32[]{:S(2)}) collective-permute-start(f32[8,128]{1,0:T(8,128)S(1)} %start.1.field_ref.r_ref), channel_id=1, source_target_pairs={{0,4},{1,5},{2,6},{3,7},{4,0},{5,1},{6,2},{7,3},{8,12},{9,13},{10,... | collective-permute-start | bytes 12296 | tf_op jit(solution)/shard_map/ppermute | solution.py:403
  27.1 3.0 %collective-permute-start.5 = (f32[8,128]{1,0:T(8,128)S(1)}, f32[8,128]{1,0:T(8,128)S(1)}, u32[]{:S(2)}, u32[]{:S(2)}) collective-permute-start(f32[8,128]{1,0:T(8,128)S(1)} %start.1.field_ref.r_ref), channel_id=1, source_target_pairs={{0,3},{1,2},{2,1},{3,0},{4,7},{5,6},{6,5},{7,4},{8,11},{9,10},{10,... | collective-permute-start | bytes 12296 | tf_op jit(solution)/shard_map/ppermute | solution.py:403
  27.1 3.0 %collective-permute-start.4 = (f32[8,128]{1,0:T(8,128)S(1)}, f32[8,128]{1,0:T(8,128)S(1)}, u32[]{:S(2)}, u32[]{:S(2)}) collective-permute-start(f32[8,128]{1,0:T(8,128)S(1)} %start.1.field_ref.r_ref), channel_id=1, source_target_pairs={{0,1},{1,0},{2,3},{3,2},{4,5},{5,4},{6,7},{7,6},{8,9},{9,8},{10,11... | collective-permute-start | bytes 12296 | tf_op jit(solution)/shard_map/ppermute | solution.py:403
  31.2 23.3 %copy-start = (s32[64,512]{1,0:T(8,128)S(1)}, s32[64,512]{1,0:T(8,128)}, u32[]{:S(2)}) copy-start(s32[64,512]{1,0:T(8,128)} %target_ref.3) | copy-start | bytes 393220
  31.2 3.7 %collective-permute-start.11 = (f32[8,128]{1,0:T(8,128)S(1)}, f32[8,128]{1,0:T(8,128)S(1)}, u32[]{:S(2)}, u32[]{:S(2)}) collective-permute-start(f32[8,128]{1,0:T(8,128)S(1)} %once.1.field_ref.w_ref), channel_id=1, source_target_pairs={{0,1},{1,0},{2,3},{3,2},{4,8},{5,9},{6,10},{7,11},{8,4},{9,5},{10,... | collective-permute-start | bytes 12296 | tf_op jit(solution)/shard_map/ppermute | solution.py:403
  31.3 4.6 %collective-permute-start.10 = (f32[8,128]{1,0:T(8,128)S(1)}, f32[8,128]{1,0:T(8,128)S(1)}, u32[]{:S(2)}, u32[]{:S(2)}) collective-permute-start(f32[8,128]{1,0:T(8,128)S(1)} %once.1.field_ref.w_ref), channel_id=1, source_target_pairs={{0,4},{1,5},{2,6},{3,7},{4,0},{5,1},{6,2},{7,3},{8,12},{9,13},{10,... | collective-permute-start | bytes 12296 | tf_op jit(solution)/shard_map/ppermute | solution.py:403
  34.3 3.0 %collective-permute-start.9 = (f32[8,128]{1,0:T(8,128)S(1)}, f32[8,128]{1,0:T(8,128)S(1)}, u32[]{:S(2)}, u32[]{:S(2)}) collective-permute-start(f32[8,128]{1,0:T(8,128)S(1)} %once.1.field_ref.w_ref), channel_id=1, source_target_pairs={{0,3},{1,2},{2,1},{3,0},{4,7},{5,6},{6,5},{7,4},{8,11},{9,10},{10,... | collective-permute-start | bytes 12296 | tf_op jit(solution)/shard_map/ppermute | solution.py:403
  34.3 3.0 %collective-permute-start.8 = (f32[8,128]{1,0:T(8,128)S(1)}, f32[8,128]{1,0:T(8,128)S(1)}, u32[]{:S(2)}, u32[]{:S(2)}) collective-permute-start(f32[8,128]{1,0:T(8,128)S(1)} %once.1.field_ref.w_ref), channel_id=1, source_target_pairs={{0,1},{1,0},{2,3},{3,2},{4,5},{5,4},{6,7},{7,6},{8,9},{9,8},{10,11... | collective-permute-start | bytes 12296 | tf_op jit(solution)/shard_map/ppermute | solution.py:403
  38.4 3.7 %collective-permute-start.15 = (f32[8,128]{1,0:T(8,128)S(1)}, f32[8,128]{1,0:T(8,128)S(1)}, u32[]{:S(2)}, u32[]{:S(2)}) collective-permute-start(f32[8,128]{1,0:T(8,128)S(1)} %twice.1.field_ref.v_ref), channel_id=1, source_target_pairs={{0,1},{1,0},{2,3},{3,2},{4,8},{5,9},{6,10},{7,11},{8,4},{9,5},{10,... | collective-permute-start | bytes 12296 | tf_op jit(solution)/shard_map/ppermute | solution.py:403
  38.4 4.6 %collective-permute-start.14 = (f32[8,128]{1,0:T(8,128)S(1)}, f32[8,128]{1,0:T(8,128)S(1)}, u32[]{:S(2)}, u32[]{:S(2)}) collective-permute-start(f32[8,128]{1,0:T(8,128)S(1)} %twice.1.field_ref.v_ref), channel_id=1, source_target_pairs={{0,4},{1,5},{2,6},{3,7},{4,0},{5,1},{6,2},{7,3},{8,12},{9,13},{10,... | collective-permute-start | bytes 12296 | tf_op jit(solution)/shard_map/ppermute | solution.py:403
  41.5 3.0 %collective-permute-start.13 = (f32[8,128]{1,0:T(8,128)S(1)}, f32[8,128]{1,0:T(8,128)S(1)}, u32[]{:S(2)}, u32[]{:S(2)}) collective-permute-start(f32[8,128]{1,0:T(8,128)S(1)} %twice.1.field_ref.v_ref), channel_id=1, source_target_pairs={{0,3},{1,2},{2,1},{3,0},{4,7},{5,6},{6,5},{7,4},{8,11},{9,10},{10,... | collective-permute-start | bytes 12296 | tf_op jit(solution)/shard_map/ppermute | solution.py:403
  41.5 3.0 %collective-permute-start.12 = (f32[8,128]{1,0:T(8,128)S(1)}, f32[8,128]{1,0:T(8,128)S(1)}, u32[]{:S(2)}, u32[]{:S(2)}) collective-permute-start(f32[8,128]{1,0:T(8,128)S(1)} %twice.1.field_ref.v_ref), channel_id=1, source_target_pairs={{0,1},{1,0},{2,3},{3,2},{4,5},{5,4},{6,7},{7,6},{8,9},{9,8},{10,11... | collective-permute-start | bytes 12296 | tf_op jit(solution)/shard_map/ppermute | solution.py:403

commit v3 on v2

v3 whole, which is shorter than its diff:
```python
import functools
import math

import jax
import jax.numpy as jnp
from jax import lax
from jax.experimental import pallas as pl
from jax.experimental.pallas import tpu as pltpu
from jax.sharding import PartitionSpec as P

SWEEPS = 8
RESIDUAL = 0.05
SIDES = 4
BOTH = ("gx", "gy")
ORDER = ((0, 1), (1, 1), (0, 0), (1, 0))
F32 = jnp.float32
BF16 = jnp.bfloat16


def partner_of(index, count, odd):
    other = ((index - odd) ^ 1) + odd
    return other, 0 <= index - odd and 0 <= other < count


def swaps(gx_count, gy_count):
    perms = []
    for axis, odd in ORDER:
        perm = []
        for x in range(gx_count):
            for y in range(gy_count):
                if axis == 1:
                    other, fits = partner_of(y, gy_count, odd)
                    across = gy_count - 1 - y if gy_count % 2 == 0 else y
                    target = (x, other if fits else across)
                else:
                    other, fits = partner_of(x, gx_count, odd)
                    beside = y ^ 1 if gy_count % 2 == 0 and gx_count % 2 == 0 else y
                    target = (other, y) if fits else (x, beside)
                perm.append((x * gy_count + y, target[0] * gy_count + target[1]))
        perms.append(perm)
    return perms


def owners_here(gx_count, gy_count):
    x = lax.axis_index("gx")
    y = lax.axis_index("gy")

    def neighbour(index, count, odd, make):
        other = ((index - odd) ^ 1) + odd
        fits = (index >= odd) & (other < count)
        return jnp.where(fits, make(other), -1)

    along = lambda other: x * gy_count + other
    across = lambda other: other * gy_count + y
    found = [x * gy_count + y]
    for axis, odd in ORDER:
        found.append(neighbour(y, gy_count, odd, along) if axis else neighbour(x, gx_count, odd, across))
    return found


def soil_tile(place, water_ref, porosity_ref, conduct_ref, exponent_ref, inflow_ref, recharge_ref):
    layers = water_ref.shape[0]
    power = exponent_ref[place]
    less = power - 1.0
    inverse = 1.0 / power
    kappa = jnp.exp2(
        (jnp.log2(power * conduct_ref[place]) - power * jnp.log2(porosity_ref[place] - RESIDUAL)) / less
    )
    back = 1.0 / kappa
    bend = less * (0.5 * math.log(2.0))
    inflow = inflow_ref[place] * (kappa * power)

    def layer(flux, content):
        turn = jnp.tanh(bend * jnp.log2(content))
        below = (flux + content) * (0.5 + 0.5 * turn)
        return below, content + (flux - below) * inverse

    pair = 2
    total = None
    for first in range(0, SWEEPS, pair):
        fluxes = [inflow] * pair
        contents = [None] * layers
        for diagonal in range(layers + pair - 1):
            for sweep in reversed(range(pair)):
                at = diagonal - sweep
                if not 0 <= at < layers:
                    continue
                here = (at,) + place
                if sweep:
                    content = contents[at]
                elif first:
                    content = water_ref[here]
                else:
                    content = (water_ref[here] - RESIDUAL) * kappa
                fluxes[sweep], content = layer(fluxes[sweep], content)
                contents[at] = content
                if sweep == pair - 1:
                    last = first + pair == SWEEPS
                    water_ref[here] = content * back + RESIDUAL if last else content
        for flux in fluxes:
            total = flux if total is None else total + flux
    recharge_ref[place] = total * (back * inverse)


def bin_rows(target, value, keys, totals_ref, width):
    rows, columns = target.shape
    slots_high = keys.shape[0]
    shift = width.bit_length() - 1
    keys = jnp.concatenate([keys] * (columns // 128), axis=1)
    cell = lax.broadcasted_iota(jnp.int32, (width, columns), 0).astype(F32).astype(BF16)
    cells = (target & (width - 1)).astype(F32)
    slot = lax.shift_right_logical(target, shift)
    high = value.astype(BF16).astype(F32)
    low = value - high
    one_hot = []
    spread = []
    for row in range(rows):
        line = slice(row, row + 1)
        wide = jnp.broadcast_to(cells[line], (16, columns)).astype(BF16)
        wide = jnp.concatenate([wide] * (width // 16), axis=0)
        one_hot.append(jnp.where(wide == cell, BF16(1), BF16(0)))
        hit = jnp.broadcast_to(slot[line], (slots_high, columns)) == keys
        parts = [
            jnp.where(hit, jnp.broadcast_to(part[line], (slots_high, columns)), 0.0) for part in (high, low)
        ]
        spread.append(jnp.concatenate(parts, axis=0).astype(BF16))
    totals_ref[...] += lax.dot_general(
        jnp.concatenate(spread, axis=1),
        jnp.concatenate(one_hot, axis=1),
        (((1,), (1,)), ((), ())),
        preferred_element_type=F32,
    )


def prepare(gx_count, gy_count, send, pattern, own_blocks, source_ref, block_ref, key_ref):
    hi_rows, width = key_ref.shape
    slots, devices = send.shape
    owners = owners_here(gx_count, gy_count)
    row = lax.broadcasted_iota(jnp.int32, (hi_rows, width), 0)
    keys = jnp.full((hi_rows, width), -1, jnp.int32)
    for k, owner in enumerate(owners):
        inside = (row >= k * slots) & (row < (k + 1) * slots) & (owner >= 0)
        keys = jnp.where(inside, owner * slots + row - k * slots, keys)
    key_ref[...] = keys
    lane = lax.broadcasted_iota(jnp.int32, (slots, devices), 1)
    block_ref[...] = jnp.full(block_ref.shape, -1, jnp.int32)
    for k, owner in enumerate(owners):
        idents = jnp.sum(jnp.where(lane == owner, send, 0), axis=1, keepdims=True)
        block_ref[k, 0:slots, :] = jnp.broadcast_to(idents, (slots, width))
    shift = own_blocks.bit_length() - 1
    most = pattern.shape[1]
    for k in range(most):
        ident = jnp.broadcast_to(pattern[:, k : k + 1], (own_blocks, width))
        side = jnp.full((own_blocks, width), -1, jnp.int32)
        for at, owner in enumerate(owners):
            side = jnp.where((lax.shift_right_arithmetic(ident, shift) == owner) & (ident >= 0), at, side)
        source_ref[k] = side
        source_ref[most + k] = ident & (own_blocks - 1)


def soil_kernel(
    gx_count, gy_count,
    water_hbm, porosity_hbm, conduct_hbm, exponent_hbm, inflow_hbm, target_hbm, heads_hbm,
    send_hbm, pattern_hbm, blocks_hbm,
    soil_hbm, source_ref, block_ref, key_ref, own_ref, *rest,
):
    side_refs = rest[:SIDES]
    (
        blocks_out, water_ref, porosity_ref, conduct_ref, exponent_ref, inflow_ref, target_ref,
        heads_ref, send_ref, pattern_ref, recharge_ref, totals_ref, small_sems, in_sems, out_sems, blocks_sem,
    ) = rest[SIDES:]
    rows, columns = recharge_ref.shape
    own_blocks, width = heads_ref.shape
    slots = send_ref.shape[0]
    hi_rows = key_ref.shape[0]
    chunks = in_sems.shape[0]
    chunk = rows // chunks
    flats = (
        (porosity_hbm, porosity_ref), (conduct_hbm, conduct_ref), (exponent_hbm, exponent_ref),
        (inflow_hbm, inflow_ref), (target_hbm, target_ref),
    )

    def small_copies():
        pairs = ((send_hbm, send_ref), (pattern_hbm, pattern_ref), (heads_hbm, heads_ref))
        return [pltpu.make_async_copy(a, b, small_sems.at[at]) for at, (a, b) in enumerate(pairs)]

    def incoming(at):
        here = (pl.ds(pl.multiple_of(at * chunk, 8), chunk), slice(None))
        deep = (slice(None),) + here
        copies = [pltpu.make_async_copy(a.at[here], b.at[here], in_sems.at[at, f]) for f, (a, b) in enumerate(flats)]
        return copies + [pltpu.make_async_copy(water_hbm.at[deep], water_ref.at[deep], in_sems.at[at, len(flats)])]

    def outgoing(at):
        deep = (slice(None), pl.ds(pl.multiple_of(at * chunk, 8), chunk), slice(None))
        return pltpu.make_async_copy(water_ref.at[deep], soil_hbm.at[deep], out_sems.at[at])

    blocks_copy = pltpu.make_async_copy(blocks_hbm, blocks_out, blocks_sem)
    for copy in small_copies() + incoming(0) + incoming(1):
        copy.start()
    totals_ref[...] = jnp.zeros_like(totals_ref)
    for copy in small_copies():
        copy.wait()
    prepare(
        gx_count, gy_count, send_ref[...], pattern_ref[...], own_blocks, source_ref, block_ref, key_ref
    )

    @pl.loop(0, chunks)
    def _(at):
        for copy in incoming(at):
            copy.wait()

        @pl.when(at + 2 < chunks)
        def _():
            for copy in incoming(at + 2):
                copy.start()

        @pl.when(at == chunks - 2)
        def _():
            blocks_copy.start()

        @pl.loop(0, chunk // 8)
        def _(tile):
            place = (pl.ds(pl.multiple_of(at * chunk + tile * 8, 8), 8), slice(None))
            soil_tile(place, water_ref, porosity_ref, conduct_ref, exponent_ref, inflow_ref, recharge_ref)

        outgoing(at).start()
        here = (pl.ds(pl.multiple_of(at * chunk, 8), chunk), slice(None))
        bin_rows(target_ref[here], recharge_ref[here], key_ref[...], totals_ref, width)

    sums = totals_ref[0:hi_rows, :] + totals_ref[hi_rows : 2 * hi_rows, :]
    block = lax.broadcasted_iota(jnp.int32, (own_blocks, width), 0)
    for k in range(SIDES + 1):
        out_ref = side_refs[k - 1] if k else own_ref
        idents = block_ref[k]
        placed = jnp.zeros((own_blocks, width), F32)
        for slot in range(slots):
            at = k * slots + slot
            placed = placed + jnp.where(block == idents[slot : slot + 1], sums[at : at + 1], 0.0)
        out_ref[0:own_blocks, :] = placed
        out_ref[own_blocks : 2 * own_blocks, :] = heads_ref[...]
    blocks_copy.wait()

    @pl.loop(0, chunks)
    def _(at):
        outgoing(at).wait()


def operate(source_ref, blocks_ref, fields):
    own_blocks, most, width = blocks_ref.shape[:3]
    nearby = []
    for k in range(most):
        side, line = source_ref[k], source_ref[most + k]
        rows = jnp.zeros((own_blocks, width), F32)
        for at, field in enumerate(fields):
            picked = jnp.take_along_axis(field, line, axis=0, mode="promise_in_bounds")
            rows = jnp.where(side == at, picked, rows)
        nearby.append(rows)
    image = jnp.zeros((own_blocks, width), F32)
    row = lax.broadcasted_iota(jnp.int32, (own_blocks, 3 * width), 0)
    for r in range(own_blocks):
        total = blocks_ref[r, 0] * nearby[0][r : r + 1]
        for k in range(1, most):
            total = total + blocks_ref[r, k] * nearby[k][r : r + 1]
        first = total.astype(BF16)
        rest = total - first.astype(F32)
        second = rest.astype(BF16)
        third = (rest - second.astype(F32)).astype(BF16)
        parts = jnp.concatenate([first, second, third], axis=1)
        ones = jnp.where(row == r, 1.0, 0.0).astype(BF16)
        image = image + lax.dot_general(
            ones, parts, (((1,), (1,)), ((), ())), preferred_element_type=F32
        )
    return image


def start_kernel(area, source_ref, blocks_ref, own_ref, *rest):
    side_refs, residual_ref = rest[:SIDES][::-1], rest[SIDES]
    own_blocks = residual_ref.shape[0]
    heads = own_ref[own_blocks:, :]
    cells = own_ref[:own_blocks, :]
    for side in side_refs:
        cells = cells + side[:own_blocks, :]
    fields = [heads] + [s[own_blocks:, :] for s in side_refs]
    residual_ref[...] = heads + area * cells - operate(source_ref, blocks_ref, fields)


def apply_kernel(source_ref, blocks_ref, *rest):
    image_ref = rest[-1]
    fields = [f[...] for f in (rest[0],) + rest[-2:0:-1]]
    image_ref[...] = operate(source_ref, blocks_ref, fields)


def whole_sum(values):
    return jnp.sum(jnp.sum(values, axis=0, keepdims=True), axis=1, keepdims=True)


def last_kernel(source_ref, blocks_ref, r_ref, w_ref, *rest):
    fields, sums_ref = [f[...] for f in (rest[0],) + rest[-2:0:-1]], rest[-1]
    z = operate(source_ref, blocks_ref, fields)
    r, w, v = r_ref[...], w_ref[...], fields[0]
    rr = whole_sum(r * r)
    ratio = whole_sum(w * w) / rr
    shift = jnp.where((ratio > 0.0) & (ratio < 1e30), jnp.sqrt(ratio), 1.0)
    inverse = 1.0 / shift
    w1 = w * inverse - r
    v1 = (v * inverse - w) * inverse
    z1 = ((z * inverse - v) * inverse) * inverse
    v2 = v1 - w1
    z2 = z1 - v1
    z3 = z2 - v2
    sums = [
        rr, shift,
        whole_sum(r * w1), whole_sum(w1 * w1), whole_sum(r * v2), whole_sum(w1 * v2), whole_sum(v2 * v2),
        whole_sum(r * z3), whole_sum(w1 * z3), whole_sum(v2 * z3),
    ]
    lane = lax.broadcasted_iota(jnp.int32, (1, 128), 1)
    packed = jnp.zeros((1, 128), F32)
    for position, value in enumerate(sums):
        packed = jnp.where(lane == position, value, packed)
    sums_ref[...] = jnp.broadcast_to(packed[None], sums_ref.shape)


def solve_step(all_sums):
    lane = lax.broadcasted_iota(jnp.int32, all_sums.shape, 1)

    def take(position):
        return jnp.sum(jnp.where(lane == position, all_sums, 0.0), axis=1, keepdims=True)

    rr, shift, rw, ww, rv, wv, vv, rz, wz, vz = [take(p) for p in range(10)]

    def over(values):
        return jnp.sum(values, axis=0, keepdims=True)

    m0 = over(rr)
    theta = over(shift * (rw + rr)) / m0
    ratio = shift / theta
    e = ratio - 1.0
    p2 = ratio * ratio
    p3 = p2 * ratio
    p4 = p2 * p2
    rw, ww, rv = rw * ratio, ww * p2, rv * p2
    wv, rz = wv * p3, rz * p3
    vv, wz = vv * p4, wz * p4
    vz = vz * (p4 * ratio)
    e2 = e * e
    twice = 2.0 * e
    new_w_r = rw + e * rr
    new_w_w = ww + e * rw
    new_v_r = rv + twice * rw + e2 * rr
    new_v_w = wv + twice * ww + e2 * rw
    new_v_v = vv + twice * wv + e2 * rv
    m1 = over(new_w_r)
    m2 = over(new_w_w + e * new_w_r)
    m3 = over(wv + e * rv + twice * new_w_w + e2 * new_w_r)
    m4 = over(new_v_v + twice * new_v_w + e2 * new_v_r)
    m5 = over(vz + twice * wz + e2 * rz + 3.0 * e * new_v_v + 3.0 * e2 * new_v_w + e * e2 * new_v_r)
    a00, a01, a02 = m0 + m1, m1 + m2, m2 + m3
    a11, a12, a22 = m2 + m3, m3 + m4, m4 + m5
    f1 = a01 / a00
    f2 = a02 / a00
    b11 = a11 - f1 * a01
    b12 = a12 - f1 * a02
    b22 = a22 - f2 * a02
    g1 = m1 - f1 * m0
    g2 = m2 - f2 * m0
    f3 = b12 / b11
    y2 = (g2 - f3 * g1) / (b22 - f3 * b12)
    y1 = (g1 - b12 * y2) / b11
    y0 = (m0 - a01 * y1 - a02 * y2) / a00
    inverse = 1.0 / theta
    y2 = y2 * inverse
    return (y0 - y1) * inverse + y2, (y1 * inverse - 2.0 * y2) * inverse, y2 * inverse * inverse


def heads_kernel(slots, block_ref, key_ref, all_ref, target_ref, own_ref, r_ref, w_ref, v_ref, *rest):
    sides = rest[: 4 * SIDES]
    heads_hbm, columns_hbm, slot_ref, heads_ref, columns_ref, sems = rest[4 * SIDES :]
    own_blocks, width = r_ref.shape
    shift = width.bit_length() - 1
    weight_r, weight_w, weight_v = solve_step(all_ref[:, 0, :])

    def new_heads(old, r, w, v):
        return old[own_blocks:, :] + weight_r * r[...] + weight_w * w[...] + weight_v * v[...]

    heads_copy = pltpu.make_async_copy(heads_ref, heads_hbm, sems.at[0])
    for k in range(SIDES + 1):
        four = sides[4 * k - 4 : 4 * k] if k else (own_ref, r_ref, w_ref, v_ref)
        heads = new_heads(*four)
        if k == 0:
            heads_ref[...] = heads
            heads_copy.start()
        lines = jnp.maximum(block_ref[k], 0)
        picked = jnp.take_along_axis(heads, lines, axis=0, mode="promise_in_bounds")
        for slot in range(slots):
            slot_ref[k * slots + slot] = jnp.broadcast_to(picked[slot : slot + 1], (8, width))
    entries = (SIDES + 1) * slots
    rows, columns = target_ref.shape
    copies = []
    for at in range(0, rows, 8):
        for part in range(0, columns, 128):
            here = (slice(at, at + 8), slice(part, part + 128))
            target = target_ref[here]
            lanes = target & (width - 1)
            key = lax.shift_right_logical(target, shift)
            found = jnp.zeros((8, 128), F32)
            for entry in range(entries):
                values = jnp.take_along_axis(slot_ref[entry], lanes, axis=1, mode="promise_in_bounds")
                wanted = jnp.broadcast_to(key_ref[entry : entry + 1, :], (8, 128))
                found = jnp.where(key == wanted, values, found)
            columns_ref[here] = found
        if (at + 8) % 16 == 0:
            here = (slice(at - 8, at + 8), slice(None))
            copies.append(
                pltpu.make_async_copy(columns_ref.at[here], columns_hbm.at[here], sems.at[1 + len(copies)])
            )
            copies[-1].start()
    heads_copy.wait()
    for copy in copies:
        copy.wait()


VMEM = pl.BlockSpec(memory_space=pltpu.VMEM)
ANY = pl.BlockSpec(memory_space=pl.ANY)


def body(
    water_content,
    porosity,
    conduct,
    exponent,
    infiltration,
    column_target,
    send_blocks,
    prior_heads,
    block_pattern,
    aquifer_blocks,
    gx_count,
    gy_count,
):
    devices, slots = send_blocks.shape[1:]
    own_blocks, width = prior_heads.shape
    layers, rows, columns = water_content.shape
    most = block_pattern.shape[1]
    hi_rows = -(-(SIDES + 1) * slots // 8) * 8
    area = own_blocks * width / (rows * columns)
    perms = swaps(gx_count, gy_count)
    in_hbm = lambda array: pltpu.with_memory_space_constraint(array, pltpu.HBM)
    field = jax.ShapeDtypeStruct((own_blocks, width), F32)
    two = jax.ShapeDtypeStruct((2 * own_blocks, width), F32)

    def trade(array):
        return [lax.ppermute(array, BOTH, perm) for perm in perms]

    chunks = rows // 16
    outs = pl.pallas_call(
        functools.partial(soil_kernel, gx_count, gy_count),
        in_specs=[ANY] * 10,
        out_specs=[ANY] + [VMEM] * (SIDES + 4) + [ANY],
        out_shape=[
            jax.ShapeDtypeStruct(water_content.shape, F32),
            jax.ShapeDtypeStruct((2 * most, own_blocks, width), jnp.int32),
            jax.ShapeDtypeStruct((SIDES + 1, own_blocks, width), jnp.int32),
            jax.ShapeDtypeStruct((hi_rows, width), jnp.int32),
        ]
        + [two] * (SIDES + 1)
        + [pltpu.VMEM(aquifer_blocks.shape, F32)],
        scratch_shapes=[
            pltpu.VMEM(water_content.shape, F32),
            *[pltpu.VMEM((rows, columns), F32)] * 4,
            pltpu.VMEM((rows, columns), jnp.int32),
            pltpu.VMEM((own_blocks, width), F32),
            pltpu.VMEM((slots, devices), jnp.int32),
            pltpu.VMEM((own_blocks, most), jnp.int32),
            pltpu.VMEM((rows, columns), F32),
            pltpu.VMEM((2 * hi_rows, width), F32),
            pltpu.SemaphoreType.DMA((3,)),
            pltpu.SemaphoreType.DMA((chunks, 6)),
            pltpu.SemaphoreType.DMA((chunks,)),
            pltpu.SemaphoreType.DMA,
        ],
        compiler_params=pltpu.CompilerParams(vmem_limit_bytes=24 * 2**20),
        name="soil",
    )(
        *map(
            in_hbm,
            (
                water_content, porosity, conduct, exponent, infiltration, column_target, prior_heads,
                send_blocks[0].T, block_pattern, aquifer_blocks,
            ),
        )
    )
    soil_water, source, block, key, own = outs[:5]
    blocks = pltpu.with_memory_space_constraint(outs[-1], pltpu.VMEM)
    got = [lax.ppermute(out, BOTH, perm) for out, perm in zip(outs[5:], perms)]

    def small(kernel, args, shape, name):
        return pl.pallas_call(
            kernel,
            in_specs=[VMEM] * (2 + len(args)),
            out_specs=VMEM,
            out_shape=shape,
            compiler_params=pltpu.CompilerParams(vmem_limit_bytes=16 * 2**20),
            name=name,
        )(source, blocks, *args)

    r = small(functools.partial(start_kernel, area), (own, *got[::-1]), field, "start")
    r_sides = trade(r)
    w = small(apply_kernel, (r, *r_sides[::-1]), field, "once")
    w_sides = trade(w)
    v = small(apply_kernel, (w, *w_sides[::-1]), field, "twice")
    v_sides = trade(v)
    sums = small(last_kernel, (r, w, v, *v_sides[::-1]), jax.ShapeDtypeStruct((devices, 1, width), F32), "sums")
    all_sums = lax.all_to_all(sums, BOTH, 0, 0)
    sides = []
    for k in range(SIDES):
        sides += [got[k], r_sides[k], w_sides[k], v_sides[k]]
    heads, column_heads = pl.pallas_call(
        functools.partial(heads_kernel, slots),
        in_specs=[VMEM] * (8 + 4 * SIDES),
        out_specs=[ANY, ANY],
        out_shape=[field, jax.ShapeDtypeStruct((rows, columns), F32)],
        scratch_shapes=[
            pltpu.VMEM((hi_rows, 8, width), F32),
            pltpu.VMEM((own_blocks, width), F32),
            pltpu.VMEM((rows, columns), F32),
            pltpu.SemaphoreType.DMA((1 + rows // 16,)),
        ],
        compiler_params=pltpu.CompilerParams(vmem_limit_bytes=16 * 2**20),
        name="heads",
    )(block, key, all_sums, column_target, own, r, w, v, *sides)
    return soil_water, heads, column_heads


def solution(mesh):
    placed = (
        P(None, "gx", "gy"),
        P("gx", "gy"),
        P("gx", "gy"),
        P("gx", "gy"),
        P("gx", "gy"),
        P("gx", "gy"),
        P(("gx", "gy"), None, None),
        P(("gx", "gy"), None),
        P(("gx", "gy"), None),
        P(("gx", "gy"), None, None, None),
    )
    return jax.shard_map(
        functools.partial(body, gx_count=mesh.shape["gx"], gy_count=mesh.shape["gy"]),
        mesh=mesh,
        in_specs=placed,
        out_specs=(P(None, "gx", "gy"), P(("gx", "gy"), None), P("gx", "gy")),
        check_vma=False,
    )
```

time: 57.5 us -> 51.8 us (0.901)
  Pallas kernels: 20.3 us -> 15.4 us
  waiting for transfers between devices: 9.27 us -> 5.32 us
  blocking collectives: 8.84 us -> 11.4 us
  starting transfers between devices: 18.2 us -> 18.8 us
    pallas_call x6, Pallas kernels: 20.3 us -> 15.4 us  [the longest x1 11.7 us: body(): pl.pallas_call(functools.partial(soil_kernel, gx_count, gy_count), in_spe...]
    ppermute x12, waiting for transfers between devices: 7.15 us -> 3.85 us  [trade(): return [lax.ppermute(array, BOTH, perm) for perm in perms]]
    all_to_all x1, blocking collectives: 8.84 us -> 11.4 us  [body(): all_sums = lax.all_to_all(sums, BOTH, 0, 0)]
    ppermute x4, waiting for transfers between devices: 2.12 us -> 1.47 us  [body(): got = [lax.ppermute(out, BOTH, perm) for out, perm in zip(outs[5:], perms)]]
  transfers between devices with their start and end apart: 16 -> 16, of which waited for: 7 -> 4; matrix products, arithmetic and copies ran while one was open for 0% -> 0% of each run, Pallas kernels for 0% -> 0%
where the time goes in v3:
time: 51.8 us; the launch traced here: 51.6 us
  starting transfers between devices  18.8 us (36%)
  Pallas kernels  15.4 us (30%)
  blocking collectives  11.4 us (22%)
  waiting for transfers between devices  5.32 us (10%)
  between operations  0.69 us (1%)
    ppermute x12, starting transfers between devices, trade(): return [lax.ppermute(array, BOTH, perm) for perm in perms]  14.1 us
    pallas_call x1, Pallas kernels, body(): pl.pallas_call(functools.partial(soil_kernel, gx_count, gy_count), in_spe...  11.7 us
    all_to_all x1, blocking collectives, body(): all_sums = lax.all_to_all(sums, BOTH, 0, 0)  11.4 us
    ppermute x4, starting transfers between devices, body(): got = [lax.ppermute(out, BOTH, perm) for out, perm in zip(outs[5:], perms)]  4.72 us
    ppermute x12, waiting for transfers between devices, trade(): return [lax.ppermute(array, BOTH, perm) for perm in perms]  3.85 us
    pallas_call x4, Pallas kernels, small(): pl.pallas_call(kernel, in_specs=[VMEM] * (2 + len(args)), out_specs=VMEM,...  2.04 us
    pallas_call x1, Pallas kernels, body(): pl.pallas_call(functools.partial(heads_kernel, slots), in_specs=[VMEM] *...  1.7 us
    ppermute x4, waiting for transfers between devices, body(): got = [lax.ppermute(out, BOTH, perm) for out, perm in zip(outs[5:], perms)]  1.47 us
  transfers between devices with their start and end apart: 16, of which 4 were waited for; matrix products, arithmetic and copies ran while one was open for 0% of the time, Pallas kernels for 0%

profile of v3, /device:TPU:0, one launch (start us, length us, event | category | flops | bytes accessed | tf_op | source)
XLA Modules:
  0.0 51.6 jit_solution(9287674085881933339)
XLA Ops:
  0.6 11.7 %soil.1 = (f32[16,64,512]{2,1,0:T(8,128)}, s32[14,8,128]{2,1,0:T(8,128)S(1)}, s32[5,8,128]{2,1,0:T(8,128)S(1)}, s32[24,128]{1,0:T(8,128)S(1)}, f32[16,128]{1,0:T...) custom-call(f32[16,64,512]{2,1,0:T(8,128)} %water_hbm.1, ...), custom_call_target="tpu_custom_call" | custom-call | tf_op jit(solution)/shard_map/soil/pallas_call | solution.py:455
  12.4 0.5 %collective-permute-start = (f32[16,128]{1,0:T(8,128)S(1)}, f32[16,128]{1,0:T(8,128)S(1)}, u32[]{:S(2)}, u32[]{:S(2)}) collective-permute-start(f32[16,128]{1,0:T(8,128)S(1)} %get-tuple-element.21), channel_id=1, source_target_pairs={{0,1},{1,0},{2,3},{3,2},{4,5},{5,4},{6,7},{7,6},{8,9},{9,8},{10,11... | collective-permute-start | bytes 24584 | tf_op jit(solution)/shard_map/ppermute | solution.py:494
  12.9 2.6 %collective-permute-start.1 = (f32[16,128]{1,0:T(8,128)S(1)}, f32[16,128]{1,0:T(8,128)S(1)}, u32[]{:S(2)}, u32[]{:S(2)}) collective-permute-start(f32[16,128]{1,0:T(8,128)S(1)} %get-tuple-element.22), channel_id=1, source_target_pairs={{0,4},{1,5},{2,6},{3,7},{4,0},{5,1},{6,2},{7,3},{8,12},{9,13},{10,... | collective-permute-start | bytes 24584 | tf_op jit(solution)/shard_map/ppermute | solution.py:494
  15.5 1.3 %collective-permute-start.2 = (f32[16,128]{1,0:T(8,128)S(1)}, f32[16,128]{1,0:T(8,128)S(1)}, u32[]{:S(2)}, u32[]{:S(2)}) collective-permute-start(f32[16,128]{1,0:T(8,128)S(1)} %get-tuple-element.23), channel_id=1, source_target_pairs={{0,3},{1,2},{2,1},{3,0},{4,7},{5,6},{6,5},{7,4},{8,11},{9,10},{10,... | collective-permute-start | bytes 24584 | tf_op jit(solution)/shard_map/ppermute | solution.py:494
  16.7 0.3 collective-permute-start.3
  17.1 0.0 collective-permute-done.rest_0_.rest_12_
  17.1 0.0 collective-permute-done.1.rest_1_.rest_8_
  17.1 1.4 %collective-permute-done.2.rest_2_.rest_4_ = f32[16,128]{1,0:T(8,128)S(1)} collective-permute-done((f32[16,128]{1,0:T(8,128)S(1)}, f32[16,128]{1,0:T(8,128)S(1)}, u32[]{:S(2)}, u32[]{:S(2)}) %collective-permute-start.2) | collective-permute-done | bytes 8224 | tf_op jit(solution)/shard_map/ppermute | solution.py:494
  18.5 0.0 collective-permute-done.3.rest_3_.rest_0_
  18.5 0.5 start.1.rest_0_.r_ref
  19.0 0.2 collective-permute-start.7
  19.2 1.4 %collective-permute-start.6 = (f32[8,128]{1,0:T(8,128)S(1)}, f32[8,128]{1,0:T(8,128)S(1)}, u32[]{:S(2)}, u32[]{:S(2)}) collective-permute-start(f32[8,128]{1,0:T(8,128)S(1)} %start.1.rest_0_.r_ref), channel_id=1, source_target_pairs={{0,3},{1,2},{2,1},{3,0},{4,7},{5,6},{6,5},{7,4},{8,11},{9,10},{10,... | collective-permute-start | bytes 12296 | tf_op jit(solution)/shard_map/ppermute | solution.py:452
  20.7 4.2 %collective-permute-start.5 = (f32[8,128]{1,0:T(8,128)S(1)}, f32[8,128]{1,0:T(8,128)S(1)}, u32[]{:S(2)}, u32[]{:S(2)}) collective-permute-start(f32[8,128]{1,0:T(8,128)S(1)} %start.1.rest_0_.r_ref), channel_id=1, source_target_pairs={{0,4},{1,5},{2,6},{3,7},{4,0},{5,1},{6,2},{7,3},{8,12},{9,13},{10,... | collective-permute-start | bytes 12296 | tf_op jit(solution)/shard_map/ppermute | solution.py:452
  24.8 0.4 collective-permute-start.4
  25.2 0.0 collective-permute-done.7.rest_4_.rest_1_
  25.2 0.0 collective-permute-done.6.rest_3_.rest_5_
  25.2 1.2 %collective-permute-done.5.rest_2_.rest_9_ = f32[8,128]{1,0:T(8,128)S(1)} collective-permute-done((f32[8,128]{1,0:T(8,128)S(1)}, f32[8,128]{1,0:T(8,128)S(1)}, u32[]{:S(2)}, u32[]{:S(2)}) %collective-permute-start.5) | collective-permute-done | bytes 4128 | tf_op jit(solution)/shard_map/ppermute | solution.py:452
  26.4 0.0 collective-permute-done.4.rest_1_.rest_13_
  26.4 0.5 once.1.rest_0_.w_ref
  26.9 0.0 copy-start
  26.9 0.0 collective-permute-start.11
  26.9 1.2 %collective-permute-start.10 = (f32[8,128]{1,0:T(8,128)S(1)}, f32[8,128]{1,0:T(8,128)S(1)}, u32[]{:S(2)}, u32[]{:S(2)}) collective-permute-start(f32[8,128]{1,0:T(8,128)S(1)} %once.1.rest_0_.w_ref), channel_id=1, source_target_pairs={{0,3},{1,2},{2,1},{3,0},{4,7},{5,6},{6,5},{7,4},{8,11},{9,10},{10,... | collective-permute-start | bytes 12296 | tf_op jit(solution)/shard_map/ppermute | solution.py:452
  28.1 2.6 %collective-permute-start.9 = (f32[8,128]{1,0:T(8,128)S(1)}, f32[8,128]{1,0:T(8,128)S(1)}, u32[]{:S(2)}, u32[]{:S(2)}) collective-permute-start(f32[8,128]{1,0:T(8,128)S(1)} %once.1.rest_0_.w_ref), channel_id=1, source_target_pairs={{0,4},{1,5},{2,6},{3,7},{4,0},{5,1},{6,2},{7,3},{8,12},{9,13},{10,... | collective-permute-start | bytes 12296 | tf_op jit(solution)/shard_map/ppermute | solution.py:452
  30.7 0.2 collective-permute-start.8
  30.9 0.0 collective-permute-done.11.rest_4_.rest_2_
  30.9 0.0 collective-permute-done.10.rest_3_.rest_6_
  30.9 1.4 %collective-permute-done.9.rest_2_.rest_10_ = f32[8,128]{1,0:T(8,128)S(1)} collective-permute-done((f32[8,128]{1,0:T(8,128)S(1)}, f32[8,128]{1,0:T(8,128)S(1)}, u32[]{:S(2)}, u32[]{:S(2)}) %collective-permute-start.9) | collective-permute-done | bytes 4128 | tf_op jit(solution)/shard_map/ppermute | solution.py:452
  32.3 0.0 collective-permute-done.8.rest_1_.rest_14_
  32.3 0.5 twice.1.rest_0_.v_ref
  32.8 0.0 collective-permute-start.15
  32.8 0.7 %collective-permute-start.14 = (f32[8,128]{1,0:T(8,128)S(1)}, f32[8,128]{1,0:T(8,128)S(1)}, u32[]{:S(2)}, u32[]{:S(2)}) collective-permute-start(f32[8,128]{1,0:T(8,128)S(1)} %twice.1.rest_0_.v_ref), channel_id=1, source_target_pairs={{0,3},{1,2},{2,1},{3,0},{4,7},{5,6},{6,5},{7,4},{8,11},{9,10},{10,... | collective-permute-start | bytes 12296 | tf_op jit(solution)/shard_map/ppermute | solution.py:452
  33.5 2.8 %collective-permute-start.13 = (f32[8,128]{1,0:T(8,128)S(1)}, f32[8,128]{1,0:T(8,128)S(1)}, u32[]{:S(2)}, u32[]{:S(2)}) collective-permute-start(f32[8,128]{1,0:T(8,128)S(1)} %twice.1.rest_0_.v_ref), channel_id=1, source_target_pairs={{0,4},{1,5},{2,6},{3,7},{4,0},{5,1},{6,2},{7,3},{8,12},{9,13},{10,... | collective-permute-start | bytes 12296 | tf_op jit(solution)/shard_map/ppermute | solution.py:452
  36.3 0.4 collective-permute-start.12
  36.7 0.0 collective-permute-done.15.rest_4_.rest_3_
  36.7 0.0 collective-permute-done.14.rest_3_.rest_7_
  36.7 1.2 %collective-permute-done.13.rest_2_.rest_11_ = f32[8,128]{1,0:T(8,128)S(1)} collective-permute-done((f32[8,128]{1,0:T(8,128)S(1)}, f32[8,128]{1,0:T(8,128)S(1)}, u32[]{:S(2)}, u32[]{:S(2)}) %collective-permute-start.13) | collective-permute-done | bytes 4128 | tf_op jit(solution)/shard_map/ppermute | solution.py:452
  37.9 0.0 collective-permute-done.12.rest_1_.rest_15_
  37.9 0.6 %sums.1 = f32[32,1,128]{2,1,0:T(1,128)S(1)} custom-call(s32[14,8,128]{2,1,0:T(8,128)S(1)} %get-tuple-element.18.source_ref, f32[8,7,128,128]{3,2,1,0:T(8,128)S(1)} %get-tuple-element.19.blocks_ref, f32[8,128]{1,0:T(8,128)S(1)} %start.1.rest_0_.r_ref, f32[8,128]{1,0:T(8,128)S(1)} %once.1.rest_0_.w_ref, f32[8,128]{1,0:T(8,128)S(1)} %twice.1.rest_0_.v_ref, ...), custom_call_target="tpu_custom_call" | custom-call | tf_op jit(solution)/shard_map/sums/pallas_call | solution.py:497
  38.5 11.4 %all_to_all.5.all_ref = f32[32,1,128]{2,1,0:T(1,128)S(1)} all-to-all(f32[32,1,128]{2,1,0:T(1,128)S(1)} %sums.1), channel_id=1, replica_groups=mesh['gx'=8,'gy'=4] {'gx','gy'}, dimensions={0} | all-to-all | bytes 32768 | tf_op jit(solution)/shard_map/all_to_all | solution.py:513
  49.9 0.0 copy-done
  49.9 1.7 %heads.1 = (f32[8,128]{1,0:T(8,128)}, f32[64,512]{1,0:T(8,128)}) custom-call(s32[5,8,128]{2,1,0:T(8,128)S(1)} %get-tuple-element.16.block_ref, s32[24,128]{1,0:T(8,128)S(1)} %get-tuple-element.17.key_ref, f32[32,1,128]{2,1,0:T(1,128)S(1)} %all_to_all.5.all_ref, s32[64,512]{1,0:T(8,128)S(1)} %copy-done, f32[16,128]{1,0:T(8,128)S(1)} %get-tuple-element.20.own_ref, ...), custom_call_target="tpu_custom_call" | custom-call | tf_op jit(solution)/shard_map/heads/pallas_call | solution.py:517
Async XLA Ops:
  12.4 4.7 %collective-permute-start = (f32[16,128]{1,0:T(8,128)S(1)}, f32[16,128]{1,0:T(8,128)S(1)}, u32[]{:S(2)}, u32[]{:S(2)}) collective-permute-start(f32[16,128]{1,0:T(8,128)S(1)} %get-tuple-element.21), channel_id=1, source_target_pairs={{0,1},{1,0},{2,3},{3,2},{4,5},{5,4},{6,7},{7,6},{8,9},{9,8},{10,11... | collective-permute-start | bytes 24584 | tf_op jit(solution)/shard_map/ppermute | solution.py:494
  12.9 4.2 %collective-permute-start.1 = (f32[16,128]{1,0:T(8,128)S(1)}, f32[16,128]{1,0:T(8,128)S(1)}, u32[]{:S(2)}, u32[]{:S(2)}) collective-permute-start(f32[16,128]{1,0:T(8,128)S(1)} %get-tuple-element.22), channel_id=1, source_target_pairs={{0,4},{1,5},{2,6},{3,7},{4,0},{5,1},{6,2},{7,3},{8,12},{9,13},{10,... | collective-permute-start | bytes 24584 | tf_op jit(solution)/shard_map/ppermute | solution.py:494
  15.5 3.1 %collective-permute-start.2 = (f32[16,128]{1,0:T(8,128)S(1)}, f32[16,128]{1,0:T(8,128)S(1)}, u32[]{:S(2)}, u32[]{:S(2)}) collective-permute-start(f32[16,128]{1,0:T(8,128)S(1)} %get-tuple-element.23), channel_id=1, source_target_pairs={{0,3},{1,2},{2,1},{3,0},{4,7},{5,6},{6,5},{7,4},{8,11},{9,10},{10,... | collective-permute-start | bytes 24584 | tf_op jit(solution)/shard_map/ppermute | solution.py:494
  16.7 1.8 %collective-permute-start.3 = (f32[16,128]{1,0:T(8,128)S(1)}, f32[16,128]{1,0:T(8,128)S(1)}, u32[]{:S(2)}, u32[]{:S(2)}) collective-permute-start(f32[16,128]{1,0:T(8,128)S(1)} %get-tuple-element.24), channel_id=1, source_target_pairs={{0,1},{1,0},{2,3},{3,2},{4,8},{5,9},{6,10},{7,11},{8,4},{9,5},{10,... | collective-permute-start | bytes 24584 | tf_op jit(solution)/shard_map/ppermute | solution.py:494
  19.0 6.2 %collective-permute-start.7 = (f32[8,128]{1,0:T(8,128)S(1)}, f32[8,128]{1,0:T(8,128)S(1)}, u32[]{:S(2)}, u32[]{:S(2)}) collective-permute-start(f32[8,128]{1,0:T(8,128)S(1)} %start.1.rest_0_.r_ref), channel_id=1, source_target_pairs={{0,1},{1,0},{2,3},{3,2},{4,8},{5,9},{6,10},{7,11},{8,4},{9,5},{10,... | collective-permute-start | bytes 12296 | tf_op jit(solution)/shard_map/ppermute | solution.py:452
  19.2 6.0 %collective-permute-start.6 = (f32[8,128]{1,0:T(8,128)S(1)}, f32[8,128]{1,0:T(8,128)S(1)}, u32[]{:S(2)}, u32[]{:S(2)}) collective-permute-start(f32[8,128]{1,0:T(8,128)S(1)} %start.1.rest_0_.r_ref), channel_id=1, source_target_pairs={{0,3},{1,2},{2,1},{3,0},{4,7},{5,6},{6,5},{7,4},{8,11},{9,10},{10,... | collective-permute-start | bytes 12296 | tf_op jit(solution)/shard_map/ppermute | solution.py:452
  20.7 5.8 %collective-permute-start.5 = (f32[8,128]{1,0:T(8,128)S(1)}, f32[8,128]{1,0:T(8,128)S(1)}, u32[]{:S(2)}, u32[]{:S(2)}) collective-permute-start(f32[8,128]{1,0:T(8,128)S(1)} %start.1.rest_0_.r_ref), channel_id=1, source_target_pairs={{0,4},{1,5},{2,6},{3,7},{4,0},{5,1},{6,2},{7,3},{8,12},{9,13},{10,... | collective-permute-start | bytes 12296 | tf_op jit(solution)/shard_map/ppermute | solution.py:452
  24.8 1.6 %collective-permute-start.4 = (f32[8,128]{1,0:T(8,128)S(1)}, f32[8,128]{1,0:T(8,128)S(1)}, u32[]{:S(2)}, u32[]{:S(2)}) collective-permute-start(f32[8,128]{1,0:T(8,128)S(1)} %start.1.rest_0_.r_ref), channel_id=1, source_target_pairs={{0,1},{1,0},{2,3},{3,2},{4,5},{5,4},{6,7},{7,6},{8,9},{9,8},{10,11... | collective-permute-start | bytes 12296 | tf_op jit(solution)/shard_map/ppermute | solution.py:452
  26.9 23.0 %copy-start = (s32[64,512]{1,0:T(8,128)S(1)}, s32[64,512]{1,0:T(8,128)}, u32[]{:S(2)}) copy-start(s32[64,512]{1,0:T(8,128)} %target_ref.1) | copy-start | bytes 393220
  26.9 4.0 %collective-permute-start.11 = (f32[8,128]{1,0:T(8,128)S(1)}, f32[8,128]{1,0:T(8,128)S(1)}, u32[]{:S(2)}, u32[]{:S(2)}) collective-permute-start(f32[8,128]{1,0:T(8,128)S(1)} %once.1.rest_0_.w_ref), channel_id=1, source_target_pairs={{0,1},{1,0},{2,3},{3,2},{4,8},{5,9},{6,10},{7,11},{8,4},{9,5},{10,... | collective-permute-start | bytes 12296 | tf_op jit(solution)/shard_map/ppermute | solution.py:452
  26.9 4.0 %collective-permute-start.10 = (f32[8,128]{1,0:T(8,128)S(1)}, f32[8,128]{1,0:T(8,128)S(1)}, u32[]{:S(2)}, u32[]{:S(2)}) collective-permute-start(f32[8,128]{1,0:T(8,128)S(1)} %once.1.rest_0_.w_ref), channel_id=1, source_target_pairs={{0,3},{1,2},{2,1},{3,0},{4,7},{5,6},{6,5},{7,4},{8,11},{9,10},{10,... | collective-permute-start | bytes 12296 | tf_op jit(solution)/shard_map/ppermute | solution.py:452
  28.1 4.2 %collective-permute-start.9 = (f32[8,128]{1,0:T(8,128)S(1)}, f32[8,128]{1,0:T(8,128)S(1)}, u32[]{:S(2)}, u32[]{:S(2)}) collective-permute-start(f32[8,128]{1,0:T(8,128)S(1)} %once.1.rest_0_.w_ref), channel_id=1, source_target_pairs={{0,4},{1,5},{2,6},{3,7},{4,0},{5,1},{6,2},{7,3},{8,12},{9,13},{10,... | collective-permute-start | bytes 12296 | tf_op jit(solution)/shard_map/ppermute | solution.py:452
  30.7 1.6 %collective-permute-start.8 = (f32[8,128]{1,0:T(8,128)S(1)}, f32[8,128]{1,0:T(8,128)S(1)}, u32[]{:S(2)}, u32[]{:S(2)}) collective-permute-start(f32[8,128]{1,0:T(8,128)S(1)} %once.1.rest_0_.w_ref), channel_id=1, source_target_pairs={{0,1},{1,0},{2,3},{3,2},{4,5},{5,4},{6,7},{7,6},{8,9},{9,8},{10,11... | collective-permute-start | bytes 12296 | tf_op jit(solution)/shard_map/ppermute | solution.py:452
  32.8 3.9 %collective-permute-start.15 = (f32[8,128]{1,0:T(8,128)S(1)}, f32[8,128]{1,0:T(8,128)S(1)}, u32[]{:S(2)}, u32[]{:S(2)}) collective-permute-start(f32[8,128]{1,0:T(8,128)S(1)} %twice.1.rest_0_.v_ref), channel_id=1, source_target_pairs={{0,1},{1,0},{2,3},{3,2},{4,8},{5,9},{6,10},{7,11},{8,4},{9,5},{10,... | collective-permute-start | bytes 12296 | tf_op jit(solution)/shard_map/ppermute | solution.py:452
  32.8 3.9 %collective-permute-start.14 = (f32[8,128]{1,0:T(8,128)S(1)}, f32[8,128]{1,0:T(8,128)S(1)}, u32[]{:S(2)}, u32[]{:S(2)}) collective-permute-start(f32[8,128]{1,0:T(8,128)S(1)} %twice.1.rest_0_.v_ref), channel_id=1, source_target_pairs={{0,3},{1,2},{2,1},{3,0},{4,7},{5,6},{6,5},{7,4},{8,11},{9,10},{10,... | collective-permute-start | bytes 12296 | tf_op jit(solution)/shard_map/ppermute | solution.py:452
  33.5 4.4 %collective-permute-start.13 = (f32[8,128]{1,0:T(8,128)S(1)}, f32[8,128]{1,0:T(8,128)S(1)}, u32[]{:S(2)}, u32[]{:S(2)}) collective-permute-start(f32[8,128]{1,0:T(8,128)S(1)} %twice.1.rest_0_.v_ref), channel_id=1, source_target_pairs={{0,4},{1,5},{2,6},{3,7},{4,0},{5,1},{6,2},{7,3},{8,12},{9,13},{10,... | collective-permute-start | bytes 12296 | tf_op jit(solution)/shard_map/ppermute | solution.py:452
  36.3 1.6 %collective-permute-start.12 = (f32[8,128]{1,0:T(8,128)S(1)}, f32[8,128]{1,0:T(8,128)S(1)}, u32[]{:S(2)}, u32[]{:S(2)}) collective-permute-start(f32[8,128]{1,0:T(8,128)S(1)} %twice.1.rest_0_.v_ref), channel_id=1, source_target_pairs={{0,1},{1,0},{2,3},{3,2},{4,5},{5,4},{6,7},{7,6},{8,9},{9,8},{10,11... | collective-permute-start | bytes 12296 | tf_op jit(solution)/shard_map/ppermute | solution.py:452

commit v4 on v3

--- a/solution.py
+++ b/solution.py
@@ -58,7 +58,7 @@
     return found
 
 
-def soil_tile(place, water_ref, porosity_ref, conduct_ref, exponent_ref, inflow_ref, recharge_ref):
+def soil_tile(place, water_ref, porosity_ref, conduct_ref, exponent_ref, inflow_ref):
     layers = water_ref.shape[0]
     power = exponent_ref[place]
     less = power - 1.0
@@ -99,7 +99,7 @@
                     water_ref[here] = content * back + RESIDUAL if last else content
         for flux in fluxes:
             total = flux if total is None else total + flux
-    recharge_ref[place] = total * (back * inverse)
+    return total * (back * inverse)
 
 
 def bin_rows(target, value, keys, totals_ref, width):
@@ -169,7 +169,7 @@
         blocks_out, water_ref, porosity_ref, conduct_ref, exponent_ref, inflow_ref, target_ref,
         heads_ref, send_ref, pattern_ref, recharge_ref, totals_ref, small_sems, in_sems, out_sems, blocks_sem,
     ) = rest[SIDES:]
-    rows, columns = recharge_ref.shape
+    rows, columns = target_ref.shape
     own_blocks, width = heads_ref.shape
     slots = send_ref.shape[0]
     hi_rows = key_ref.shape[0]
@@ -198,12 +198,18 @@
     for copy in small_copies() + incoming(0) + incoming(1):
         copy.start()
     totals_ref[...] = jnp.zeros_like(totals_ref)
+    recharge_ref[0:8, :] = jnp.zeros((8, columns), F32)
     for copy in small_copies():
         copy.wait()
     prepare(
         gx_count, gy_count, send_ref[...], pattern_ref[...], own_blocks, source_ref, block_ref, key_ref
     )
 
+    def bin_tile(tile):
+        target = target_ref[pl.ds(pl.multiple_of(jnp.maximum(tile, 0) * 8, 8), 8), :]
+        value = recharge_ref[pl.ds(pl.multiple_of(tile * 8 + 8, 8), 8), :]
+        bin_rows(target, value, key_ref[...], totals_ref, width)
+
     @pl.loop(0, chunks)
     def _(at):
         for copy in incoming(at):
@@ -220,13 +226,16 @@
 
         @pl.loop(0, chunk // 8)
         def _(tile):
-            place = (pl.ds(pl.multiple_of(at * chunk + tile * 8, 8), 8), slice(None))
-            soil_tile(place, water_ref, porosity_ref, conduct_ref, exponent_ref, inflow_ref, recharge_ref)
+            tile = at * (chunk // 8) + tile
+            bin_tile(tile - 1)
+            place = (pl.ds(pl.multiple_of(tile * 8, 8), 8), slice(None))
+            recharge_ref[pl.ds(pl.multiple_of(tile * 8 + 8, 8), 8), :] = soil_tile(
+                place, water_ref, porosity_ref, conduct_ref, exponent_ref, inflow_ref
+            )
 
         outgoing(at).start()
-        here = (pl.ds(pl.multiple_of(at * chunk, 8), chunk), slice(None))
-        bin_rows(target_ref[here], recharge_ref[here], key_ref[...], totals_ref, width)
-
+
+    bin_tile(rows // 8 - 1)
     sums = totals_ref[0:hi_rows, :] + totals_ref[hi_rows : 2 * hi_rows, :]
     block = lax.broadcasted_iota(jnp.int32, (own_blocks, width), 0)
     for k in range(SIDES + 1):
@@ -274,7 +283,7 @@
 
 
 def start_kernel(area, source_ref, blocks_ref, own_ref, *rest):
-    side_refs, residual_ref = rest[:SIDES][::-1], rest[SIDES]
+    side_refs, residual_ref = rest[:SIDES], rest[SIDES]
     own_blocks = residual_ref.shape[0]
     heads = own_ref[own_blocks:, :]
     cells = own_ref[:own_blocks, :]
@@ -471,7 +480,7 @@
             pltpu.VMEM((own_blocks, width), F32),
             pltpu.VMEM((slots, devices), jnp.int32),
             pltpu.VMEM((own_blocks, most), jnp.int32),
-            pltpu.VMEM((rows, columns), F32),
+            pltpu.VMEM((rows + 8, columns), F32),
             pltpu.VMEM((2 * hi_rows, width), F32),
             pltpu.SemaphoreType.DMA((3,)),
             pltpu.SemaphoreType.DMA((chunks, 6)),
@@ -503,7 +512,7 @@
             name=name,
         )(source, blocks, *args)
 
-    r = small(functools.partial(start_kernel, area), (own, *got[::-1]), field, "start")
+    r = small(functools.partial(start_kernel, area), (own, *got), field, "start")
     r_sides = trade(r)
     w = small(apply_kernel, (r, *r_sides[::-1]), field, "once")
     w_sides = trade(w)

time: 51.8 us -> 50.4 us (0.973)
  waiting for transfers between devices: 5.32 us -> 3.58 us
  blocking collectives: 11.4 us -> 12.1 us
  Pallas kernels: 15.4 us -> 14.8 us
    ppermute x12, waiting for transfers between devices: 3.85 us -> 2.63 us  [trade(): return [lax.ppermute(array, BOTH, perm) for perm in perms]]
    ppermute x4, starting transfers between devices: 4.72 us -> 5.88 us  [body(): got = [lax.ppermute(out, BOTH, perm) for out, perm in zip(outs[5:], perms)]]
    ppermute x12, starting transfers between devices: 14.1 us -> 13.2 us  [trade(): return [lax.ppermute(array, BOTH, perm) for perm in perms]]
    all_to_all x1, blocking collectives: 11.4 us -> 12.1 us  [body(): all_sums = lax.all_to_all(sums, BOTH, 0, 0)]
    pallas_call x1, Pallas kernels: 11.7 us -> 11.1 us  [body(): pl.pallas_call(functools.partial(soil_kernel, gx_count, gy_count), in_spe...]
  transfers between devices with their start and end apart: 16 -> 16, of which waited for: 4 -> 6; matrix products, arithmetic and copies ran while one was open for 0% -> 0% of each run, Pallas kernels for 0% -> 0%
where the time goes in v4:
time: 50.4 us; the launch traced here: 50.2 us
  starting transfers between devices  19.1 us (38%)
  Pallas kernels  14.8 us (29%)
  blocking collectives  12.1 us (24%)
  waiting for transfers between devices  3.58 us (7%)
  between operations  0.67 us (1%)
    ppermute x12, starting transfers between devices, trade(): return [lax.ppermute(array, BOTH, perm) for perm in perms]  13.2 us
    all_to_all x1, blocking collectives, body(): all_sums = lax.all_to_all(sums, BOTH, 0, 0)  12.1 us
    pallas_call x1, Pallas kernels, body(): pl.pallas_call(functools.partial(soil_kernel, gx_count, gy_count), in_spe...  11.1 us
    ppermute x4, starting transfers between devices, body(): got = [lax.ppermute(out, BOTH, perm) for out, perm in zip(outs[5:], perms)]  5.88 us
    ppermute x12, waiting for transfers between devices, trade(): return [lax.ppermute(array, BOTH, perm) for perm in perms]  2.63 us
    pallas_call x4, Pallas kernels, small(): pl.pallas_call(kernel, in_specs=[VMEM] * (2 + len(args)), out_specs=VMEM,...  2.03 us
    pallas_call x1, Pallas kernels, body(): pl.pallas_call(functools.partial(heads_kernel, slots), in_specs=[VMEM] *...  1.7 us
  transfers between devices with their start and end apart: 16, of which 6 were waited for; matrix products, arithmetic and copies ran while one was open for 0% of the time, Pallas kernels for 0%

profile of v4, /device:TPU:0, one launch (start us, length us, event | category | flops | bytes accessed | tf_op | source)
XLA Modules:
  0.0 50.2 jit_solution(7611890871758833632)
XLA Ops:
  0.6 11.1 %soil.1 = (f32[16,64,512]{2,1,0:T(8,128)}, s32[14,8,128]{2,1,0:T(8,128)S(1)}, s32[5,8,128]{2,1,0:T(8,128)S(1)}, s32[24,128]{1,0:T(8,128)S(1)}, f32[16,128]{1,0:T...) custom-call(f32[16,64,512]{2,1,0:T(8,128)} %water_hbm.1, ...), custom_call_target="tpu_custom_call" | custom-call | tf_op jit(solution)/shard_map/soil/pallas_call | solution.py:464
  11.7 0.5 %collective-permute-start = (f32[16,128]{1,0:T(8,128)S(1)}, f32[16,128]{1,0:T(8,128)S(1)}, u32[]{:S(2)}, u32[]{:S(2)}) collective-permute-start(f32[16,128]{1,0:T(8,128)S(1)} %get-tuple-element.21), channel_id=1, source_target_pairs={{0,1},{1,0},{2,3},{3,2},{4,8},{5,9},{6,10},{7,11},{8,4},{9,5},{10,... | collective-permute-start | bytes 24584 | tf_op jit(solution)/shard_map/ppermute | solution.py:503
  12.2 2.6 %collective-permute-start.1 = (f32[16,128]{1,0:T(8,128)S(1)}, f32[16,128]{1,0:T(8,128)S(1)}, u32[]{:S(2)}, u32[]{:S(2)}) collective-permute-start(f32[16,128]{1,0:T(8,128)S(1)} %get-tuple-element.22), channel_id=1, source_target_pairs={{0,3},{1,2},{2,1},{3,0},{4,7},{5,6},{6,5},{7,4},{8,11},{9,10},{10,... | collective-permute-start | bytes 24584 | tf_op jit(solution)/shard_map/ppermute | solution.py:503
  14.8 2.1 %collective-permute-start.2 = (f32[16,128]{1,0:T(8,128)S(1)}, f32[16,128]{1,0:T(8,128)S(1)}, u32[]{:S(2)}, u32[]{:S(2)}) collective-permute-start(f32[16,128]{1,0:T(8,128)S(1)} %get-tuple-element.23), channel_id=1, source_target_pairs={{0,4},{1,5},{2,6},{3,7},{4,0},{5,1},{6,2},{7,3},{8,12},{9,13},{10,... | collective-permute-start | bytes 24584 | tf_op jit(solution)/shard_map/ppermute | solution.py:503
  16.9 0.7 %collective-permute-start.3 = (f32[16,128]{1,0:T(8,128)S(1)}, f32[16,128]{1,0:T(8,128)S(1)}, u32[]{:S(2)}, u32[]{:S(2)}) collective-permute-start(f32[16,128]{1,0:T(8,128)S(1)} %get-tuple-element.24), channel_id=1, source_target_pairs={{0,1},{1,0},{2,3},{3,2},{4,5},{5,4},{6,7},{7,6},{8,9},{9,8},{10,11... | collective-permute-start | bytes 24584 | tf_op jit(solution)/shard_map/ppermute | solution.py:503
  17.6 0.0 collective-permute-done.rest_0_
  17.6 0.0 collective-permute-done.1.rest_1_.rest_4_
  17.6 0.9 %collective-permute-done.2.rest_2_.rest_8_ = f32[16,128]{1,0:T(8,128)S(1)} collective-permute-done((f32[16,128]{1,0:T(8,128)S(1)}, f32[16,128]{1,0:T(8,128)S(1)}, u32[]{:S(2)}, u32[]{:S(2)}) %collective-permute-start.2) | collective-permute-done | bytes 8224 | tf_op jit(solution)/shard_map/ppermute | solution.py:503
  18.5 0.0 collective-permute-done.3.rest_3_.rest_12_
  18.5 0.5 start.1.rest_0_.r_ref
  19.0 0.2 collective-permute-start.7
  19.2 0.8 %collective-permute-start.6 = (f32[8,128]{1,0:T(8,128)S(1)}, f32[8,128]{1,0:T(8,128)S(1)}, u32[]{:S(2)}, u32[]{:S(2)}) collective-permute-start(f32[8,128]{1,0:T(8,128)S(1)} %start.1.rest_0_.r_ref), channel_id=1, source_target_pairs={{0,3},{1,2},{2,1},{3,0},{4,7},{5,6},{6,5},{7,4},{8,11},{9,10},{10,... | collective-permute-start | bytes 12296 | tf_op jit(solution)/shard_map/ppermute | solution.py:461
  20.0 2.5 %collective-permute-start.5 = (f32[8,128]{1,0:T(8,128)S(1)}, f32[8,128]{1,0:T(8,128)S(1)}, u32[]{:S(2)}, u32[]{:S(2)}) collective-permute-start(f32[8,128]{1,0:T(8,128)S(1)} %start.1.rest_0_.r_ref), channel_id=1, source_target_pairs={{0,4},{1,5},{2,6},{3,7},{4,0},{5,1},{6,2},{7,3},{8,12},{9,13},{10,... | collective-permute-start | bytes 12296 | tf_op jit(solution)/shard_map/ppermute | solution.py:461
  22.5 0.6 %collective-permute-start.4 = (f32[8,128]{1,0:T(8,128)S(1)}, f32[8,128]{1,0:T(8,128)S(1)}, u32[]{:S(2)}, u32[]{:S(2)}) collective-permute-start(f32[8,128]{1,0:T(8,128)S(1)} %start.1.rest_0_.r_ref), channel_id=1, source_target_pairs={{0,1},{1,0},{2,3},{3,2},{4,5},{5,4},{6,7},{7,6},{8,9},{9,8},{10,11... | collective-permute-start | bytes 12296 | tf_op jit(solution)/shard_map/ppermute | solution.py:461
  23.1 0.0 collective-permute-done.7.rest_4_.rest_1_
  23.1 0.0 collective-permute-done.6.rest_3_.rest_5_
  23.1 1.0 %collective-permute-done.5.rest_2_.rest_9_ = f32[8,128]{1,0:T(8,128)S(1)} collective-permute-done((f32[8,128]{1,0:T(8,128)S(1)}, f32[8,128]{1,0:T(8,128)S(1)}, u32[]{:S(2)}, u32[]{:S(2)}) %collective-permute-start.5) | collective-permute-done | bytes 4128 | tf_op jit(solution)/shard_map/ppermute | solution.py:461
  24.1 0.0 collective-permute-done.4.rest_1_.rest_13_
  24.1 0.5 once.1.rest_0_.w_ref
  24.6 0.0 copy-start
  24.6 0.2 collective-permute-start.11
  24.8 1.4 %collective-permute-start.10 = (f32[8,128]{1,0:T(8,128)S(1)}, f32[8,128]{1,0:T(8,128)S(1)}, u32[]{:S(2)}, u32[]{:S(2)}) collective-permute-start(f32[8,128]{1,0:T(8,128)S(1)} %once.1.rest_0_.w_ref), channel_id=1, source_target_pairs={{0,3},{1,2},{2,1},{3,0},{4,7},{5,6},{6,5},{7,4},{8,11},{9,10},{10,... | collective-permute-start | bytes 12296 | tf_op jit(solution)/shard_map/ppermute | solution.py:461
  26.2 2.3 %collective-permute-start.9 = (f32[8,128]{1,0:T(8,128)S(1)}, f32[8,128]{1,0:T(8,128)S(1)}, u32[]{:S(2)}, u32[]{:S(2)}) collective-permute-start(f32[8,128]{1,0:T(8,128)S(1)} %once.1.rest_0_.w_ref), channel_id=1, source_target_pairs={{0,4},{1,5},{2,6},{3,7},{4,0},{5,1},{6,2},{7,3},{8,12},{9,13},{10,... | collective-permute-start | bytes 12296 | tf_op jit(solution)/shard_map/ppermute | solution.py:461
  28.5 1.0 %collective-permute-start.8 = (f32[8,128]{1,0:T(8,128)S(1)}, f32[8,128]{1,0:T(8,128)S(1)}, u32[]{:S(2)}, u32[]{:S(2)}) collective-permute-start(f32[8,128]{1,0:T(8,128)S(1)} %once.1.rest_0_.w_ref), channel_id=1, source_target_pairs={{0,1},{1,0},{2,3},{3,2},{4,5},{5,4},{6,7},{7,6},{8,9},{9,8},{10,11... | collective-permute-start | bytes 12296 | tf_op jit(solution)/shard_map/ppermute | solution.py:461
  29.5 0.0 collective-permute-done.11.rest_4_.rest_2_
  29.5 0.0 collective-permute-done.10.rest_3_.rest_6_
  29.5 0.6 %collective-permute-done.9.rest_2_.rest_10_ = f32[8,128]{1,0:T(8,128)S(1)} collective-permute-done((f32[8,128]{1,0:T(8,128)S(1)}, f32[8,128]{1,0:T(8,128)S(1)}, u32[]{:S(2)}, u32[]{:S(2)}) %collective-permute-start.9) | collective-permute-done | bytes 4128 | tf_op jit(solution)/shard_map/ppermute | solution.py:461
  30.1 0.2 collective-permute-done.8.rest_1_.rest_14_
  30.3 0.5 twice.1.rest_0_.v_ref
  30.8 0.4 collective-permute-start.15
  31.1 0.7 %collective-permute-start.14 = (f32[8,128]{1,0:T(8,128)S(1)}, f32[8,128]{1,0:T(8,128)S(1)}, u32[]{:S(2)}, u32[]{:S(2)}) collective-permute-start(f32[8,128]{1,0:T(8,128)S(1)} %twice.1.rest_0_.v_ref), channel_id=1, source_target_pairs={{0,3},{1,2},{2,1},{3,0},{4,7},{5,6},{6,5},{7,4},{8,11},{9,10},{10,... | collective-permute-start | bytes 12296 | tf_op jit(solution)/shard_map/ppermute | solution.py:461
  31.9 2.2 %collective-permute-start.13 = (f32[8,128]{1,0:T(8,128)S(1)}, f32[8,128]{1,0:T(8,128)S(1)}, u32[]{:S(2)}, u32[]{:S(2)}) collective-permute-start(f32[8,128]{1,0:T(8,128)S(1)} %twice.1.rest_0_.v_ref), channel_id=1, source_target_pairs={{0,4},{1,5},{2,6},{3,7},{4,0},{5,1},{6,2},{7,3},{8,12},{9,13},{10,... | collective-permute-start | bytes 12296 | tf_op jit(solution)/shard_map/ppermute | solution.py:461
  34.1 0.9 %collective-permute-start.12 = (f32[8,128]{1,0:T(8,128)S(1)}, f32[8,128]{1,0:T(8,128)S(1)}, u32[]{:S(2)}, u32[]{:S(2)}) collective-permute-start(f32[8,128]{1,0:T(8,128)S(1)} %twice.1.rest_0_.v_ref), channel_id=1, source_target_pairs={{0,1},{1,0},{2,3},{3,2},{4,5},{5,4},{6,7},{7,6},{8,9},{9,8},{10,11... | collective-permute-start | bytes 12296 | tf_op jit(solution)/shard_map/ppermute | solution.py:461
  35.0 0.0 collective-permute-done.15.rest_4_.rest_3_
  35.0 0.0 collective-permute-done.14.rest_3_.rest_7_
  35.0 0.7 %collective-permute-done.13.rest_2_.rest_11_ = f32[8,128]{1,0:T(8,128)S(1)} collective-permute-done((f32[8,128]{1,0:T(8,128)S(1)}, f32[8,128]{1,0:T(8,128)S(1)}, u32[]{:S(2)}, u32[]{:S(2)}) %collective-permute-start.13) | collective-permute-done | bytes 4128 | tf_op jit(solution)/shard_map/ppermute | solution.py:461
  35.7 0.1 collective-permute-done.12.rest_1_.rest_15_
  35.8 0.6 %sums.1 = f32[32,1,128]{2,1,0:T(1,128)S(1)} custom-call(s32[14,8,128]{2,1,0:T(8,128)S(1)} %get-tuple-element.18.source_ref, f32[8,7,128,128]{3,2,1,0:T(8,128)S(1)} %get-tuple-element.19.blocks_ref, f32[8,128]{1,0:T(8,128)S(1)} %start.1.rest_0_.r_ref, f32[8,128]{1,0:T(8,128)S(1)} %once.1.rest_0_.w_ref, f32[8,128]{1,0:T(8,128)S(1)} %twice.1.rest_0_.v_ref, ...), custom_call_target="tpu_custom_call" | custom-call | tf_op jit(solution)/shard_map/sums/pallas_call | solution.py:506
  36.4 12.1 %all_to_all.5.all_ref = f32[32,1,128]{2,1,0:T(1,128)S(1)} all-to-all(f32[32,1,128]{2,1,0:T(1,128)S(1)} %sums.1), channel_id=1, replica_groups=mesh['gx'=8,'gy'=4] {'gx','gy'}, dimensions={0} | all-to-all | bytes 32768 | tf_op jit(solution)/shard_map/all_to_all | solution.py:522
  48.5 0.0 copy-done
  48.5 1.7 %heads.1 = (f32[8,128]{1,0:T(8,128)}, f32[64,512]{1,0:T(8,128)}) custom-call(s32[5,8,128]{2,1,0:T(8,128)S(1)} %get-tuple-element.16.block_ref, s32[24,128]{1,0:T(8,128)S(1)} %get-tuple-element.17.key_ref, f32[32,1,128]{2,1,0:T(1,128)S(1)} %all_to_all.5.all_ref, s32[64,512]{1,0:T(8,128)S(1)} %copy-done, f32[16,128]{1,0:T(8,128)S(1)} %get-tuple-element.20.own_ref, ...), custom_call_target="tpu_custom_call" | custom-call | tf_op jit(solution)/shard_map/heads/pallas_call | solution.py:526
Async XLA Ops:
  11.7 5.9 %collective-permute-start = (f32[16,128]{1,0:T(8,128)S(1)}, f32[16,128]{1,0:T(8,128)S(1)}, u32[]{:S(2)}, u32[]{:S(2)}) collective-permute-start(f32[16,128]{1,0:T(8,128)S(1)} %get-tuple-element.21), channel_id=1, source_target_pairs={{0,1},{1,0},{2,3},{3,2},{4,8},{5,9},{6,10},{7,11},{8,4},{9,5},{10,... | collective-permute-start | bytes 24584 | tf_op jit(solution)/shard_map/ppermute | solution.py:503
  12.2 5.4 %collective-permute-start.1 = (f32[16,128]{1,0:T(8,128)S(1)}, f32[16,128]{1,0:T(8,128)S(1)}, u32[]{:S(2)}, u32[]{:S(2)}) collective-permute-start(f32[16,128]{1,0:T(8,128)S(1)} %get-tuple-element.22), channel_id=1, source_target_pairs={{0,3},{1,2},{2,1},{3,0},{4,7},{5,6},{6,5},{7,4},{8,11},{9,10},{10,... | collective-permute-start | bytes 24584 | tf_op jit(solution)/shard_map/ppermute | solution.py:503
  14.8 3.7 %collective-permute-start.2 = (f32[16,128]{1,0:T(8,128)S(1)}, f32[16,128]{1,0:T(8,128)S(1)}, u32[]{:S(2)}, u32[]{:S(2)}) collective-permute-start(f32[16,128]{1,0:T(8,128)S(1)} %get-tuple-element.23), channel_id=1, source_target_pairs={{0,4},{1,5},{2,6},{3,7},{4,0},{5,1},{6,2},{7,3},{8,12},{9,13},{10,... | collective-permute-start | bytes 24584 | tf_op jit(solution)/shard_map/ppermute | solution.py:503
  16.9 1.6 %collective-permute-start.3 = (f32[16,128]{1,0:T(8,128)S(1)}, f32[16,128]{1,0:T(8,128)S(1)}, u32[]{:S(2)}, u32[]{:S(2)}) collective-permute-start(f32[16,128]{1,0:T(8,128)S(1)} %get-tuple-element.24), channel_id=1, source_target_pairs={{0,1},{1,0},{2,3},{3,2},{4,5},{5,4},{6,7},{7,6},{8,9},{9,8},{10,11... | collective-permute-start | bytes 24584 | tf_op jit(solution)/shard_map/ppermute | solution.py:503
  19.0 4.1 %collective-permute-start.7 = (f32[8,128]{1,0:T(8,128)S(1)}, f32[8,128]{1,0:T(8,128)S(1)}, u32[]{:S(2)}, u32[]{:S(2)}) collective-permute-start(f32[8,128]{1,0:T(8,128)S(1)} %start.1.rest_0_.r_ref), channel_id=1, source_target_pairs={{0,1},{1,0},{2,3},{3,2},{4,8},{5,9},{6,10},{7,11},{8,4},{9,5},{10,... | collective-permute-start | bytes 12296 | tf_op jit(solution)/shard_map/ppermute | solution.py:461
  19.2 3.9 %collective-permute-start.6 = (f32[8,128]{1,0:T(8,128)S(1)}, f32[8,128]{1,0:T(8,128)S(1)}, u32[]{:S(2)}, u32[]{:S(2)}) collective-permute-start(f32[8,128]{1,0:T(8,128)S(1)} %start.1.rest_0_.r_ref), channel_id=1, source_target_pairs={{0,3},{1,2},{2,1},{3,0},{4,7},{5,6},{6,5},{7,4},{8,11},{9,10},{10,... | collective-permute-start | bytes 12296 | tf_op jit(solution)/shard_map/ppermute | solution.py:461
  20.0 4.1 %collective-permute-start.5 = (f32[8,128]{1,0:T(8,128)S(1)}, f32[8,128]{1,0:T(8,128)S(1)}, u32[]{:S(2)}, u32[]{:S(2)}) collective-permute-start(f32[8,128]{1,0:T(8,128)S(1)} %start.1.rest_0_.r_ref), channel_id=1, source_target_pairs={{0,4},{1,5},{2,6},{3,7},{4,0},{5,1},{6,2},{7,3},{8,12},{9,13},{10,... | collective-permute-start | bytes 12296 | tf_op jit(solution)/shard_map/ppermute | solution.py:461
  22.5 1.6 %collective-permute-start.4 = (f32[8,128]{1,0:T(8,128)S(1)}, f32[8,128]{1,0:T(8,128)S(1)}, u32[]{:S(2)}, u32[]{:S(2)}) collective-permute-start(f32[8,128]{1,0:T(8,128)S(1)} %start.1.rest_0_.r_ref), channel_id=1, source_target_pairs={{0,1},{1,0},{2,3},{3,2},{4,5},{5,4},{6,7},{7,6},{8,9},{9,8},{10,11... | collective-permute-start | bytes 12296 | tf_op jit(solution)/shard_map/ppermute | solution.py:461
  24.6 23.9 %copy-start = (s32[64,512]{1,0:T(8,128)S(1)}, s32[64,512]{1,0:T(8,128)}, u32[]{:S(2)}) copy-start(s32[64,512]{1,0:T(8,128)} %target_ref.1) | copy-start | bytes 393220
  24.6 4.9 %collective-permute-start.11 = (f32[8,128]{1,0:T(8,128)S(1)}, f32[8,128]{1,0:T(8,128)S(1)}, u32[]{:S(2)}, u32[]{:S(2)}) collective-permute-start(f32[8,128]{1,0:T(8,128)S(1)} %once.1.rest_0_.w_ref), channel_id=1, source_target_pairs={{0,1},{1,0},{2,3},{3,2},{4,8},{5,9},{6,10},{7,11},{8,4},{9,5},{10,... | collective-permute-start | bytes 12296 | tf_op jit(solution)/shard_map/ppermute | solution.py:461
  24.8 4.7 %collective-permute-start.10 = (f32[8,128]{1,0:T(8,128)S(1)}, f32[8,128]{1,0:T(8,128)S(1)}, u32[]{:S(2)}, u32[]{:S(2)}) collective-permute-start(f32[8,128]{1,0:T(8,128)S(1)} %once.1.rest_0_.w_ref), channel_id=1, source_target_pairs={{0,3},{1,2},{2,1},{3,0},{4,7},{5,6},{6,5},{7,4},{8,11},{9,10},{10,... | collective-permute-start | bytes 12296 | tf_op jit(solution)/shard_map/ppermute | solution.py:461
  26.2 3.8 %collective-permute-start.9 = (f32[8,128]{1,0:T(8,128)S(1)}, f32[8,128]{1,0:T(8,128)S(1)}, u32[]{:S(2)}, u32[]{:S(2)}) collective-permute-start(f32[8,128]{1,0:T(8,128)S(1)} %once.1.rest_0_.w_ref), channel_id=1, source_target_pairs={{0,4},{1,5},{2,6},{3,7},{4,0},{5,1},{6,2},{7,3},{8,12},{9,13},{10,... | collective-permute-start | bytes 12296 | tf_op jit(solution)/shard_map/ppermute | solution.py:461
  28.5 1.8 %collective-permute-start.8 = (f32[8,128]{1,0:T(8,128)S(1)}, f32[8,128]{1,0:T(8,128)S(1)}, u32[]{:S(2)}, u32[]{:S(2)}) collective-permute-start(f32[8,128]{1,0:T(8,128)S(1)} %once.1.rest_0_.w_ref), channel_id=1, source_target_pairs={{0,1},{1,0},{2,3},{3,2},{4,5},{5,4},{6,7},{7,6},{8,9},{9,8},{10,11... | collective-permute-start | bytes 12296 | tf_op jit(solution)/shard_map/ppermute | solution.py:461
  30.8 4.2 %collective-permute-start.15 = (f32[8,128]{1,0:T(8,128)S(1)}, f32[8,128]{1,0:T(8,128)S(1)}, u32[]{:S(2)}, u32[]{:S(2)}) collective-permute-start(f32[8,128]{1,0:T(8,128)S(1)} %twice.1.rest_0_.v_ref), channel_id=1, source_target_pairs={{0,1},{1,0},{2,3},{3,2},{4,8},{5,9},{6,10},{7,11},{8,4},{9,5},{10,... | collective-permute-start | bytes 12296 | tf_op jit(solution)/shard_map/ppermute | solution.py:461
  31.1 3.9 %collective-permute-start.14 = (f32[8,128]{1,0:T(8,128)S(1)}, f32[8,128]{1,0:T(8,128)S(1)}, u32[]{:S(2)}, u32[]{:S(2)}) collective-permute-start(f32[8,128]{1,0:T(8,128)S(1)} %twice.1.rest_0_.v_ref), channel_id=1, source_target_pairs={{0,3},{1,2},{2,1},{3,0},{4,7},{5,6},{6,5},{7,4},{8,11},{9,10},{10,... | collective-permute-start | bytes 12296 | tf_op jit(solution)/shard_map/ppermute | solution.py:461
  31.9 3.8 %collective-permute-start.13 = (f32[8,128]{1,0:T(8,128)S(1)}, f32[8,128]{1,0:T(8,128)S(1)}, u32[]{:S(2)}, u32[]{:S(2)}) collective-permute-start(f32[8,128]{1,0:T(8,128)S(1)} %twice.1.rest_0_.v_ref), channel_id=1, source_target_pairs={{0,4},{1,5},{2,6},{3,7},{4,0},{5,1},{6,2},{7,3},{8,12},{9,13},{10,... | collective-permute-start | bytes 12296 | tf_op jit(solution)/shard_map/ppermute | solution.py:461
  34.1 1.7 %collective-permute-start.12 = (f32[8,128]{1,0:T(8,128)S(1)}, f32[8,128]{1,0:T(8,128)S(1)}, u32[]{:S(2)}, u32[]{:S(2)}) collective-permute-start(f32[8,128]{1,0:T(8,128)S(1)} %twice.1.rest_0_.v_ref), channel_id=1, source_target_pairs={{0,1},{1,0},{2,3},{3,2},{4,5},{5,4},{6,7},{7,6},{8,9},{9,8},{10,11... | collective-permute-start | bytes 12296 | tf_op jit(solution)/shard_map/ppermute | solution.py:461

commit v5 on v4

--- a/solution.py
+++ b/solution.py
@@ -11,6 +11,7 @@
 SWEEPS = 8
 RESIDUAL = 0.05
 SIDES = 4
+PARTS = 2
 BOTH = ("gx", "gy")
 ORDER = ((0, 1), (1, 1), (0, 0), (1, 0))
 F32 = jnp.float32
@@ -102,7 +103,8 @@
     return total * (back * inverse)
 
 
-def bin_rows(target, value, keys, totals_ref, width):
+def bin_rows(target, value, keys, totals_ref):
+    width = totals_ref.shape[1]
     rows, columns = target.shape
     slots_high = keys.shape[0]
     shift = width.bit_length() - 1
@@ -132,7 +134,9 @@
     )
 
 
-def prepare(gx_count, gy_count, send, pattern, own_blocks, source_ref, block_ref, key_ref):
+def prepare(
+    gx_count, gy_count, send, pattern, own_blocks, source_ref, block_ref, key_ref, part_key_ref, part_width
+):
     hi_rows, width = key_ref.shape
     slots, devices = send.shape
     owners = owners_here(gx_count, gy_count)
@@ -142,6 +146,16 @@
         inside = (row >= k * slots) & (row < (k + 1) * slots) & (owner >= 0)
         keys = jnp.where(inside, owner * slots + row - k * slots, keys)
     key_ref[...] = keys
+    parts = width // part_width
+    entries = (SIDES + 1) * slots
+    row = lax.broadcasted_iota(jnp.int32, part_key_ref.shape, 0)
+    keys = jnp.full(part_key_ref.shape, -1, jnp.int32)
+    for part in range(parts):
+        for k, owner in enumerate(owners):
+            first = part * entries + k * slots
+            inside = (row >= first) & (row < first + slots) & (owner >= 0)
+            keys = jnp.where(inside, (owner * slots + row - first) * parts + part, keys)
+    part_key_ref[...] = keys
     lane = lax.broadcasted_iota(jnp.int32, (slots, devices), 1)
     block_ref[...] = jnp.full(block_ref.shape, -1, jnp.int32)
     for k, owner in enumerate(owners):
@@ -167,12 +181,11 @@
     side_refs = rest[:SIDES]
     (
         blocks_out, water_ref, porosity_ref, conduct_ref, exponent_ref, inflow_ref, target_ref,
-        heads_ref, send_ref, pattern_ref, recharge_ref, totals_ref, small_sems, in_sems, out_sems, blocks_sem,
+        heads_ref, send_ref, pattern_ref, recharge_ref, part_key_ref, totals_ref, small_sems, in_sems, out_sems, blocks_sem,
     ) = rest[SIDES:]
     rows, columns = target_ref.shape
     own_blocks, width = heads_ref.shape
     slots = send_ref.shape[0]
-    hi_rows = key_ref.shape[0]
     chunks = in_sems.shape[0]
     chunk = rows // chunks
     flats = (
@@ -202,13 +215,14 @@
     for copy in small_copies():
         copy.wait()
     prepare(
-        gx_count, gy_count, send_ref[...], pattern_ref[...], own_blocks, source_ref, block_ref, key_ref
+        gx_count, gy_count, send_ref[...], pattern_ref[...], own_blocks, source_ref, block_ref, key_ref,
+        part_key_ref, totals_ref.shape[1],
     )
 
     def bin_tile(tile):
         target = target_ref[pl.ds(pl.multiple_of(jnp.maximum(tile, 0) * 8, 8), 8), :]
         value = recharge_ref[pl.ds(pl.multiple_of(tile * 8 + 8, 8), 8), :]
-        bin_rows(target, value, key_ref[...], totals_ref, width)
+        bin_rows(target, value, part_key_ref[...], totals_ref)
 
     @pl.loop(0, chunks)
     def _(at):
@@ -224,8 +238,7 @@
         def _():
             blocks_copy.start()
 
-        @pl.loop(0, chunk // 8)
-        def _(tile):
+        for tile in range(chunk // 8):
             tile = at * (chunk // 8) + tile
             bin_tile(tile - 1)
             place = (pl.ds(pl.multiple_of(tile * 8, 8), 8), slice(None))
@@ -236,7 +249,11 @@
         outgoing(at).start()
 
     bin_tile(rows // 8 - 1)
-    sums = totals_ref[0:hi_rows, :] + totals_ref[hi_rows : 2 * hi_rows, :]
+    part_rows = part_key_ref.shape[0]
+    entries = (SIDES + 1) * slots
+    sums = totals_ref[0:part_rows, :] + totals_ref[part_rows : 2 * part_rows, :]
+    parts = width // totals_ref.shape[1]
+    sums = jnp.concatenate([sums[part * entries : (part + 1) * entries] for part in range(parts)], axis=1)
     block = lax.broadcasted_iota(jnp.int32, (own_blocks, width), 0)
     for k in range(SIDES + 1):
         out_ref = side_refs[k - 1] if k else own_ref
@@ -451,6 +468,7 @@
     layers, rows, columns = water_content.shape
     most = block_pattern.shape[1]
     hi_rows = -(-(SIDES + 1) * slots // 8) * 8
+    part_rows = -(-PARTS * (SIDES + 1) * slots // 8) * 8
     area = own_blocks * width / (rows * columns)
     perms = swaps(gx_count, gy_count)
     in_hbm = lambda array: pltpu.with_memory_space_constraint(array, pltpu.HBM)
@@ -481,7 +499,8 @@
             pltpu.VMEM((slots, devices), jnp.int32),
             pltpu.VMEM((own_blocks, most), jnp.int32),
             pltpu.VMEM((rows + 8, columns), F32),
-            pltpu.VMEM((2 * hi_rows, width), F32),
+            pltpu.VMEM((part_rows, width), jnp.int32),
+            pltpu.VMEM((2 * part_rows, width // PARTS), F32),
             pltpu.SemaphoreType.DMA((3,)),
             pltpu.SemaphoreType.DMA((chunks, 6)),
             pltpu.SemaphoreType.DMA((chunks,)),

time: 50.4 us -> 49.6 us (0.984)
  Pallas kernels: 14.8 us -> 14 us
    pallas_call x1, Pallas kernels: 11.1 us -> 10.3 us  [body(): pl.pallas_call(functools.partial(soil_kernel, gx_count, gy_count), in_spe...]
where the time goes in v5:
time: 49.6 us; the launch traced here: 49.5 us
  starting transfers between devices  19.1 us (39%)
  Pallas kernels  14 us (28%)
  blocking collectives  12.1 us (24%)
  waiting for transfers between devices  3.58 us (7%)
  between operations  0.67 us (1%)
    ppermute x12, starting transfers between devices, trade(): return [lax.ppermute(array, BOTH, perm) for perm in perms]  13.2 us
    all_to_all x1, blocking collectives, body(): all_sums = lax.all_to_all(sums, BOTH, 0, 0)  12.1 us
    pallas_call x1, Pallas kernels, body(): pl.pallas_call(functools.partial(soil_kernel, gx_count, gy_count), in_spe...  10.3 us
    ppermute x4, starting transfers between devices, body(): got = [lax.ppermute(out, BOTH, perm) for out, perm in zip(outs[5:], perms)]  5.88 us
    ppermute x12, waiting for transfers between devices, trade(): return [lax.ppermute(array, BOTH, perm) for perm in perms]  2.63 us
    pallas_call x4, Pallas kernels, small(): pl.pallas_call(kernel, in_specs=[VMEM] * (2 + len(args)), out_specs=VMEM,...  2.03 us
    pallas_call x1, Pallas kernels, body(): pl.pallas_call(functools.partial(heads_kernel, slots), in_specs=[VMEM] *...  1.7 us
  transfers between devices with their start and end apart: 16, of which 6 were waited for; matrix products, arithmetic and copies ran while one was open for 0% of the time, Pallas kernels for 0%

profile of v5, /device:TPU:0, one launch (start us, length us, event | category | flops | bytes accessed | tf_op | source)
XLA Modules:
  0.0 49.5 jit_solution(12111493311746234471)
XLA Ops:
  0.6 10.3 %soil.1 = (f32[16,64,512]{2,1,0:T(8,128)}, s32[14,8,128]{2,1,0:T(8,128)S(1)}, s32[5,8,128]{2,1,0:T(8,128)S(1)}, s32[24,128]{1,0:T(8,128)S(1)}, f32[16,128]{1,0:T...) custom-call(f32[16,64,512]{2,1,0:T(8,128)} %water_hbm.1, ...), custom_call_target="tpu_custom_call" | custom-call | tf_op jit(solution)/shard_map/soil/pallas_call | solution.py:482
  10.9 0.5 %collective-permute-start = (f32[16,128]{1,0:T(8,128)S(1)}, f32[16,128]{1,0:T(8,128)S(1)}, u32[]{:S(2)}, u32[]{:S(2)}) collective-permute-start(f32[16,128]{1,0:T(8,128)S(1)} %get-tuple-element.21), channel_id=1, source_target_pairs={{0,1},{1,0},{2,3},{3,2},{4,8},{5,9},{6,10},{7,11},{8,4},{9,5},{10,... | collective-permute-start | bytes 24584 | tf_op jit(solution)/shard_map/ppermute | solution.py:522
  11.4 2.6 %collective-permute-start.1 = (f32[16,128]{1,0:T(8,128)S(1)}, f32[16,128]{1,0:T(8,128)S(1)}, u32[]{:S(2)}, u32[]{:S(2)}) collective-permute-start(f32[16,128]{1,0:T(8,128)S(1)} %get-tuple-element.22), channel_id=1, source_target_pairs={{0,3},{1,2},{2,1},{3,0},{4,7},{5,6},{6,5},{7,4},{8,11},{9,10},{10,... | collective-permute-start | bytes 24584 | tf_op jit(solution)/shard_map/ppermute | solution.py:522
  14.0 2.1 %collective-permute-start.2 = (f32[16,128]{1,0:T(8,128)S(1)}, f32[16,128]{1,0:T(8,128)S(1)}, u32[]{:S(2)}, u32[]{:S(2)}) collective-permute-start(f32[16,128]{1,0:T(8,128)S(1)} %get-tuple-element.23), channel_id=1, source_target_pairs={{0,4},{1,5},{2,6},{3,7},{4,0},{5,1},{6,2},{7,3},{8,12},{9,13},{10,... | collective-permute-start | bytes 24584 | tf_op jit(solution)/shard_map/ppermute | solution.py:522
  16.1 0.7 %collective-permute-start.3 = (f32[16,128]{1,0:T(8,128)S(1)}, f32[16,128]{1,0:T(8,128)S(1)}, u32[]{:S(2)}, u32[]{:S(2)}) collective-permute-start(f32[16,128]{1,0:T(8,128)S(1)} %get-tuple-element.24), channel_id=1, source_target_pairs={{0,1},{1,0},{2,3},{3,2},{4,5},{5,4},{6,7},{7,6},{8,9},{9,8},{10,11... | collective-permute-start | bytes 24584 | tf_op jit(solution)/shard_map/ppermute | solution.py:522
  16.8 0.0 collective-permute-done.rest_0_
  16.8 0.0 collective-permute-done.1.rest_1_.rest_4_
  16.8 0.9 %collective-permute-done.2.rest_2_.rest_8_ = f32[16,128]{1,0:T(8,128)S(1)} collective-permute-done((f32[16,128]{1,0:T(8,128)S(1)}, f32[16,128]{1,0:T(8,128)S(1)}, u32[]{:S(2)}, u32[]{:S(2)}) %collective-permute-start.2) | collective-permute-done | bytes 8224 | tf_op jit(solution)/shard_map/ppermute | solution.py:522
  17.7 0.0 collective-permute-done.3.rest_3_.rest_12_
  17.7 0.5 start.1.rest_0_.r_ref
  18.2 0.2 collective-permute-start.7
  18.5 0.8 %collective-permute-start.6 = (f32[8,128]{1,0:T(8,128)S(1)}, f32[8,128]{1,0:T(8,128)S(1)}, u32[]{:S(2)}, u32[]{:S(2)}) collective-permute-start(f32[8,128]{1,0:T(8,128)S(1)} %start.1.rest_0_.r_ref), channel_id=1, source_target_pairs={{0,3},{1,2},{2,1},{3,0},{4,7},{5,6},{6,5},{7,4},{8,11},{9,10},{10,... | collective-permute-start | bytes 12296 | tf_op jit(solution)/shard_map/ppermute | solution.py:479
  19.3 2.5 %collective-permute-start.5 = (f32[8,128]{1,0:T(8,128)S(1)}, f32[8,128]{1,0:T(8,128)S(1)}, u32[]{:S(2)}, u32[]{:S(2)}) collective-permute-start(f32[8,128]{1,0:T(8,128)S(1)} %start.1.rest_0_.r_ref), channel_id=1, source_target_pairs={{0,4},{1,5},{2,6},{3,7},{4,0},{5,1},{6,2},{7,3},{8,12},{9,13},{10,... | collective-permute-start | bytes 12296 | tf_op jit(solution)/shard_map/ppermute | solution.py:479
  21.8 0.6 %collective-permute-start.4 = (f32[8,128]{1,0:T(8,128)S(1)}, f32[8,128]{1,0:T(8,128)S(1)}, u32[]{:S(2)}, u32[]{:S(2)}) collective-permute-start(f32[8,128]{1,0:T(8,128)S(1)} %start.1.rest_0_.r_ref), channel_id=1, source_target_pairs={{0,1},{1,0},{2,3},{3,2},{4,5},{5,4},{6,7},{7,6},{8,9},{9,8},{10,11... | collective-permute-start | bytes 12296 | tf_op jit(solution)/shard_map/ppermute | solution.py:479
  22.4 0.0 collective-permute-done.7.rest_4_.rest_1_
  22.4 0.0 collective-permute-done.6.rest_3_.rest_5_
  22.4 1.0 %collective-permute-done.5.rest_2_.rest_9_ = f32[8,128]{1,0:T(8,128)S(1)} collective-permute-done((f32[8,128]{1,0:T(8,128)S(1)}, f32[8,128]{1,0:T(8,128)S(1)}, u32[]{:S(2)}, u32[]{:S(2)}) %collective-permute-start.5) | collective-permute-done | bytes 4128 | tf_op jit(solution)/shard_map/ppermute | solution.py:479
  23.3 0.0 collective-permute-done.4.rest_1_.rest_13_
  23.3 0.5 once.1.rest_0_.w_ref
  23.8 0.0 copy-start
  23.8 0.2 collective-permute-start.11
  24.0 1.4 %collective-permute-start.10 = (f32[8,128]{1,0:T(8,128)S(1)}, f32[8,128]{1,0:T(8,128)S(1)}, u32[]{:S(2)}, u32[]{:S(2)}) collective-permute-start(f32[8,128]{1,0:T(8,128)S(1)} %once.1.rest_0_.w_ref), channel_id=1, source_target_pairs={{0,3},{1,2},{2,1},{3,0},{4,7},{5,6},{6,5},{7,4},{8,11},{9,10},{10,... | collective-permute-start | bytes 12296 | tf_op jit(solution)/shard_map/ppermute | solution.py:479
  25.4 2.3 %collective-permute-start.9 = (f32[8,128]{1,0:T(8,128)S(1)}, f32[8,128]{1,0:T(8,128)S(1)}, u32[]{:S(2)}, u32[]{:S(2)}) collective-permute-start(f32[8,128]{1,0:T(8,128)S(1)} %once.1.rest_0_.w_ref), channel_id=1, source_target_pairs={{0,4},{1,5},{2,6},{3,7},{4,0},{5,1},{6,2},{7,3},{8,12},{9,13},{10,... | collective-permute-start | bytes 12296 | tf_op jit(solution)/shard_map/ppermute | solution.py:479
  27.7 1.0 %collective-permute-start.8 = (f32[8,128]{1,0:T(8,128)S(1)}, f32[8,128]{1,0:T(8,128)S(1)}, u32[]{:S(2)}, u32[]{:S(2)}) collective-permute-start(f32[8,128]{1,0:T(8,128)S(1)} %once.1.rest_0_.w_ref), channel_id=1, source_target_pairs={{0,1},{1,0},{2,3},{3,2},{4,5},{5,4},{6,7},{7,6},{8,9},{9,8},{10,11... | collective-permute-start | bytes 12296 | tf_op jit(solution)/shard_map/ppermute | solution.py:479
  28.7 0.0 collective-permute-done.11.rest_4_.rest_2_
  28.7 0.0 collective-permute-done.10.rest_3_.rest_6_
  28.7 0.6 %collective-permute-done.9.rest_2_.rest_10_ = f32[8,128]{1,0:T(8,128)S(1)} collective-permute-done((f32[8,128]{1,0:T(8,128)S(1)}, f32[8,128]{1,0:T(8,128)S(1)}, u32[]{:S(2)}, u32[]{:S(2)}) %collective-permute-start.9) | collective-permute-done | bytes 4128 | tf_op jit(solution)/shard_map/ppermute | solution.py:479
  29.3 0.2 collective-permute-done.8.rest_1_.rest_14_
  29.5 0.5 twice.1.rest_0_.v_ref
  30.0 0.4 collective-permute-start.15
  30.3 0.7 %collective-permute-start.14 = (f32[8,128]{1,0:T(8,128)S(1)}, f32[8,128]{1,0:T(8,128)S(1)}, u32[]{:S(2)}, u32[]{:S(2)}) collective-permute-start(f32[8,128]{1,0:T(8,128)S(1)} %twice.1.rest_0_.v_ref), channel_id=1, source_target_pairs={{0,3},{1,2},{2,1},{3,0},{4,7},{5,6},{6,5},{7,4},{8,11},{9,10},{10,... | collective-permute-start | bytes 12296 | tf_op jit(solution)/shard_map/ppermute | solution.py:479
  31.1 2.2 %collective-permute-start.13 = (f32[8,128]{1,0:T(8,128)S(1)}, f32[8,128]{1,0:T(8,128)S(1)}, u32[]{:S(2)}, u32[]{:S(2)}) collective-permute-start(f32[8,128]{1,0:T(8,128)S(1)} %twice.1.rest_0_.v_ref), channel_id=1, source_target_pairs={{0,4},{1,5},{2,6},{3,7},{4,0},{5,1},{6,2},{7,3},{8,12},{9,13},{10,... | collective-permute-start | bytes 12296 | tf_op jit(solution)/shard_map/ppermute | solution.py:479
  33.3 0.9 %collective-permute-start.12 = (f32[8,128]{1,0:T(8,128)S(1)}, f32[8,128]{1,0:T(8,128)S(1)}, u32[]{:S(2)}, u32[]{:S(2)}) collective-permute-start(f32[8,128]{1,0:T(8,128)S(1)} %twice.1.rest_0_.v_ref), channel_id=1, source_target_pairs={{0,1},{1,0},{2,3},{3,2},{4,5},{5,4},{6,7},{7,6},{8,9},{9,8},{10,11... | collective-permute-start | bytes 12296 | tf_op jit(solution)/shard_map/ppermute | solution.py:479
  34.2 0.0 collective-permute-done.15.rest_4_.rest_3_
  34.2 0.0 collective-permute-done.14.rest_3_.rest_7_
  34.2 0.7 %collective-permute-done.13.rest_2_.rest_11_ = f32[8,128]{1,0:T(8,128)S(1)} collective-permute-done((f32[8,128]{1,0:T(8,128)S(1)}, f32[8,128]{1,0:T(8,128)S(1)}, u32[]{:S(2)}, u32[]{:S(2)}) %collective-permute-start.13) | collective-permute-done | bytes 4128 | tf_op jit(solution)/shard_map/ppermute | solution.py:479
  34.9 0.1 collective-permute-done.12.rest_1_.rest_15_
  35.0 0.6 %sums.1 = f32[32,1,128]{2,1,0:T(1,128)S(1)} custom-call(s32[14,8,128]{2,1,0:T(8,128)S(1)} %get-tuple-element.18.source_ref, f32[8,7,128,128]{3,2,1,0:T(8,128)S(1)} %get-tuple-element.19.blocks_ref, f32[8,128]{1,0:T(8,128)S(1)} %start.1.rest_0_.r_ref, f32[8,128]{1,0:T(8,128)S(1)} %once.1.rest_0_.w_ref, f32[8,128]{1,0:T(8,128)S(1)} %twice.1.rest_0_.v_ref, ...), custom_call_target="tpu_custom_call" | custom-call | tf_op jit(solution)/shard_map/sums/pallas_call | solution.py:525
  35.6 12.1 %all_to_all.5.all_ref = f32[32,1,128]{2,1,0:T(1,128)S(1)} all-to-all(f32[32,1,128]{2,1,0:T(1,128)S(1)} %sums.1), channel_id=1, replica_groups=mesh['gx'=8,'gy'=4] {'gx','gy'}, dimensions={0} | all-to-all | bytes 32768 | tf_op jit(solution)/shard_map/all_to_all | solution.py:541
  47.8 0.0 copy-done
  47.8 1.7 %heads.1 = (f32[8,128]{1,0:T(8,128)}, f32[64,512]{1,0:T(8,128)}) custom-call(s32[5,8,128]{2,1,0:T(8,128)S(1)} %get-tuple-element.16.block_ref, s32[24,128]{1,0:T(8,128)S(1)} %get-tuple-element.17.key_ref, f32[32,1,128]{2,1,0:T(1,128)S(1)} %all_to_all.5.all_ref, s32[64,512]{1,0:T(8,128)S(1)} %copy-done, f32[16,128]{1,0:T(8,128)S(1)} %get-tuple-element.20.own_ref, ...), custom_call_target="tpu_custom_call" | custom-call | tf_op jit(solution)/shard_map/heads/pallas_call | solution.py:545
Async XLA Ops:
  10.9 5.9 %collective-permute-start = (f32[16,128]{1,0:T(8,128)S(1)}, f32[16,128]{1,0:T(8,128)S(1)}, u32[]{:S(2)}, u32[]{:S(2)}) collective-permute-start(f32[16,128]{1,0:T(8,128)S(1)} %get-tuple-element.21), channel_id=1, source_target_pairs={{0,1},{1,0},{2,3},{3,2},{4,8},{5,9},{6,10},{7,11},{8,4},{9,5},{10,... | collective-permute-start | bytes 24584 | tf_op jit(solution)/shard_map/ppermute | solution.py:522
  11.4 5.4 %collective-permute-start.1 = (f32[16,128]{1,0:T(8,128)S(1)}, f32[16,128]{1,0:T(8,128)S(1)}, u32[]{:S(2)}, u32[]{:S(2)}) collective-permute-start(f32[16,128]{1,0:T(8,128)S(1)} %get-tuple-element.22), channel_id=1, source_target_pairs={{0,3},{1,2},{2,1},{3,0},{4,7},{5,6},{6,5},{7,4},{8,11},{9,10},{10,... | collective-permute-start | bytes 24584 | tf_op jit(solution)/shard_map/ppermute | solution.py:522
  14.0 3.7 %collective-permute-start.2 = (f32[16,128]{1,0:T(8,128)S(1)}, f32[16,128]{1,0:T(8,128)S(1)}, u32[]{:S(2)}, u32[]{:S(2)}) collective-permute-start(f32[16,128]{1,0:T(8,128)S(1)} %get-tuple-element.23), channel_id=1, source_target_pairs={{0,4},{1,5},{2,6},{3,7},{4,0},{5,1},{6,2},{7,3},{8,12},{9,13},{10,... | collective-permute-start | bytes 24584 | tf_op jit(solution)/shard_map/ppermute | solution.py:522
  16.1 1.6 %collective-permute-start.3 = (f32[16,128]{1,0:T(8,128)S(1)}, f32[16,128]{1,0:T(8,128)S(1)}, u32[]{:S(2)}, u32[]{:S(2)}) collective-permute-start(f32[16,128]{1,0:T(8,128)S(1)} %get-tuple-element.24), channel_id=1, source_target_pairs={{0,1},{1,0},{2,3},{3,2},{4,5},{5,4},{6,7},{7,6},{8,9},{9,8},{10,11... | collective-permute-start | bytes 24584 | tf_op jit(solution)/shard_map/ppermute | solution.py:522
  18.2 4.1 %collective-permute-start.7 = (f32[8,128]{1,0:T(8,128)S(1)}, f32[8,128]{1,0:T(8,128)S(1)}, u32[]{:S(2)}, u32[]{:S(2)}) collective-permute-start(f32[8,128]{1,0:T(8,128)S(1)} %start.1.rest_0_.r_ref), channel_id=1, source_target_pairs={{0,1},{1,0},{2,3},{3,2},{4,8},{5,9},{6,10},{7,11},{8,4},{9,5},{10,... | collective-permute-start | bytes 12296 | tf_op jit(solution)/shard_map/ppermute | solution.py:479
  18.5 3.9 %collective-permute-start.6 = (f32[8,128]{1,0:T(8,128)S(1)}, f32[8,128]{1,0:T(8,128)S(1)}, u32[]{:S(2)}, u32[]{:S(2)}) collective-permute-start(f32[8,128]{1,0:T(8,128)S(1)} %start.1.rest_0_.r_ref), channel_id=1, source_target_pairs={{0,3},{1,2},{2,1},{3,0},{4,7},{5,6},{6,5},{7,4},{8,11},{9,10},{10,... | collective-permute-start | bytes 12296 | tf_op jit(solution)/shard_map/ppermute | solution.py:479
  19.3 4.1 %collective-permute-start.5 = (f32[8,128]{1,0:T(8,128)S(1)}, f32[8,128]{1,0:T(8,128)S(1)}, u32[]{:S(2)}, u32[]{:S(2)}) collective-permute-start(f32[8,128]{1,0:T(8,128)S(1)} %start.1.rest_0_.r_ref), channel_id=1, source_target_pairs={{0,4},{1,5},{2,6},{3,7},{4,0},{5,1},{6,2},{7,3},{8,12},{9,13},{10,... | collective-permute-start | bytes 12296 | tf_op jit(solution)/shard_map/ppermute | solution.py:479
  21.8 1.6 %collective-permute-start.4 = (f32[8,128]{1,0:T(8,128)S(1)}, f32[8,128]{1,0:T(8,128)S(1)}, u32[]{:S(2)}, u32[]{:S(2)}) collective-permute-start(f32[8,128]{1,0:T(8,128)S(1)} %start.1.rest_0_.r_ref), channel_id=1, source_target_pairs={{0,1},{1,0},{2,3},{3,2},{4,5},{5,4},{6,7},{7,6},{8,9},{9,8},{10,11... | collective-permute-start | bytes 12296 | tf_op jit(solution)/shard_map/ppermute | solution.py:479
  23.8 23.9 %copy-start = (s32[64,512]{1,0:T(8,128)S(1)}, s32[64,512]{1,0:T(8,128)}, u32[]{:S(2)}) copy-start(s32[64,512]{1,0:T(8,128)} %target_ref.1) | copy-start | bytes 393220
  23.8 4.9 %collective-permute-start.11 = (f32[8,128]{1,0:T(8,128)S(1)}, f32[8,128]{1,0:T(8,128)S(1)}, u32[]{:S(2)}, u32[]{:S(2)}) collective-permute-start(f32[8,128]{1,0:T(8,128)S(1)} %once.1.rest_0_.w_ref), channel_id=1, source_target_pairs={{0,1},{1,0},{2,3},{3,2},{4,8},{5,9},{6,10},{7,11},{8,4},{9,5},{10,... | collective-permute-start | bytes 12296 | tf_op jit(solution)/shard_map/ppermute | solution.py:479
  24.0 4.7 %collective-permute-start.10 = (f32[8,128]{1,0:T(8,128)S(1)}, f32[8,128]{1,0:T(8,128)S(1)}, u32[]{:S(2)}, u32[]{:S(2)}) collective-permute-start(f32[8,128]{1,0:T(8,128)S(1)} %once.1.rest_0_.w_ref), channel_id=1, source_target_pairs={{0,3},{1,2},{2,1},{3,0},{4,7},{5,6},{6,5},{7,4},{8,11},{9,10},{10,... | collective-permute-start | bytes 12296 | tf_op jit(solution)/shard_map/ppermute | solution.py:479
  25.4 3.8 %collective-permute-start.9 = (f32[8,128]{1,0:T(8,128)S(1)}, f32[8,128]{1,0:T(8,128)S(1)}, u32[]{:S(2)}, u32[]{:S(2)}) collective-permute-start(f32[8,128]{1,0:T(8,128)S(1)} %once.1.rest_0_.w_ref), channel_id=1, source_target_pairs={{0,4},{1,5},{2,6},{3,7},{4,0},{5,1},{6,2},{7,3},{8,12},{9,13},{10,... | collective-permute-start | bytes 12296 | tf_op jit(solution)/shard_map/ppermute | solution.py:479
  27.7 1.8 %collective-permute-start.8 = (f32[8,128]{1,0:T(8,128)S(1)}, f32[8,128]{1,0:T(8,128)S(1)}, u32[]{:S(2)}, u32[]{:S(2)}) collective-permute-start(f32[8,128]{1,0:T(8,128)S(1)} %once.1.rest_0_.w_ref), channel_id=1, source_target_pairs={{0,1},{1,0},{2,3},{3,2},{4,5},{5,4},{6,7},{7,6},{8,9},{9,8},{10,11... | collective-permute-start | bytes 12296 | tf_op jit(solution)/shard_map/ppermute | solution.py:479
  30.0 4.2 %collective-permute-start.15 = (f32[8,128]{1,0:T(8,128)S(1)}, f32[8,128]{1,0:T(8,128)S(1)}, u32[]{:S(2)}, u32[]{:S(2)}) collective-permute-start(f32[8,128]{1,0:T(8,128)S(1)} %twice.1.rest_0_.v_ref), channel_id=1, source_target_pairs={{0,1},{1,0},{2,3},{3,2},{4,8},{5,9},{6,10},{7,11},{8,4},{9,5},{10,... | collective-permute-start | bytes 12296 | tf_op jit(solution)/shard_map/ppermute | solution.py:479
  30.3 3.9 %collective-permute-start.14 = (f32[8,128]{1,0:T(8,128)S(1)}, f32[8,128]{1,0:T(8,128)S(1)}, u32[]{:S(2)}, u32[]{:S(2)}) collective-permute-start(f32[8,128]{1,0:T(8,128)S(1)} %twice.1.rest_0_.v_ref), channel_id=1, source_target_pairs={{0,3},{1,2},{2,1},{3,0},{4,7},{5,6},{6,5},{7,4},{8,11},{9,10},{10,... | collective-permute-start | bytes 12296 | tf_op jit(solution)/shard_map/ppermute | solution.py:479
  31.1 3.8 %collective-permute-start.13 = (f32[8,128]{1,0:T(8,128)S(1)}, f32[8,128]{1,0:T(8,128)S(1)}, u32[]{:S(2)}, u32[]{:S(2)}) collective-permute-start(f32[8,128]{1,0:T(8,128)S(1)} %twice.1.rest_0_.v_ref), channel_id=1, source_target_pairs={{0,4},{1,5},{2,6},{3,7},{4,0},{5,1},{6,2},{7,3},{8,12},{9,13},{10,... | collective-permute-start | bytes 12296 | tf_op jit(solution)/shard_map/ppermute | solution.py:479
  33.3 1.7 %collective-permute-start.12 = (f32[8,128]{1,0:T(8,128)S(1)}, f32[8,128]{1,0:T(8,128)S(1)}, u32[]{:S(2)}, u32[]{:S(2)}) collective-permute-start(f32[8,128]{1,0:T(8,128)S(1)} %twice.1.rest_0_.v_ref), channel_id=1, source_target_pairs={{0,1},{1,0},{2,3},{3,2},{4,5},{5,4},{6,7},{7,6},{8,9},{9,8},{10,11... | collective-permute-start | bytes 12296 | tf_op jit(solution)/shard_map/ppermute | solution.py:479

commit v6 on v4

--- a/solution.py
+++ b/solution.py
@@ -11,6 +11,7 @@
 SWEEPS = 8
 RESIDUAL = 0.05
 SIDES = 4
+PARTS = 2
 BOTH = ("gx", "gy")
 ORDER = ((0, 1), (1, 1), (0, 0), (1, 0))
 F32 = jnp.float32
@@ -102,28 +103,28 @@
     return total * (back * inverse)
 
 
-def bin_rows(target, value, keys, totals_ref, width):
+def bin_rows(target, value, part, totals_ref):
+    width = totals_ref.shape[1]
+    part_rows = totals_ref.shape[0] // 2
     rows, columns = target.shape
-    slots_high = keys.shape[0]
-    shift = width.bit_length() - 1
-    keys = jnp.concatenate([keys] * (columns // 128), axis=1)
     cell = lax.broadcasted_iota(jnp.int32, (width, columns), 0).astype(F32).astype(BF16)
     cells = (target & (width - 1)).astype(F32)
-    slot = lax.shift_right_logical(target, shift)
+    part = part.astype(F32)
+    keys = lax.broadcasted_iota(jnp.int32, (part_rows, columns), 0).astype(F32).astype(BF16)
     high = value.astype(BF16).astype(F32)
     low = value - high
     one_hot = []
     spread = []
     for row in range(rows):
         line = slice(row, row + 1)
-        wide = jnp.broadcast_to(cells[line], (16, columns)).astype(BF16)
-        wide = jnp.concatenate([wide] * (width // 16), axis=0)
-        one_hot.append(jnp.where(wide == cell, BF16(1), BF16(0)))
-        hit = jnp.broadcast_to(slot[line], (slots_high, columns)) == keys
-        parts = [
-            jnp.where(hit, jnp.broadcast_to(part[line], (slots_high, columns)), 0.0) for part in (high, low)
-        ]
-        spread.append(jnp.concatenate(parts, axis=0).astype(BF16))
+        def wide(array, count):
+            packed = jnp.broadcast_to(array[line], (16, columns)).astype(BF16)
+            return jnp.concatenate([packed] * (count // 16), axis=0)
+
+        one_hot.append(jnp.where(wide(cells, width) == cell, BF16(1), BF16(0)))
+        hit = wide(part, part_rows) == keys
+        parts = [jnp.where(hit, wide(piece, part_rows), BF16(0)) for piece in (high, low)]
+        spread.append(jnp.concatenate(parts, axis=0))
     totals_ref[...] += lax.dot_general(
         jnp.concatenate(spread, axis=1),
         jnp.concatenate(one_hot, axis=1),
@@ -172,7 +173,6 @@
     rows, columns = target_ref.shape
     own_blocks, width = heads_ref.shape
     slots = send_ref.shape[0]
-    hi_rows = key_ref.shape[0]
     chunks = in_sems.shape[0]
     chunk = rows // chunks
     flats = (
@@ -198,17 +198,31 @@
     for copy in small_copies() + incoming(0) + incoming(1):
         copy.start()
     totals_ref[...] = jnp.zeros_like(totals_ref)
-    recharge_ref[0:8, :] = jnp.zeros((8, columns), F32)
+    recharge_ref[0:chunk, :] = jnp.zeros((chunk, columns), F32)
     for copy in small_copies():
         copy.wait()
     prepare(
         gx_count, gy_count, send_ref[...], pattern_ref[...], own_blocks, source_ref, block_ref, key_ref
     )
 
-    def bin_tile(tile):
-        target = target_ref[pl.ds(pl.multiple_of(jnp.maximum(tile, 0) * 8, 8), 8), :]
-        value = recharge_ref[pl.ds(pl.multiple_of(tile * 8 + 8, 8), 8), :]
-        bin_rows(target, value, key_ref[...], totals_ref, width)
+    owners = owners_here(gx_count, gy_count)
+    entries = (SIDES + 1) * slots
+    shift = totals_ref.shape[1].bit_length() - 1
+    parts = width // totals_ref.shape[1]
+
+    def part_of(target):
+        part = lax.shift_right_logical(target, shift)
+        slot = lax.shift_right_logical(part, parts.bit_length() - 1)
+        owner = lax.shift_right_logical(slot, slots.bit_length() - 1)
+        side = jnp.zeros_like(target)
+        for k in range(1, SIDES + 1):
+            side = jnp.where(owner == owners[k], k * slots, side)
+        return side + (slot & (slots - 1)) + (part & (parts - 1)) * entries
+
+    def bin_chunk(at):
+        target = target_ref[pl.ds(pl.multiple_of(jnp.maximum(at, 0) * chunk, 8), chunk), :]
+        value = recharge_ref[pl.ds(pl.multiple_of(at * chunk + chunk, 8), chunk), :]
+        bin_rows(target, value, part_of(target), totals_ref)
 
     @pl.loop(0, chunks)
     def _(at):
@@ -224,19 +238,20 @@
         def _():
             blocks_copy.start()
 
-        @pl.loop(0, chunk // 8)
-        def _(tile):
+        bin_chunk(at - 1)
+        for tile in range(chunk // 8):
             tile = at * (chunk // 8) + tile
-            bin_tile(tile - 1)
             place = (pl.ds(pl.multiple_of(tile * 8, 8), 8), slice(None))
-            recharge_ref[pl.ds(pl.multiple_of(tile * 8 + 8, 8), 8), :] = soil_tile(
+            recharge_ref[pl.ds(pl.multiple_of(tile * 8 + chunk, 8), 8), :] = soil_tile(
                 place, water_ref, porosity_ref, conduct_ref, exponent_ref, inflow_ref
             )
 
         outgoing(at).start()
 
-    bin_tile(rows // 8 - 1)
-    sums = totals_ref[0:hi_rows, :] + totals_ref[hi_rows : 2 * hi_rows, :]
+    bin_chunk(chunks - 1)
+    part_rows = totals_ref.shape[0] // 2
+    sums = totals_ref[0:part_rows, :] + totals_ref[part_rows : 2 * part_rows, :]
+    sums = jnp.concatenate([sums[part * entries : (part + 1) * entries] for part in range(parts)], axis=1)
     block = lax.broadcasted_iota(jnp.int32, (own_blocks, width), 0)
     for k in range(SIDES + 1):
         out_ref = side_refs[k - 1] if k else own_ref
@@ -254,7 +269,7 @@
         outgoing(at).wait()
 
 
-def operate(source_ref, blocks_ref, fields):
+def operate(source_ref, blocks_ref, fields, pieces=3):
     own_blocks, most, width = blocks_ref.shape[:3]
     nearby = []
     for k in range(most):
@@ -265,7 +280,7 @@
             rows = jnp.where(side == at, picked, rows)
         nearby.append(rows)
     image = jnp.zeros((own_blocks, width), F32)
-    row = lax.broadcasted_iota(jnp.int32, (own_blocks, 3 * width), 0)
+    row = lax.broadcasted_iota(jnp.int32, (own_blocks, pieces * width), 0)
     for r in range(own_blocks):
         total = blocks_ref[r, 0] * nearby[0][r : r + 1]
         for k in range(1, most):
@@ -273,8 +288,10 @@
         first = total.astype(BF16)
         rest = total - first.astype(F32)
         second = rest.astype(BF16)
-        third = (rest - second.astype(F32)).astype(BF16)
-        parts = jnp.concatenate([first, second, third], axis=1)
+        parts = [first, second]
+        if pieces == 3:
+            parts.append((rest - second.astype(F32)).astype(BF16))
+        parts = jnp.concatenate(parts, axis=1)
         ones = jnp.where(row == r, 1.0, 0.0).astype(BF16)
         image = image + lax.dot_general(
             ones, parts, (((1,), (1,)), ((), ())), preferred_element_type=F32
@@ -305,7 +322,7 @@
 
 def last_kernel(source_ref, blocks_ref, r_ref, w_ref, *rest):
     fields, sums_ref = [f[...] for f in (rest[0],) + rest[-2:0:-1]], rest[-1]
-    z = operate(source_ref, blocks_ref, fields)
+    z = operate(source_ref, blocks_ref, fields, 2)
     r, w, v = r_ref[...], w_ref[...], fields[0]
     rr = whole_sum(r * r)
     ratio = whole_sum(w * w) / rr
@@ -451,6 +468,7 @@
     layers, rows, columns = water_content.shape
     most = block_pattern.shape[1]
     hi_rows = -(-(SIDES + 1) * slots // 8) * 8
+    part_rows = -(-PARTS * (SIDES + 1) * slots // 16) * 16
     area = own_blocks * width / (rows * columns)
     perms = swaps(gx_count, gy_count)
     in_hbm = lambda array: pltpu.with_memory_space_constraint(array, pltpu.HBM)
@@ -480,8 +498,8 @@
             pltpu.VMEM((own_blocks, width), F32),
             pltpu.VMEM((slots, devices), jnp.int32),
             pltpu.VMEM((own_blocks, most), jnp.int32),
-            pltpu.VMEM((rows + 8, columns), F32),
-            pltpu.VMEM((2 * hi_rows, width), F32),
+            pltpu.VMEM((rows + 16, columns), F32),
+            pltpu.VMEM((2 * part_rows, width // PARTS), F32),
             pltpu.SemaphoreType.DMA((3,)),
             pltpu.SemaphoreType.DMA((chunks, 6)),
             pltpu.SemaphoreType.DMA((chunks,)),

time: 50.4 us -> 49.3 us (0.978)
  Pallas kernels: 14.8 us -> 13.7 us
    pallas_call x1, Pallas kernels: 11.1 us -> 10 us  [body(): pl.pallas_call(functools.partial(soil_kernel, gx_count, gy_count), in_spe...]
where the time goes in v6:
time: 49.3 us; the launch traced here: 49.1 us
  starting transfers between devices  19.1 us (39%)
  Pallas kernels  13.7 us (28%)
  blocking collectives  12.1 us (25%)
  waiting for transfers between devices  3.58 us (7%)
  between operations  0.67 us (1%)
    ppermute x12, starting transfers between devices, trade(): return [lax.ppermute(array, BOTH, perm) for perm in perms]  13.2 us
    all_to_all x1, blocking collectives, body(): all_sums = lax.all_to_all(sums, BOTH, 0, 0)  12.1 us
    pallas_call x1, Pallas kernels, body(): pl.pallas_call(functools.partial(soil_kernel, gx_count, gy_count), in_spe...  10 us
    ppermute x4, starting transfers between devices, body(): got = [lax.ppermute(out, BOTH, perm) for out, perm in zip(outs[5:], perms)]  5.88 us
    ppermute x12, waiting for transfers between devices, trade(): return [lax.ppermute(array, BOTH, perm) for perm in perms]  2.63 us
    pallas_call x4, Pallas kernels, small(): pl.pallas_call(kernel, in_specs=[VMEM] * (2 + len(args)), out_specs=VMEM,...  1.95 us
    pallas_call x1, Pallas kernels, body(): pl.pallas_call(functools.partial(heads_kernel, slots), in_specs=[VMEM] *...  1.7 us
  transfers between devices with their start and end apart: 16, of which 6 were waited for; matrix products, arithmetic and copies ran while one was open for 0% of the time, Pallas kernels for 0%

profile of v6, /device:TPU:0, one launch (start us, length us, event | category | flops | bytes accessed | tf_op | source)
XLA Modules:
  0.0 49.1 jit_solution(6645241332746354329)
XLA Ops:
  0.6 10.0 %soil.1 = (f32[16,64,512]{2,1,0:T(8,128)}, s32[14,8,128]{2,1,0:T(8,128)S(1)}, s32[5,8,128]{2,1,0:T(8,128)S(1)}, s32[24,128]{1,0:T(8,128)S(1)}, f32[16,128]{1,0:T...) custom-call(f32[16,64,512]{2,1,0:T(8,128)} %water_hbm.1, ...), custom_call_target="tpu_custom_call" | custom-call | tf_op jit(solution)/shard_map/soil/pallas_call | solution.py:482
  10.6 0.5 %collective-permute-start = (f32[16,128]{1,0:T(8,128)S(1)}, f32[16,128]{1,0:T(8,128)S(1)}, u32[]{:S(2)}, u32[]{:S(2)}) collective-permute-start(f32[16,128]{1,0:T(8,128)S(1)} %get-tuple-element.21), channel_id=1, source_target_pairs={{0,1},{1,0},{2,3},{3,2},{4,8},{5,9},{6,10},{7,11},{8,4},{9,5},{10,... | collective-permute-start | bytes 24584 | tf_op jit(solution)/shard_map/ppermute | solution.py:521
  11.2 2.6 %collective-permute-start.1 = (f32[16,128]{1,0:T(8,128)S(1)}, f32[16,128]{1,0:T(8,128)S(1)}, u32[]{:S(2)}, u32[]{:S(2)}) collective-permute-start(f32[16,128]{1,0:T(8,128)S(1)} %get-tuple-element.22), channel_id=1, source_target_pairs={{0,3},{1,2},{2,1},{3,0},{4,7},{5,6},{6,5},{7,4},{8,11},{9,10},{10,... | collective-permute-start | bytes 24584 | tf_op jit(solution)/shard_map/ppermute | solution.py:521
  13.8 2.1 %collective-permute-start.2 = (f32[16,128]{1,0:T(8,128)S(1)}, f32[16,128]{1,0:T(8,128)S(1)}, u32[]{:S(2)}, u32[]{:S(2)}) collective-permute-start(f32[16,128]{1,0:T(8,128)S(1)} %get-tuple-element.23), channel_id=1, source_target_pairs={{0,4},{1,5},{2,6},{3,7},{4,0},{5,1},{6,2},{7,3},{8,12},{9,13},{10,... | collective-permute-start | bytes 24584 | tf_op jit(solution)/shard_map/ppermute | solution.py:521
  15.8 0.7 %collective-permute-start.3 = (f32[16,128]{1,0:T(8,128)S(1)}, f32[16,128]{1,0:T(8,128)S(1)}, u32[]{:S(2)}, u32[]{:S(2)}) collective-permute-start(f32[16,128]{1,0:T(8,128)S(1)} %get-tuple-element.24), channel_id=1, source_target_pairs={{0,1},{1,0},{2,3},{3,2},{4,5},{5,4},{6,7},{7,6},{8,9},{9,8},{10,11... | collective-permute-start | bytes 24584 | tf_op jit(solution)/shard_map/ppermute | solution.py:521
  16.5 0.0 collective-permute-done.rest_0_
  16.5 0.0 collective-permute-done.1.rest_1_.rest_4_
  16.5 0.9 %collective-permute-done.2.rest_2_.rest_8_ = f32[16,128]{1,0:T(8,128)S(1)} collective-permute-done((f32[16,128]{1,0:T(8,128)S(1)}, f32[16,128]{1,0:T(8,128)S(1)}, u32[]{:S(2)}, u32[]{:S(2)}) %collective-permute-start.2) | collective-permute-done | bytes 8224 | tf_op jit(solution)/shard_map/ppermute | solution.py:521
  17.5 0.0 collective-permute-done.3.rest_3_.rest_12_
  17.5 0.5 start.1.rest_0_.r_ref
  18.0 0.2 collective-permute-start.7
  18.2 0.8 %collective-permute-start.6 = (f32[8,128]{1,0:T(8,128)S(1)}, f32[8,128]{1,0:T(8,128)S(1)}, u32[]{:S(2)}, u32[]{:S(2)}) collective-permute-start(f32[8,128]{1,0:T(8,128)S(1)} %start.1.rest_0_.r_ref), channel_id=1, source_target_pairs={{0,3},{1,2},{2,1},{3,0},{4,7},{5,6},{6,5},{7,4},{8,11},{9,10},{10,... | collective-permute-start | bytes 12296 | tf_op jit(solution)/shard_map/ppermute | solution.py:479
  19.0 2.5 %collective-permute-start.5 = (f32[8,128]{1,0:T(8,128)S(1)}, f32[8,128]{1,0:T(8,128)S(1)}, u32[]{:S(2)}, u32[]{:S(2)}) collective-permute-start(f32[8,128]{1,0:T(8,128)S(1)} %start.1.rest_0_.r_ref), channel_id=1, source_target_pairs={{0,4},{1,5},{2,6},{3,7},{4,0},{5,1},{6,2},{7,3},{8,12},{9,13},{10,... | collective-permute-start | bytes 12296 | tf_op jit(solution)/shard_map/ppermute | solution.py:479
  21.5 0.6 %collective-permute-start.4 = (f32[8,128]{1,0:T(8,128)S(1)}, f32[8,128]{1,0:T(8,128)S(1)}, u32[]{:S(2)}, u32[]{:S(2)}) collective-permute-start(f32[8,128]{1,0:T(8,128)S(1)} %start.1.rest_0_.r_ref), channel_id=1, source_target_pairs={{0,1},{1,0},{2,3},{3,2},{4,5},{5,4},{6,7},{7,6},{8,9},{9,8},{10,11... | collective-permute-start | bytes 12296 | tf_op jit(solution)/shard_map/ppermute | solution.py:479
  22.1 0.0 collective-permute-done.7.rest_4_.rest_1_
  22.1 0.0 collective-permute-done.6.rest_3_.rest_5_
  22.1 1.0 %collective-permute-done.5.rest_2_.rest_9_ = f32[8,128]{1,0:T(8,128)S(1)} collective-permute-done((f32[8,128]{1,0:T(8,128)S(1)}, f32[8,128]{1,0:T(8,128)S(1)}, u32[]{:S(2)}, u32[]{:S(2)}) %collective-permute-start.5) | collective-permute-done | bytes 4128 | tf_op jit(solution)/shard_map/ppermute | solution.py:479
  23.1 0.0 collective-permute-done.4.rest_1_.rest_13_
  23.1 0.5 once.1.rest_0_.w_ref
  23.6 0.0 copy-start
  23.6 0.2 collective-permute-start.11
  23.8 1.4 %collective-permute-start.10 = (f32[8,128]{1,0:T(8,128)S(1)}, f32[8,128]{1,0:T(8,128)S(1)}, u32[]{:S(2)}, u32[]{:S(2)}) collective-permute-start(f32[8,128]{1,0:T(8,128)S(1)} %once.1.rest_0_.w_ref), channel_id=1, source_target_pairs={{0,3},{1,2},{2,1},{3,0},{4,7},{5,6},{6,5},{7,4},{8,11},{9,10},{10,... | collective-permute-start | bytes 12296 | tf_op jit(solution)/shard_map/ppermute | solution.py:479
  25.2 2.3 %collective-permute-start.9 = (f32[8,128]{1,0:T(8,128)S(1)}, f32[8,128]{1,0:T(8,128)S(1)}, u32[]{:S(2)}, u32[]{:S(2)}) collective-permute-start(f32[8,128]{1,0:T(8,128)S(1)} %once.1.rest_0_.w_ref), channel_id=1, source_target_pairs={{0,4},{1,5},{2,6},{3,7},{4,0},{5,1},{6,2},{7,3},{8,12},{9,13},{10,... | collective-permute-start | bytes 12296 | tf_op jit(solution)/shard_map/ppermute | solution.py:479
  27.4 1.0 %collective-permute-start.8 = (f32[8,128]{1,0:T(8,128)S(1)}, f32[8,128]{1,0:T(8,128)S(1)}, u32[]{:S(2)}, u32[]{:S(2)}) collective-permute-start(f32[8,128]{1,0:T(8,128)S(1)} %once.1.rest_0_.w_ref), channel_id=1, source_target_pairs={{0,1},{1,0},{2,3},{3,2},{4,5},{5,4},{6,7},{7,6},{8,9},{9,8},{10,11... | collective-permute-start | bytes 12296 | tf_op jit(solution)/shard_map/ppermute | solution.py:479
  28.4 0.0 collective-permute-done.11.rest_4_.rest_2_
  28.4 0.0 collective-permute-done.10.rest_3_.rest_6_
  28.4 0.6 %collective-permute-done.9.rest_2_.rest_10_ = f32[8,128]{1,0:T(8,128)S(1)} collective-permute-done((f32[8,128]{1,0:T(8,128)S(1)}, f32[8,128]{1,0:T(8,128)S(1)}, u32[]{:S(2)}, u32[]{:S(2)}) %collective-permute-start.9) | collective-permute-done | bytes 4128 | tf_op jit(solution)/shard_map/ppermute | solution.py:479
  29.0 0.2 collective-permute-done.8.rest_1_.rest_14_
  29.2 0.5 twice.1.rest_0_.v_ref
  29.7 0.4 collective-permute-start.15
  30.1 0.7 %collective-permute-start.14 = (f32[8,128]{1,0:T(8,128)S(1)}, f32[8,128]{1,0:T(8,128)S(1)}, u32[]{:S(2)}, u32[]{:S(2)}) collective-permute-start(f32[8,128]{1,0:T(8,128)S(1)} %twice.1.rest_0_.v_ref), channel_id=1, source_target_pairs={{0,3},{1,2},{2,1},{3,0},{4,7},{5,6},{6,5},{7,4},{8,11},{9,10},{10,... | collective-permute-start | bytes 12296 | tf_op jit(solution)/shard_map/ppermute | solution.py:479
  30.8 2.2 %collective-permute-start.13 = (f32[8,128]{1,0:T(8,128)S(1)}, f32[8,128]{1,0:T(8,128)S(1)}, u32[]{:S(2)}, u32[]{:S(2)}) collective-permute-start(f32[8,128]{1,0:T(8,128)S(1)} %twice.1.rest_0_.v_ref), channel_id=1, source_target_pairs={{0,4},{1,5},{2,6},{3,7},{4,0},{5,1},{6,2},{7,3},{8,12},{9,13},{10,... | collective-permute-start | bytes 12296 | tf_op jit(solution)/shard_map/ppermute | solution.py:479
  33.0 0.9 %collective-permute-start.12 = (f32[8,128]{1,0:T(8,128)S(1)}, f32[8,128]{1,0:T(8,128)S(1)}, u32[]{:S(2)}, u32[]{:S(2)}) collective-permute-start(f32[8,128]{1,0:T(8,128)S(1)} %twice.1.rest_0_.v_ref), channel_id=1, source_target_pairs={{0,1},{1,0},{2,3},{3,2},{4,5},{5,4},{6,7},{7,6},{8,9},{9,8},{10,11... | collective-permute-start | bytes 12296 | tf_op jit(solution)/shard_map/ppermute | solution.py:479
  33.9 0.0 collective-permute-done.15.rest_4_.rest_3_
  33.9 0.0 collective-permute-done.14.rest_3_.rest_7_
  33.9 0.7 %collective-permute-done.13.rest_2_.rest_11_ = f32[8,128]{1,0:T(8,128)S(1)} collective-permute-done((f32[8,128]{1,0:T(8,128)S(1)}, f32[8,128]{1,0:T(8,128)S(1)}, u32[]{:S(2)}, u32[]{:S(2)}) %collective-permute-start.13) | collective-permute-done | bytes 4128 | tf_op jit(solution)/shard_map/ppermute | solution.py:479
  34.6 0.1 collective-permute-done.12.rest_1_.rest_15_
  34.8 0.5 %sums.1 = f32[32,1,128]{2,1,0:T(1,128)S(1)} custom-call(s32[14,8,128]{2,1,0:T(8,128)S(1)} %get-tuple-element.18.source_ref, f32[8,7,128,128]{3,2,1,0:T(8,128)S(1)} %get-tuple-element.19.blocks_ref, f32[8,128]{1,0:T(8,128)S(1)} %start.1.rest_0_.r_ref, f32[8,128]{1,0:T(8,128)S(1)} %once.1.rest_0_.w_ref, f32[8,128]{1,0:T(8,128)S(1)} %twice.1.rest_0_.v_ref, ...), custom_call_target="tpu_custom_call" | custom-call | tf_op jit(solution)/shard_map/sums/pallas_call | solution.py:524
  35.3 12.1 %all_to_all.5.all_ref = f32[32,1,128]{2,1,0:T(1,128)S(1)} all-to-all(f32[32,1,128]{2,1,0:T(1,128)S(1)} %sums.1), channel_id=1, replica_groups=mesh['gx'=8,'gy'=4] {'gx','gy'}, dimensions={0} | all-to-all | bytes 32768 | tf_op jit(solution)/shard_map/all_to_all | solution.py:540
  47.4 0.0 copy-done
  47.4 1.7 %heads.1 = (f32[8,128]{1,0:T(8,128)}, f32[64,512]{1,0:T(8,128)}) custom-call(s32[5,8,128]{2,1,0:T(8,128)S(1)} %get-tuple-element.16.block_ref, s32[24,128]{1,0:T(8,128)S(1)} %get-tuple-element.17.key_ref, f32[32,1,128]{2,1,0:T(1,128)S(1)} %all_to_all.5.all_ref, s32[64,512]{1,0:T(8,128)S(1)} %copy-done, f32[16,128]{1,0:T(8,128)S(1)} %get-tuple-element.20.own_ref, ...), custom_call_target="tpu_custom_call" | custom-call | tf_op jit(solution)/shard_map/heads/pallas_call | solution.py:544
Async XLA Ops:
  10.6 5.9 %collective-permute-start = (f32[16,128]{1,0:T(8,128)S(1)}, f32[16,128]{1,0:T(8,128)S(1)}, u32[]{:S(2)}, u32[]{:S(2)}) collective-permute-start(f32[16,128]{1,0:T(8,128)S(1)} %get-tuple-element.21), channel_id=1, source_target_pairs={{0,1},{1,0},{2,3},{3,2},{4,8},{5,9},{6,10},{7,11},{8,4},{9,5},{10,... | collective-permute-start | bytes 24584 | tf_op jit(solution)/shard_map/ppermute | solution.py:521
  11.2 5.4 %collective-permute-start.1 = (f32[16,128]{1,0:T(8,128)S(1)}, f32[16,128]{1,0:T(8,128)S(1)}, u32[]{:S(2)}, u32[]{:S(2)}) collective-permute-start(f32[16,128]{1,0:T(8,128)S(1)} %get-tuple-element.22), channel_id=1, source_target_pairs={{0,3},{1,2},{2,1},{3,0},{4,7},{5,6},{6,5},{7,4},{8,11},{9,10},{10,... | collective-permute-start | bytes 24584 | tf_op jit(solution)/shard_map/ppermute | solution.py:521
  13.8 3.7 %collective-permute-start.2 = (f32[16,128]{1,0:T(8,128)S(1)}, f32[16,128]{1,0:T(8,128)S(1)}, u32[]{:S(2)}, u32[]{:S(2)}) collective-permute-start(f32[16,128]{1,0:T(8,128)S(1)} %get-tuple-element.23), channel_id=1, source_target_pairs={{0,4},{1,5},{2,6},{3,7},{4,0},{5,1},{6,2},{7,3},{8,12},{9,13},{10,... | collective-permute-start | bytes 24584 | tf_op jit(solution)/shard_map/ppermute | solution.py:521
  15.8 1.6 %collective-permute-start.3 = (f32[16,128]{1,0:T(8,128)S(1)}, f32[16,128]{1,0:T(8,128)S(1)}, u32[]{:S(2)}, u32[]{:S(2)}) collective-permute-start(f32[16,128]{1,0:T(8,128)S(1)} %get-tuple-element.24), channel_id=1, source_target_pairs={{0,1},{1,0},{2,3},{3,2},{4,5},{5,4},{6,7},{7,6},{8,9},{9,8},{10,11... | collective-permute-start | bytes 24584 | tf_op jit(solution)/shard_map/ppermute | solution.py:521
  18.0 4.1 %collective-permute-start.7 = (f32[8,128]{1,0:T(8,128)S(1)}, f32[8,128]{1,0:T(8,128)S(1)}, u32[]{:S(2)}, u32[]{:S(2)}) collective-permute-start(f32[8,128]{1,0:T(8,128)S(1)} %start.1.rest_0_.r_ref), channel_id=1, source_target_pairs={{0,1},{1,0},{2,3},{3,2},{4,8},{5,9},{6,10},{7,11},{8,4},{9,5},{10,... | collective-permute-start | bytes 12296 | tf_op jit(solution)/shard_map/ppermute | solution.py:479
  18.2 3.9 %collective-permute-start.6 = (f32[8,128]{1,0:T(8,128)S(1)}, f32[8,128]{1,0:T(8,128)S(1)}, u32[]{:S(2)}, u32[]{:S(2)}) collective-permute-start(f32[8,128]{1,0:T(8,128)S(1)} %start.1.rest_0_.r_ref), channel_id=1, source_target_pairs={{0,3},{1,2},{2,1},{3,0},{4,7},{5,6},{6,5},{7,4},{8,11},{9,10},{10,... | collective-permute-start | bytes 12296 | tf_op jit(solution)/shard_map/ppermute | solution.py:479
  19.0 4.1 %collective-permute-start.5 = (f32[8,128]{1,0:T(8,128)S(1)}, f32[8,128]{1,0:T(8,128)S(1)}, u32[]{:S(2)}, u32[]{:S(2)}) collective-permute-start(f32[8,128]{1,0:T(8,128)S(1)} %start.1.rest_0_.r_ref), channel_id=1, source_target_pairs={{0,4},{1,5},{2,6},{3,7},{4,0},{5,1},{6,2},{7,3},{8,12},{9,13},{10,... | collective-permute-start | bytes 12296 | tf_op jit(solution)/shard_map/ppermute | solution.py:479
  21.5 1.6 %collective-permute-start.4 = (f32[8,128]{1,0:T(8,128)S(1)}, f32[8,128]{1,0:T(8,128)S(1)}, u32[]{:S(2)}, u32[]{:S(2)}) collective-permute-start(f32[8,128]{1,0:T(8,128)S(1)} %start.1.rest_0_.r_ref), channel_id=1, source_target_pairs={{0,1},{1,0},{2,3},{3,2},{4,5},{5,4},{6,7},{7,6},{8,9},{9,8},{10,11... | collective-permute-start | bytes 12296 | tf_op jit(solution)/shard_map/ppermute | solution.py:479
  23.6 23.9 %copy-start = (s32[64,512]{1,0:T(8,128)S(1)}, s32[64,512]{1,0:T(8,128)}, u32[]{:S(2)}) copy-start(s32[64,512]{1,0:T(8,128)} %target_ref.1) | copy-start | bytes 393220
  23.6 4.9 %collective-permute-start.11 = (f32[8,128]{1,0:T(8,128)S(1)}, f32[8,128]{1,0:T(8,128)S(1)}, u32[]{:S(2)}, u32[]{:S(2)}) collective-permute-start(f32[8,128]{1,0:T(8,128)S(1)} %once.1.rest_0_.w_ref), channel_id=1, source_target_pairs={{0,1},{1,0},{2,3},{3,2},{4,8},{5,9},{6,10},{7,11},{8,4},{9,5},{10,... | collective-permute-start | bytes 12296 | tf_op jit(solution)/shard_map/ppermute | solution.py:479
  23.8 4.6 %collective-permute-start.10 = (f32[8,128]{1,0:T(8,128)S(1)}, f32[8,128]{1,0:T(8,128)S(1)}, u32[]{:S(2)}, u32[]{:S(2)}) collective-permute-start(f32[8,128]{1,0:T(8,128)S(1)} %once.1.rest_0_.w_ref), channel_id=1, source_target_pairs={{0,3},{1,2},{2,1},{3,0},{4,7},{5,6},{6,5},{7,4},{8,11},{9,10},{10,... | collective-permute-start | bytes 12296 | tf_op jit(solution)/shard_map/ppermute | solution.py:479
  25.2 3.8 %collective-permute-start.9 = (f32[8,128]{1,0:T(8,128)S(1)}, f32[8,128]{1,0:T(8,128)S(1)}, u32[]{:S(2)}, u32[]{:S(2)}) collective-permute-start(f32[8,128]{1,0:T(8,128)S(1)} %once.1.rest_0_.w_ref), channel_id=1, source_target_pairs={{0,4},{1,5},{2,6},{3,7},{4,0},{5,1},{6,2},{7,3},{8,12},{9,13},{10,... | collective-permute-start | bytes 12296 | tf_op jit(solution)/shard_map/ppermute | solution.py:479
  27.4 1.8 %collective-permute-start.8 = (f32[8,128]{1,0:T(8,128)S(1)}, f32[8,128]{1,0:T(8,128)S(1)}, u32[]{:S(2)}, u32[]{:S(2)}) collective-permute-start(f32[8,128]{1,0:T(8,128)S(1)} %once.1.rest_0_.w_ref), channel_id=1, source_target_pairs={{0,1},{1,0},{2,3},{3,2},{4,5},{5,4},{6,7},{7,6},{8,9},{9,8},{10,11... | collective-permute-start | bytes 12296 | tf_op jit(solution)/shard_map/ppermute | solution.py:479
  29.7 4.2 %collective-permute-start.15 = (f32[8,128]{1,0:T(8,128)S(1)}, f32[8,128]{1,0:T(8,128)S(1)}, u32[]{:S(2)}, u32[]{:S(2)}) collective-permute-start(f32[8,128]{1,0:T(8,128)S(1)} %twice.1.rest_0_.v_ref), channel_id=1, source_target_pairs={{0,1},{1,0},{2,3},{3,2},{4,8},{5,9},{6,10},{7,11},{8,4},{9,5},{10,... | collective-permute-start | bytes 12296 | tf_op jit(solution)/shard_map/ppermute | solution.py:479
  30.1 3.9 %collective-permute-start.14 = (f32[8,128]{1,0:T(8,128)S(1)}, f32[8,128]{1,0:T(8,128)S(1)}, u32[]{:S(2)}, u32[]{:S(2)}) collective-permute-start(f32[8,128]{1,0:T(8,128)S(1)} %twice.1.rest_0_.v_ref), channel_id=1, source_target_pairs={{0,3},{1,2},{2,1},{3,0},{4,7},{5,6},{6,5},{7,4},{8,11},{9,10},{10,... | collective-permute-start | bytes 12296 | tf_op jit(solution)/shard_map/ppermute | solution.py:479
  30.8 3.8 %collective-permute-start.13 = (f32[8,128]{1,0:T(8,128)S(1)}, f32[8,128]{1,0:T(8,128)S(1)}, u32[]{:S(2)}, u32[]{:S(2)}) collective-permute-start(f32[8,128]{1,0:T(8,128)S(1)} %twice.1.rest_0_.v_ref), channel_id=1, source_target_pairs={{0,4},{1,5},{2,6},{3,7},{4,0},{5,1},{6,2},{7,3},{8,12},{9,13},{10,... | collective-permute-start | bytes 12296 | tf_op jit(solution)/shard_map/ppermute | solution.py:479
  33.0 1.7 %collective-permute-start.12 = (f32[8,128]{1,0:T(8,128)S(1)}, f32[8,128]{1,0:T(8,128)S(1)}, u32[]{:S(2)}, u32[]{:S(2)}) collective-permute-start(f32[8,128]{1,0:T(8,128)S(1)} %twice.1.rest_0_.v_ref), channel_id=1, source_target_pairs={{0,1},{1,0},{2,3},{3,2},{4,5},{5,4},{6,7},{7,6},{8,9},{9,8},{10,11... | collective-permute-start | bytes 12296 | tf_op jit(solution)/shard_map/ppermute | solution.py:479
